TPU v7x, 128 devices: a whole 4x4x4 slice. The times are simulated.
128 devices in a mesh: dp: 16 (over y_hi, z, core), space: 8 (over x, y_lo).
Axes of the slice: x: 4, y: 4 (y_hi: 2, y_lo: 2; y = y_hi * 2 + y_lo), z: 4, core: 2. Of those that a mesh axis runs over, the one named last changes fastest.
Arguments:
- features: bfloat16 [16, 32, 128, 704], P('dp', 'space'), may hold values from -24 to 24
- kernel: float32 [7, 7, 704], replicated, may hold values from -0.875 to 0.875
- norm_gain: float32 [704], replicated, may hold values from 0.1 to 1.9
- w_up: bfloat16 [2816, 704], P('dp'), may hold values from -0.21875 to 0.21875
- grn_gamma: float32 [2816], replicated, may hold values from -2.5 to 2.5
- grn_beta: float32 [2816], replicated, may hold values from -3 to 3
- w_down: bfloat16 [2816, 704], P('dp'), may hold values from -0.109375 to 0.109375
- upstream: bfloat16 [16, 32, 128, 704], P('dp', 'space'), may hold values from -24 to 24
- labels: int32 [16, 32, 128], P('dp', 'space'), may hold values from 0 to 149
- class_weight: float32 [150], replicated, may hold values from 0.3 to 3
Outputs:
- grad_features: float32 [16, 32, 128, 704], P('dp', 'space')
- grad_kernel: float32 [7, 7, 704], replicated
- grad_gain: float32 [704], replicated
- grad_up: float32 [2816, 704], P('dp')
- grad_gamma: float32 [2816], replicated
- grad_beta: float32 [2816], replicated
- grad_down: float32 [2816, 704], P('dp')
Inputs may be any that keep to these rules, and one draw needn't show every extreme that they name: `labels`: the class of each pixel.
All inputs are finite; a program needn't handle non-finite values.
Results may differ from a plain program's by a relative error of at most 0.0048.
Values may be sent and summed in bfloat16 or wider, within the bound.
No kernel may reach another device: no remote copies, remote signals or barrier semaphores. Data moves between devices by JAX's collectives and lax.ppermute only.
A program may use at most 128 MiB of HBM per device.

v0:
```python
import math

import jax
import jax.numpy as jnp
from jax import lax
from jax.sharding import PartitionSpec as P

EPS_NORM = 1e-06


def with_halo(shard, sides, width):
    for axis, dim in sides:
        devices, length = (lax.axis_size(axis), shard.shape[dim])
        up = [(i, (i + 1) % devices) for i in range(devices - 1)]
        down = [(j, i) for i, j in up]
        last = lax.slice_in_dim(shard, length - width, length, axis=dim)
        leading = lax.slice_in_dim(shard, 0, width, axis=dim)
        before = lax.ppermute(last, axis, up)
        after = lax.ppermute(leading, axis, down)
        shard = jnp.concatenate([before, shard, after], axis=dim)
    return shard


def depthwise(padded, kernel, rows, cols):
    total = jnp.zeros(padded.shape[:1] + (rows, cols, padded.shape[3]), jnp.float32)
    for down in range(7):
        for across in range(7):
            total = (
                total
                + padded[:, down : down + rows, across : across + cols, :].astype(jnp.float32)
                * kernel[down, across]
            )
    return total


def transpose_taps(grad_pad, kernel, rows, cols):
    total = jnp.zeros(grad_pad.shape[:1] + (rows, cols, grad_pad.shape[3]), jnp.float32)
    for down in range(7):
        for across in range(7):
            total = (
                total
                + grad_pad[:, 6 - down : 6 - down + rows, 6 - across : 6 - across + cols, :]
                * kernel[down, across]
            )
    return total


def kernel_terms(grad_conv, padded, rows, cols):
    lines = []
    for down in range(7):
        taps = []
        for across in range(7):
            window = padded[:, down : down + rows, across : across + cols, :].astype(jnp.float32)
            taps.append(jnp.sum(grad_conv * window, axis=(0, 1, 2)))
        lines.append(jnp.stack(taps, axis=0))
    return jnp.stack(lines, axis=0)


def layer_norm(conv, gain):
    mean = jnp.mean(conv, axis=-1, keepdims=True)
    centred = conv - mean
    var = jnp.mean(centred * centred, axis=-1, keepdims=True)
    return centred * lax.rsqrt(var + EPS_NORM) * gain


def exact_gelu(value):
    return jax.nn.gelu(value, approximate=False)


def response_norm(act, total_sq, gamma, beta):
    energy = jnp.sqrt(total_sq)
    ratio = energy / (jnp.mean(energy, axis=-1, keepdims=True) + EPS_NORM)
    return gamma * act * ratio[:, None, :] + beta + act


def body(
    features, kernel, norm_gain, w_up, grn_gamma, grn_beta, w_down, upstream, labels, class_weight
):
    crops, rows, cols, width = features.shape
    hidden_width = w_up.shape[0] * lax.axis_size("dp")
    padded = with_halo(features, (("space", 1),), 3)
    padded = jnp.pad(padded, ((0, 0), (0, 0), (3, 3), (0, 0)))
    conv = depthwise(padded, kernel, rows, cols)
    normed_f, ln_back = jax.vjp(layer_norm, conv, norm_gain)
    normed = normed_f.astype(jnp.bfloat16).reshape(-1, width)
    hidden = lax.dot_general(
        normed,
        lax.all_gather(w_up, "dp", axis=0, tiled=True),
        (((1,), (1,)), ((), ())),
        preferred_element_type=jnp.float32,
    )
    act, gelu_back = jax.vjp(exact_gelu, hidden)
    act3 = act.reshape(crops, rows * cols, hidden_width)
    local_sq = jnp.sum(act3 * act3, axis=1)
    total_sq = lax.psum(local_sq, "space")
    mixed_f, grn_back = jax.vjp(response_norm, act3, total_sq, grn_gamma, grn_beta)
    mixed = mixed_f.astype(jnp.bfloat16).reshape(-1, hidden_width)
    classes = jnp.arange(class_weight.shape[0], dtype=jnp.int32)
    pixel_weight = jnp.sum(jnp.where(labels[..., None] == classes, class_weight, 0.0), axis=-1)
    pixel_grad = upstream.astype(jnp.float32) * pixel_weight[..., None]
    weighted = pixel_grad.astype(jnp.bfloat16).reshape(-1, width)
    grad_mixed = lax.dot_general(
        weighted,
        lax.all_gather(w_down, "dp", axis=0, tiled=True),
        (((1,), (1,)), ((), ())),
        preferred_element_type=jnp.float32,
    )
    grad_act, sq_part, gamma_part, beta_part = grn_back(grad_mixed.reshape(act3.shape))
    grad_sq = lax.psum(sq_part, "space")
    grad_act = grad_act + 2.0 * act3 * grad_sq[:, None, :]
    grad_hidden = gelu_back(grad_act.reshape(act.shape))[0].astype(jnp.bfloat16)
    grad_normed = jnp.dot(
        grad_hidden,
        lax.all_gather(w_up, "dp", axis=0, tiled=True),
        preferred_element_type=jnp.float32,
    )
    up_term = lax.dot_general(
        grad_hidden, normed, (((0,), (0,)), ((), ())), preferred_element_type=jnp.float32
    )
    down_term = lax.dot_general(
        mixed, weighted, (((0,), (0,)), ((), ())), preferred_element_type=jnp.float32
    )
    partial_rows = lax.psum_scatter(
        jnp.concatenate([up_term, down_term], axis=1), "dp", scatter_dimension=0, tiled=True
    )
    summed = lax.psum(partial_rows, "space")
    grad_conv, gain_part = ln_back(grad_normed.reshape(crops, rows, cols, width))
    grad_pad = with_halo(grad_conv, (("space", 1),), 3)
    grad_pad = jnp.pad(grad_pad, ((0, 0), (0, 0), (3, 3), (0, 0)))
    conv_back = transpose_taps(grad_pad, kernel, rows, cols)
    kernel_part = kernel_terms(grad_conv, padded, rows, cols)
    grad_features = pixel_grad + conv_back
    kernel_sum, gain_sum, gamma_sum, beta_sum = lax.psum(
        (kernel_part, gain_part, gamma_part, beta_part), ("dp", "space")
    )
    pixels = crops * lax.axis_size("dp") * rows * lax.axis_size("space") * cols
    scale = 1.0 / math.sqrt(pixels)
    grad_up = scale * summed[:, :width]
    grad_down = scale * summed[:, width:]
    return (
        grad_features,
        scale * kernel_sum,
        scale * gain_sum,
        grad_up,
        scale * gamma_sum,
        scale * beta_sum,
        grad_down,
    )


def solution(mesh):
    return jax.shard_map(
        body,
        mesh=mesh,
        in_specs=(
            P("dp", "space", None, None),
            P(),
            P(),
            P("dp", None),
            P(),
            P(),
            P("dp", None),
            P("dp", "space", None, None),
            P("dp", "space", None),
            P(),
        ),
        out_specs=(P("dp", "space", None, None), P(), P(), P("dp", None), P(), P(), P("dp", None)),
        check_vma=False,
    )
```

profile of v0, /device:TPU:0, one launch (start us, length us, event | category | flops | bytes accessed | tf_op | source)
XLA Modules:
  0.0 619.1 jit_solution(17434311103422240103)
XLA Ops:
  10.6 4.6 collective-permute-start
  16.7 23.0 %collective-permute-done = bf16[1,3,128,704]{2,3,1,0:T(8,128)(2,1)S(1)} collective-permute-done((bf16[1,3,128,704]{2,3,1,0:T(8,128)(2,1)S(1)}, bf16[1,3,128,704]{2,3,1,0:T(8,128)(2,1)S(1)}, u32[]{:S(2)}, u32[]{:S(2)}) %collective-permute-start) | collective-permute-done | bytes 540704 | tf_op jit(solution)/shard_map/ppermute | solution.py:18
  40.1 2.4 fusion.11
  42.6 13.4 %fusion.187 = (f32[4,128]{1,0:T(4,128)S(1)}, f32[1,4,128,704]{2,3,1,0:T(8,128)S(1)}) fusion(f32[704]{0:T(1024)S(1)} %get-tuple-element.145, bf16[1,10,134,704]{2,3,1,0:T(8,128)(2,1)S(1)} %fusion.11, f32[704]{0:T(1024)S(1)} %get-tuple-element.146, f32[704]{0:T(1024)S(1)} %get-tuple-element.99, f32[704]{0:T(1024)S(1)} %get-tuple-element.100, ...), kind=kLoop, calls=%fused_computation.443 | loop fusion | flops 52985344 | bytes 36905728 | tf_op jit(solution)/shard_map/jvp()/reduce_sum | solution.py:60
  57.5 19.4 %all-gather.3.cloned.1.call-done = bf16[2816,704]{1,0:T(8,128)(2,1)} async-done(((bf16[176,704]{1,0:T(8,128)(2,1)}), bf16[2816,704]{1,0:T(8,128)(2,1)}) %all-gather.3.cloned.1.call-update) | async-done | bytes 3964944 | tf_op jit(solution)/shard_map/all_gather | solution.py:88
  76.9 17.9 %multiply_reduce_fusion.2 = (f32[2816]{0:T(1024)S(1)}, f32[512,2816]{1,0:T(8,128)}, f32[512,2816]{1,0:T(8,128)}) fusion(bf16[2816,704]{1,0:T(8,128)(2,1)} %all-gather.3.cloned.1.call-done, bf16[88,8,4,128]{3,2,1,0:T(4,128)(2,1)S(1)} %bitcast.47), kind=kOutput, calls=%fused_computation.12 | convolution fusion | flops 2125198592 | bytes 16231424 | tf_op jit(solution)/shard_map/dot_general | solution.py:86
  94.8 33.8 %psum.49 = f32[1,2816]{1,0:T(1,128)S(1)} all-reduce(f32[1,2816]{1,0:T(1,128)S(1)} %reduce_sum.583), channel_id=1, replica_groups=mesh['dp'=16,'space'=8] {'space'}, use_global_device_ids=true, to_apply=%region_4.5 | all-reduce | flops 2816 | bytes 22528 | tf_op jit(solution)/shard_map/psum | solution.py:95
  130.0 3.6 all-gather.5.cloned.1.call-done
  133.6 8.8 %multiply_reduce_fusion = (f32[2816]{0:T(1024)S(1)}, f32[2816]{0:T(1024)S(1)}, f32[2816]{0:T(1024)S(1)}, f32[512,2816]{1,0:T(8,128)}) fusion(f32[2816]{0:T(1024)S(1)} %divide_reduce_fusion, f32[512,2816]{1,0:T(8,128)} %get-tuple-element.152, f32[512,2816]{1,0:T(8,128)} %get-tuple-element.163, f32[2816]{0:T(1024)S(1)} %copy-done.19, ...), kind=kOutput, calls=%fused_computation.8 | convolution fusion | flops 2043010816 | bytes 22043648 | tf_op jit(solution)/shard_map/dot_general | solution.py:102
  143.7 33.1 %psum.50 = f32[1,2816]{1,0:T(1,128)S(1)} all-reduce(f32[1,2816]{1,0:T(1,128)S(1)} %divide_multiply_fusion), channel_id=1, replica_groups=mesh['dp'=16,'space'=8] {'space'}, use_global_device_ids=true, to_apply=%region_8.9 | all-reduce | flops 2816 | bytes 22528 | tf_op jit(solution)/shard_map/psum | solution.py:109
  176.9 7.9 %add_convert_fusion.1 = bf16[512,2816]{1,0:T(8,128)(2,1)S(1)} fusion(f32[512,2816]{1,0:T(8,128)} %get-tuple-element.152, f32[512,2816]{1,0:T(8,128)} %get-tuple-element.164, f32[512,2816]{1,0:T(8,128)} %get-tuple-element.163, f32[2816]{0:T(1024)S(1)} %multiply_reduce_fusion.6, f32[2816]{0:T(1024)S(1)} %divide_reduce_fusion, f32[2816]{0:T(1024)S(1)} %copy-done.19), kind=kLoop, calls=%fused_computation.10 | loop fusion | flops 28835840 | bytes 20218880 | tf_op jit(solution)/shard_map/convert_element_type | solution.py:111
  184.8 1.6 copy-done.9
  186.4 3.4 fusion.191
  189.8 1.7 reshape.372
  194.1 7.6 %fusion.112 = (f32[704]{0:T(1024)S(1)}, f32[704]{0:T(1024)S(1)}, f32[704]{0:T(1024)S(1)}, f32[704]{0:T(1024)S(1)}, f32[704]{0:T(1024)S(1)}, /*index=5*/f32[704]{...) fusion(bf16[1,10,134,704]{2,3,1,0:T(8,128)(2,1)S(1)} %copy-done, ...), kind=kLoop, calls=%fused_computation.239 | loop fusion | flops 21974656 | bytes 17363200 | tf_op jit(solution)/shard_map/reduce_sum | solution.py:54
  201.8 4.0 fusion.109
  205.8 10.9 %fusion.111 = (f32[704]{0:T(1024)S(1)}, f32[704]{0:T(1024)S(1)}, f32[704]{0:T(1024)S(1)}, f32[704]{0:T(1024)S(1)}, f32[704]{0:T(1024)S(1)}, /*index=5*/f32[704]{...) fusion(f32[1,4,128,704]{2,3,1,0:T(8,128)S(1)} %get-tuple-elemen, ...), kind=kLoop, calls=%fused_computation.238 | loop fusion | flops 19451520 | bytes 14468608 | tf_op jit(solution)/shard_map/reduce_sum | solution.py:54
  216.7 5.3 fusion.176
  223.8 6.7 %fusion.12 = f32[2816,704]{0,1:T(8,128)S(1)} fusion(f32[2816]{0:T(1024)S(1)} %copy-done.21, f32[2816]{0:T(1024)S(1)} %divide_reduce_fusion, f32[2816]{0:T(1024)S(1)} %copy-done.19, bf16[88,8,4,128]{3,2,1,0:T(4,128)(2,1)S(1)} %bitcast.46, f32[512,2816]{1,0:T(8,128)} %get-tuple-element.152, f32[512,2816]{1,0:T(8,128)} %get-tuple-element.163), kind=kOutput, calls=%fused_computation.40 | convolution fusion | flops 2040135680 | bytes 20218880 | tf_op jit(solution)/shard_map/dot_general | solution.py:120
  230.4 9.1 %pad_maximum_fusion = f32[2816,1408]{0,1:T(8,128)} fusion(f32[2816,704]{0,1:T(8,128)S(1)} %fusion.12, f32[2816,704]{0,1:T(8,128)} %fusion.176), kind=kLoop, calls=%fused_computation | loop fusion | flops 3964928 | bytes 31719424 | tf_op jit(solution)/shard_map/concatenate | solution.py:124
  239.6 17.2 %copy.39 = f32[2816,1408]{1,0:T(8,128)} copy(f32[2816,1408]{0,1:T(8,128)} %pad_maximum_fusion) | data formatting | bytes 31719424
  256.8 1.5 fusion.189
  258.3 1.3 collective-permute-start.2
  260.9 96.6 %all-reduce.2 = (f32[704]{0:T(1024)S(1)}, f32[2816]{0:T(1024)S(1)}, f32[2816]{0:T(1024)S(1)}) all-reduce(f32[704]{0:T(1024)S(1)} %get-tuple-element.80, f32[2816]{0:T(1024)S(1)} %get-tuple-element.35, f32[2816]{0:T(1024)S(1)} %get-tuple-element.37), channel_id=1, replica_groups=mesh['dp'=16,'space'=8] {'dp','space'}, use_global_device_ids=true, to_apply=%region_62.63 | all-reduce | flops 6336 | bytes 50688 | tf_op jit(solution)/shard_map/psum | solution.py:133
  358.7 17.2 %all-reduce.6.cloned.1.call-done = f32[7,7,704]{2,1,0:T(8,128)} async-done(((f32[7,7,704]{2,1,0:T(8,128)}), f32[7,7,704]{2,1,0:T(8,128)}) %all-reduce.6.cloned.1.call-update) | async-done | bytes 138000 | tf_op jit(solution)/shard_map/psum | solution.py:133
  375.9 1.6 broadcast_multiply_fusion
  377.5 5.8 select_maximum_fusion
  383.4 140.4 %reduce-scatter.4.cloned.1.call-done = f32[176,1408]{1,0:T(8,128)} async-done(((f32[2816,1408]{1,0:T(8,128)}), f32[176,1408]{1,0:T(8,128)}) %reduce-scatter.4.cloned.1.call-update) | async-done | bytes 991248
  523.7 2.8 copy.40
  526.5 45.2 %fusion.126 = f32[1,4,128,704]{2,3,1,0:T(8,128)} fusion(f32[1,4,128,704]{2,3,1,0:T(8,128)S(1)} %get-tuple-element.150, f32[1,3,128,704]{2,3,1,0:T(8,128)S(1)} %collective-permute-done.2, f32[1,3,128,704]{2,3,1,0:T(8,128)} %collective-permute-done.3, f32[1,10,134,704]{2,3,1,0:T(8,128)} %select_maximum_fusion, bf16[1,4,128,704]{2,3,1,0:T(8,128)(2,1)S(1)} %copy-done.16, ...), kind=kLoop, calls=%fused_computation.253 | loop fusion | flops 38207488 | bytes 66462464 | tf_op jit(solution)/shard_map/add | solution.py:132
  571.7 36.9 %all-reduce.8.cloned.1.call-done = f32[176,1408]{0,1:T(8,128)} async-done(((f32[176,1408]{0,1:T(8,128)}), f32[176,1408]{0,1:T(8,128)}) %all-reduce.8.cloned.1.call-update) | async-done | bytes 991248 | tf_op jit(solution)/shard_map/psum | solution.py:126
  608.6 1.4 slice_multiply_fusion.42
  (158 shorter events, 16.5 us)
Async XLA Ops:
  7.2 8.1 %copy-start.23 = (f32[150]{0:T(256)S(1)}, f32[150]{0:T(256)}, u32[]{:S(2)}) copy-start(f32[150]{0:T(256)} %param.19) | copy-start | bytes 1804
  7.2 8.1 %copy-start.22 = (s32[1,4,128]{2,1,0:T(4,128)S(1)}, s32[1,4,128]{2,1,0:T(4,128)}, u32[]{:S(2)}) copy-start(s32[1,4,128]{2,1,0:T(4,128)} %param.18) | copy-start | bytes 6148
  7.2 8.3 %copy-start.15 = (bf16[1,4,128,704]{2,3,1,0:T(8,128)(2,1)S(1)}, bf16[1,4,128,704]{2,3,1,0:T(8,128)(2,1)}, u32[]{:S(2)}) copy-start(bf16[1,4,128,704]{2,3,1,0:T(8,128)(2,1)} %param.17) | copy-start | bytes 2162692
  7.2 69.7 %all-gather.3.cloned.1.call-start = ((), (), s32[]{:S(2)}) async-start(), calls=%async_computation.1 | async-start | bytes 4595712 | tf_op jit(solution)/shard_map/all_gather | solution.py:88
  7.9 7.7 %copy-start.18 = (f32[7,7,704]{2,1,0:T(8,128)S(1)}, f32[7,7,704]{2,1,0:T(8,128)}, u32[]{:S(2)}) copy-start(f32[7,7,704]{2,1,0:T(8,128)} %param.11) | copy-start | bytes 413956
  7.9 125.7 %all-gather.5.cloned.1.call-start = ((), (), s32[]{:S(2)}) async-start(), calls=%async_computation.2 | async-start | bytes 4595712 | tf_op jit(solution)/shard_map/all_gather | solution.py:104
  9.3 30.8 %collective-permute-start.1 = (bf16[1,3,128,704]{2,3,1,0:T(8,128)(2,1)S(1)}, bf16[1,3,128,704]{2,3,1,0:T(8,128)(2,1)S(1)}, u32[]{:S(2)}, u32[]{:S(2)}) collective-permute-start(bf16[1,3,128,704]{2,3,1,0:T(8,128)(2,1)S(1)} %get-tuple-element.162), channel_id=1, source_target_pairs={{1,0},{2,1},{3,2},{4,3},{5,4},{6,5},{7,6},{9,8},{10,9},{11,10},{12... | collective-permute-start | bytes 1622024 | tf_op jit(solution)/shard_map/ppermute | solution.py:19
  10.6 29.2 %collective-permute-start = (bf16[1,3,128,704]{2,3,1,0:T(8,128)(2,1)S(1)}, bf16[1,3,128,704]{2,3,1,0:T(8,128)(2,1)S(1)}, u32[]{:S(2)}, u32[]{:S(2)}) collective-permute-start(bf16[1,3,128,704]{2,3,1,0:T(8,128)(2,1)S(1)} %get-tuple-element.161), channel_id=1, source_target_pairs={{0,1},{1,2},{2,3},{3,4},{4,5},{5,6},{6,7},{8,9},{9,10},{10,11},{11... | collective-permute-start | bytes 1622024 | tf_op jit(solution)/shard_map/ppermute | solution.py:18
  15.2 360.7 %all-reduce.6.cloned.1.call-start = ((), (), s32[]{:S(2)}) async-start(), calls=%async_computation.3 | async-start | bytes 344064 | tf_op jit(solution)/shard_map/psum | solution.py:133
  15.7 24.1 %copy-start.3 = (bf16[1,4,128,704]{2,3,1,0:T(8,128)(2,1)S(1)}, bf16[1,4,128,704]{2,3,1,0:T(8,128)(2,1)}, u32[]{:S(2)}) copy-start(bf16[1,4,128,704]{2,3,1,0:T(8,128)(2,1)} %param.10) | copy-start | bytes 2162692
  16.3 117.2 %copy-start.11 = (bf16[1,4,128,704]{2,1,3,0:T(4,128)(2,1)}, bf16[1,4,128,704]{2,1,3,0:T(4,128)(2,1)S(1)}, u32[]{:S(2)}) copy-start(bf16[1,4,128,704]{2,1,3,0:T(4,128)(2,1)S(1)} %copy.34) | copy-start | bytes 2162692
  40.0 2.5 copy-start.7
  40.1 2.4 copy-start.5
  42.6 13.4 %copy-start = (bf16[1,10,134,704]{2,3,1,0:T(8,128)(2,1)}, bf16[1,10,134,704]{2,3,1,0:T(8,128)(2,1)S(1)}, u32[]{:S(2)}) copy-start(bf16[1,10,134,704]{2,3,1,0:T(8,128)(2,1)S(1)} %fusion.11) | copy-start | bytes 5660164
  57.4 37.3 %copy-start.13 = (bf16[1,4,128,704]{2,1,3,0:T(4,128)(2,1)}, bf16[1,4,128,704]{2,1,3,0:T(4,128)(2,1)S(1)}, u32[]{:S(2)}) copy-start(bf16[1,4,128,704]{2,1,3,0:T(4,128)(2,1)S(1)} %copy.33) | copy-start | bytes 2162692
  76.9 56.7 %copy-start.19 = (f32[2816]{0:T(1024)S(1)}, f32[2816]{0:T(1024)}, u32[]{:S(2)}) copy-start(f32[2816]{0:T(1024)} %param.14) | copy-start | bytes 33796
  176.9 9.6 %copy-start.24 = (bf16[2816,704]{1,0:T(8,128)(2,1)S(1)}, bf16[2816,704]{1,0:T(8,128)(2,1)}, u32[]{:S(2)}) copy-start(bf16[2816,704]{1,0:T(8,128)(2,1)} %all-gather.3.cloned.1.call-done) | copy-start | bytes 11894788
  184.8 1.6 copy-start.9
  191.6 1.1 copy-start.2
  191.6 2.5 copy-start.1
  194.1 7.6 %copy-start.4 = (bf16[1,4,128,704]{2,3,1,0:T(8,128)(2,1)S(1)}, bf16[1,4,128,704]{2,3,1,0:T(8,128)(2,1)}, u32[]{:S(2)}) copy-start(bf16[1,4,128,704]{2,3,1,0:T(8,128)(2,1)} %param.10) | copy-start | bytes 2162692
  194.1 7.6 %copy-start.6 = (bf16[1,7,128,704]{2,3,1,0:T(8,128)(2,1)S(1)}, bf16[1,7,128,704]{2,3,1,0:T(8,128)(2,1)}, u32[]{:S(2)}) copy-start(bf16[1,7,128,704]{2,3,1,0:T(8,128)(2,1)} %copy-done.5) | copy-start | bytes 3784708
  194.1 7.6 %copy-start.8 = (bf16[1,7,128,704]{2,3,1,0:T(8,128)(2,1)S(1)}, bf16[1,7,128,704]{2,3,1,0:T(8,128)(2,1)}, u32[]{:S(2)}) copy-start(bf16[1,7,128,704]{2,3,1,0:T(8,128)(2,1)} %copy-done.7) | copy-start | bytes 3784708
  205.7 10.9 %copy-start.10 = (bf16[512,2816]{1,0:T(8,128)(2,1)S(1)}, bf16[512,2816]{1,0:T(8,128)(2,1)}, u32[]{:S(2)}) copy-start(bf16[512,2816]{1,0:T(8,128)(2,1)} %copy-done.9) | copy-start | bytes 8650756
  205.8 10.9 %copy-start.14 = (bf16[1,4,128,704]{2,1,3,0:T(4,128)(2,1)S(1)}, bf16[1,4,128,704]{2,1,3,0:T(4,128)(2,1)}, u32[]{:S(2)}) copy-start(bf16[1,4,128,704]{2,1,3,0:T(4,128)(2,1)} %copy-done.13) | copy-start | bytes 2162692
  216.7 7.1 %copy-start.21 = (f32[2816]{0:T(1024)S(1)}, f32[2816]{0:T(1024)}, u32[]{:S(2)}) copy-start(f32[2816]{0:T(1024)} %param.15) | copy-start | bytes 33796
  222.0 1.8 copy-start.12
  223.7 300.1 %reduce-scatter.4.cloned.1.call-start = ((), (), s32[]{:S(2)}) async-start(), calls=%async_computation.5 | async-start | bytes 16850944
  256.8 351.8 %all-reduce.8.cloned.1.call-start = ((), (), s32[]{:S(2)}) async-start(), calls=%async_computation.4 | async-start | bytes 2883584 | tf_op jit(solution)/shard_map/psum | solution.py:126
  258.3 119.2 %collective-permute-start.2 = (f32[1,3,128,704]{2,3,1,0:T(8,128)}, f32[1,3,128,704]{2,3,1,0:T(8,128)S(1)}, u32[]{:S(2)}, u32[]{:S(2)}) collective-permute-start(f32[1,3,128,704]{2,3,1,0:T(8,128)} %get-tuple-element.158), channel_id=1, source_target_pairs={{0,1},{1,2},{2,3},{3,4},{4,5},{5,6},{6,7},{8,9},{9,10},{10,11},{11... | collective-permute-start | bytes 3244040 | tf_op jit(solution)/shard_map/ppermute | solution.py:18
  259.6 117.9 %collective-permute-start.3 = (f32[1,3,128,704]{2,3,1,0:T(8,128)}, f32[1,3,128,704]{2,3,1,0:T(8,128)}, u32[]{:S(2)}, u32[]{:S(2)}) collective-permute-start(f32[1,3,128,704]{2,3,1,0:T(8,128)} %get-tuple-element.157), channel_id=1, source_target_pairs={{1,0},{2,1},{3,2},{4,3},{5,4},{6,5},{7,6},{9,8},{10,9},{11,10},{12... | collective-permute-start | bytes 3244040 | tf_op jit(solution)/shard_map/ppermute | solution.py:19
  383.4 143.2 %copy-start.16 = (bf16[1,4,128,704]{2,3,1,0:T(8,128)(2,1)S(1)}, bf16[1,4,128,704]{2,3,1,0:T(8,128)(2,1)}, u32[]{:S(2)}) copy-start(bf16[1,4,128,704]{2,3,1,0:T(8,128)(2,1)} %param.17) | copy-start | bytes 2162692
  (2 other events, 1.4 us)
Sparse Core Ops, SparseCore 0:
  10.5 66.3 all-gather.2
  79.4 54.1 all-gather.4
  223.8 152.0 all-reduce.5
  380.9 142.8 reduce-scatter.3
  526.7 81.9 all-reduce.7
where the time goes:
time: 627 us; the launch traced here: 619 us
  waiting for transfers between devices  241 us (38%)
  blocking collectives  163 us (26%)
  other arithmetic  114 us (18%)
  matrix products  42 us (7%)
  local copies, waits for them, and re-layouts  33.5 us (5%)
  between operations  16.5 us (3%)
  starting transfers between devices  8.71 us (1%)
    unnamed x6, waiting for transfers between devices  141 us
    psum x1, blocking collectives, body(): lax.psum((kernel_part, gain_part, gamma_part, beta_part), ('dp', 'space'))  96.6 us
    add x1, other arithmetic, body(): grad_features = pixel_grad + conv_back  45.2 us
    psum x1, waiting for transfers between devices, body(): summed = lax.psum(partial_rows, 'space')  36.9 us
    psum x1, blocking collectives, body(): total_sq = lax.psum(local_sq, 'space')  33.8 us
    psum x1, blocking collectives, body(): grad_sq = lax.psum(sq_part, 'space')  33.1 us
    unnamed x61, local copies, waits for them, and re-layouts  26.6 us
    ppermute x2, waiting for transfers between devices, with_halo(): before = lax.ppermute(last, axis, up)  23.1 us
  transfers between devices with their start and end apart: 9, of which 6 were waited for; matrix products, arithmetic and copies ran while one was open for 20% of the time, Pallas kernels for 0%

commit v1 on v0

v1 whole, which is shorter than its diff:
```python
import functools
import math

import jax
import jax.numpy as jnp
from jax import lax
from jax.experimental import pallas as pl
from jax.experimental.pallas import tpu as pltpu
from jax.sharding import PartitionSpec as P

EPS_NORM = 1e-06
F32 = jnp.float32
BF16 = jnp.bfloat16
VMEM_LIMIT = 56 * 1024 * 1024
LANES = 128
PAD = 8
TILE = 8
GROUP = 4


def params(*semantics):
    return pltpu.CompilerParams(dimension_semantics=semantics, vmem_limit_bytes=VMEM_LIMIT)


def fill_padded(dst, src, first):
    rows, cols, lanes = src.shape
    zeros = jnp.zeros((rows, PAD, lanes), F32)
    dst[first : first + rows, 0:PAD, :] = zeros
    dst[first : first + rows, PAD + cols : PAD + cols + PAD, :] = zeros
    dst[first : first + rows, PAD : PAD + cols, :] = src[...].astype(F32)


def spread_taps(dst, k_ref, flip):
    for i in range(7):
        for j in range(7):
            tap = k_ref[6 - i, 6 - j : 7 - j, :] if flip else k_ref[i, j : j + 1, :]
            dst[i * 7 + j] = jnp.broadcast_to(tap, (TILE, LANES))


def taps_group(src, taps, pairs, start, acc):
    rows = sorted({r for r, _, _ in pairs})
    for j in range(7):
        for r in rows:
            todo = [(o, i) for rr, o, i in pairs if rr == r]
            xs = [src[r, start + TILE * b + PAD - 3 + j : start + TILE * b + PAD - 3 + j + TILE, :] for b in range(GROUP)]
            for o, i in todo:
                tap = taps[i * 7 + j]
                for b in range(GROUP):
                    acc[o][b] = acc[o][b] + xs[b] * tap
    return acc


def own_pairs():
    return [(s, o, s - o + 3) for s in range(4) for o in range(4)]


def halo_pairs():
    above = [(s, o, s - o) for s in range(3) for o in range(4) if 0 <= s - o <= 6]
    below = [(3 + s, o, s + 7 - o) for s in range(3) for o in range(4) if 0 <= s + 7 - o <= 6]
    return above + below


def conv_own_kernel(flip, feat, k_ref, out, xs, taps):
    fill_padded(xs, feat, 0)
    spread_taps(taps, k_ref, flip)
    cols = feat.shape[1]
    for start in range(0, cols, GROUP * TILE):
        acc = [[jnp.zeros((TILE, LANES), F32) for _ in range(GROUP)] for _ in range(4)]
        acc = taps_group(xs, taps, own_pairs(), start, acc)
        for o in range(4):
            for b in range(GROUP):
                out[o, start + TILE * b : start + TILE * (b + 1), :] = acc[o][b]


def conv_own(feat, kernel, flip):
    rows, cols, width = feat.shape
    chunks = pl.cdiv(width, LANES)
    return pl.pallas_call(
        functools.partial(conv_own_kernel, flip),
        grid=(chunks,),
        in_specs=[
            pl.BlockSpec((rows, cols, LANES), lambda c: (0, 0, c)),
            pl.BlockSpec((7, 7, LANES), lambda c: (0, 0, c)),
        ],
        out_specs=pl.BlockSpec((rows, cols, LANES), lambda c: (0, 0, c)),
        out_shape=jax.ShapeDtypeStruct((rows, cols, width), F32),
        scratch_shapes=[
            pltpu.VMEM((rows, cols + 2 * PAD, LANES), F32),
            pltpu.VMEM((49, TILE, LANES), F32),
        ],
        compiler_params=params("arbitrary"),
        name="conv_own",
    )(feat, kernel)


def conv_norm_kernel(width, chunks, part, above, below, k_ref, gain, normed, xhat, rstd, xs, taps, conv):
    c = pl.program_id(0)
    fill_padded(xs, above, 0)
    fill_padded(xs, below, 3)
    spread_taps(taps, k_ref, False)
    cols = part.shape[1]
    for start in range(0, cols, GROUP * TILE):
        acc = [
            [part[o, start + TILE * b : start + TILE * (b + 1), :] for b in range(GROUP)] for o in range(4)
        ]
        acc = taps_group(xs, taps, halo_pairs(), start, acc)
        for o in range(4):
            for b in range(GROUP):
                conv[c, o * cols + start + TILE * b : o * cols + start + TILE * (b + 1), :] = acc[o][b]

    @pl.when(c == chunks - 1)
    def _():
        last = width - (chunks - 1) * LANES
        block = 64

        def one(t, carry):
            at = pl.multiple_of(t * block, block)
            parts = [conv[n, pl.ds(at, block), :] for n in range(chunks)]
            lane = lax.broadcasted_iota(jnp.int32, (block, LANES), 1)
            inside = lane < last
            parts[-1] = jnp.where(inside, parts[-1], 0.0)
            mean = jnp.sum(sum(parts[1:], parts[0]), axis=-1, keepdims=True) / width
            centred = [p - mean for p in parts]
            centred[-1] = jnp.where(inside, centred[-1], 0.0)
            squares = [p * p for p in centred]
            var = jnp.sum(sum(squares[1:], squares[0]), axis=-1, keepdims=True) / width
            scale = lax.rsqrt(var + EPS_NORM)
            rstd[pl.ds(at, block), :] = jnp.broadcast_to(scale, (block, LANES))
            for n in range(chunks):
                w = min(LANES, width - n * LANES)
                hat = centred[n] * scale
                g = gain[:, n * LANES : n * LANES + w]
                xhat[pl.ds(at, block), n * LANES : n * LANES + w] = hat[:, :w]
                normed[pl.ds(at, block), n * LANES : n * LANES + w] = (hat[:, :w] * g).astype(BF16)
            return carry

        lax.fori_loop(0, (4 * cols) // block, one, 0)


def conv_norm(part, above, below, kernel, gain):
    rows, cols, width = part.shape
    chunks = pl.cdiv(width, LANES)
    pixels = rows * cols
    whole = lambda *s: pl.BlockSpec(s, lambda c: (0,) * len(s))
    return pl.pallas_call(
        functools.partial(conv_norm_kernel, width, chunks),
        grid=(chunks,),
        in_specs=[
            pl.BlockSpec((rows, cols, LANES), lambda c: (0, 0, c)),
            pl.BlockSpec((3, cols, LANES), lambda c: (0, 0, c)),
            pl.BlockSpec((3, cols, LANES), lambda c: (0, 0, c)),
            pl.BlockSpec((7, 7, LANES), lambda c: (0, 0, c)),
            whole(1, width),
        ],
        out_specs=[whole(pixels, width), whole(pixels, width), whole(pixels, LANES)],
        out_shape=[
            jax.ShapeDtypeStruct((pixels, width), BF16),
            jax.ShapeDtypeStruct((pixels, width), F32),
            jax.ShapeDtypeStruct((pixels, LANES), F32),
        ],
        scratch_shapes=[
            pltpu.VMEM((6, cols + 2 * PAD, LANES), F32),
            pltpu.VMEM((49, TILE, LANES), F32),
            pltpu.VMEM((chunks, pixels, LANES), F32),
        ],
        compiler_params=params("arbitrary"),
        name="conv_norm",
    )(part, above, below, kernel, gain.reshape(1, width))


def up_kernel(normed, weighted, w_up, w_down, act_ref, slope_ref, gm_ref, sums):
    nt = (((1,), (1,)), ((), ()))
    hidden = lax.dot_general(normed[...], w_up[...], nt, preferred_element_type=F32)
    gm = lax.dot_general(weighted[...], w_down[...], nt, preferred_element_type=F32)
    cdf = 0.5 * (1.0 + lax.erf(hidden * (2.0**-0.5)))
    act = hidden * cdf
    slope = cdf + hidden * (jnp.exp(hidden * hidden * -0.5) * (1.0 / math.sqrt(2.0 * math.pi)))
    act_ref[...] = act
    slope_ref[...] = slope
    gm_ref[...] = gm
    sums[0:1, :] = jnp.sum(act * act, axis=0, keepdims=True)
    sums[1:2, :] = jnp.sum(gm * act, axis=0, keepdims=True)
    sums[2:3, :] = jnp.sum(gm, axis=0, keepdims=True)
    sums[3:8, :] = jnp.zeros((5, sums.shape[1]), F32)


def up_project(normed, weighted, w_up, w_down, block=256):
    pixels, width = normed.shape
    hid = w_up.shape[0]
    whole = pl.BlockSpec((pixels, width), lambda h: (0, 0))
    rows = pl.BlockSpec((block, width), lambda h: (h, 0))
    cols = pl.BlockSpec((pixels, block), lambda h: (0, h))
    big = jax.ShapeDtypeStruct((pixels, hid), F32)
    return pl.pallas_call(
        up_kernel,
        grid=(hid // block,),
        in_specs=[whole, whole, rows, rows],
        out_specs=[cols, cols, cols, pl.BlockSpec((8, block), lambda h: (0, h))],
        out_shape=[big, big, big, jax.ShapeDtypeStruct((8, hid), F32)],
        compiler_params=params("arbitrary"),
        name="up_project",
    )(normed, weighted, w_up, w_down)


def ratio_of(sums, gamma):
    energy = jnp.sqrt(sums[0:1, :])
    hid = energy.shape[1]
    mean = jnp.sum(energy, axis=1, keepdims=True) / hid + EPS_NORM
    ratio = energy / mean
    grad_ratio = gamma * sums[1:2, :]
    shared = jnp.sum(grad_ratio * energy, axis=1, keepdims=True) / (mean * mean) / hid
    grad_energy = grad_ratio / mean - shared
    return ratio, grad_energy / energy


def down_kernel(act, weighted, sums, gamma, beta, down_term, ratio, twice, parts):
    h = pl.program_id(0)
    block = act.shape[1]

    @pl.when(h == 0)
    def _():
        r, t = ratio_of(sums, gamma[...])
        ratio[...] = r
        twice[...] = t
        parts[0:1, :] = sums[1:2, :] * r
        parts[1:2, :] = sums[2:3, :]
        parts[2:8, :] = jnp.zeros((6, r.shape[1]), F32)

    here = pl.ds(pl.multiple_of(h * block, block), block)
    a = act[...]
    mixed = (gamma[:, here] * a * ratio[:, here] + beta[:, here] + a).astype(BF16)
    down_term[...] = lax.dot_general(
        mixed, weighted[...], (((0,), (0,)), ((), ())), preferred_element_type=F32
    ).astype(BF16)


def down_grad(act, weighted, sums, gamma, beta, block=256):
    pixels, hid = act.shape
    width = weighted.shape[1]
    whole = lambda *s: pl.BlockSpec(s, lambda h: (0,) * len(s))
    return pl.pallas_call(
        down_kernel,
        grid=(hid // block,),
        in_specs=[
            pl.BlockSpec((pixels, block), lambda h: (0, h)),
            whole(pixels, width),
            whole(8, hid),
            whole(1, hid),
            whole(1, hid),
        ],
        out_specs=[
            pl.BlockSpec((block, width), lambda h: (h, 0)),
            whole(1, hid),
            whole(1, hid),
            whole(8, hid),
        ],
        out_shape=[
            jax.ShapeDtypeStruct((hid, width), BF16),
            jax.ShapeDtypeStruct((1, hid), F32),
            jax.ShapeDtypeStruct((1, hid), F32),
            jax.ShapeDtypeStruct((8, hid), F32),
        ],
        compiler_params=params("arbitrary"),
        name="down_grad",
    )(act, weighted, sums, gamma, beta)


def hidden_kernel(
    n, act, slope, gm, w_up, normed, ratio, twice, gamma, gain, xhat, rstd, up_term, grad_conv, ends, gain_part, total
):
    h = pl.program_id(0)
    a = act[...]
    grad_act = gm[...] * (gamma[...] * ratio[...] + 1.0) + a * twice[...]
    grad_hidden = (grad_act * slope[...]).astype(BF16)
    up_term[...] = lax.dot_general(
        grad_hidden, normed[...], (((0,), (0,)), ((), ())), preferred_element_type=F32
    ).astype(BF16)
    step = jnp.dot(grad_hidden, w_up[...], preferred_element_type=F32)

    @pl.when(h == 0)
    def _():
        total[...] = step

    @pl.when(h > 0)
    def _():
        total[...] += step

    @pl.when(h == n - 1)
    def _():
        pixels, width = total.shape
        block = 64

        def one(t, carry):
            at = pl.ds(pl.multiple_of(t * block, block), block)
            g = total[at, :]
            hat = xhat[at, :]
            carry = carry + jnp.sum((g * hat).reshape(block // 8, 8, width), axis=0)
            g = g * gain[...]
            mean_g = jnp.sum(g, axis=-1, keepdims=True) / width
            mean_gh = jnp.sum(g * hat, axis=-1, keepdims=True) / width
            out = rstd[at, 0:1] * (g - mean_g - hat * mean_gh)
            grad_conv[at, :] = out
            ends[at, :] = out.astype(BF16)
            return carry

        gain_part[...] = lax.fori_loop(0, pixels // block, one, jnp.zeros((8, width), F32))


def hidden_grad(act, slope, gm, w_up, normed, ratio, twice, gamma, gain, xhat, rstd, block=256):
    pixels, hid = act.shape
    width = normed.shape[1]
    n = hid // block
    whole = lambda *s: pl.BlockSpec(s, lambda h: (0,) * len(s))
    cols = pl.BlockSpec((pixels, block), lambda h: (0, h))
    vec = pl.BlockSpec((1, block), lambda h: (0, h))
    rows = pl.BlockSpec((block, width), lambda h: (h, 0))
    return pl.pallas_call(
        functools.partial(hidden_kernel, n),
        grid=(n,),
        in_specs=[
            cols, cols, cols, rows, whole(pixels, width), vec, vec, vec,
            whole(1, width), whole(pixels, width), whole(pixels, LANES),
        ],
        out_specs=[rows, whole(pixels, width), whole(pixels, width), whole(8, width)],
        out_shape=[
            jax.ShapeDtypeStruct((hid, width), BF16),
            jax.ShapeDtypeStruct((pixels, width), F32),
            jax.ShapeDtypeStruct((pixels, width), BF16),
            jax.ShapeDtypeStruct((8, width), F32),
        ],
        scratch_shapes=[pltpu.VMEM((pixels, width), F32)],
        compiler_params=params("arbitrary"),
        name="hidden_grad",
    )(act, slope, gm, w_up, normed, ratio, twice, gamma, gain.reshape(1, width), xhat, rstd)


def taps_grad_kernel(feat, above, below, grad, k_ref, ktaps, part, xs, gs, taps):
    fill_padded(xs, above, 0)
    fill_padded(xs, feat, 3)
    fill_padded(xs, below, 7)
    fill_padded(gs, grad, 0)
    spread_taps(taps, k_ref, True)
    cols = feat.shape[1]
    for start in range(0, cols, GROUP * TILE):
        acc = [[jnp.zeros((TILE, LANES), F32) for _ in range(GROUP)] for _ in range(4)]
        acc = taps_group(gs, taps, own_pairs(), start, acc)
        for o in range(4):
            for b in range(GROUP):
                part[o, start + TILE * b : start + TILE * (b + 1), :] = acc[o][b]
    for j in range(7):
        sums = [jnp.zeros((TILE, LANES), F32) for _ in range(7)]
        for start in range(0, cols, TILE):
            g = [gs[o, PAD + start : PAD + start + TILE, :] for o in range(4)]
            for r in range(10):
                x = xs[r, PAD - 3 + j + start : PAD - 3 + j + start + TILE, :]
                for o in range(4):
                    if 0 <= r - o <= 6:
                        sums[r - o] = sums[r - o] + x * g[o]
        for i in range(7):
            ktaps[i, j : j + 1, :] = jnp.sum(sums[i], axis=0, keepdims=True)


def taps_grad(feat, above, below, grad, kernel):
    rows, cols, width = feat.shape
    chunks = pl.cdiv(width, LANES)
    blk = lambda r: pl.BlockSpec((r, cols, LANES), lambda c: (0, 0, c))
    k = pl.BlockSpec((7, 7, LANES), lambda c: (0, 0, c))
    return pl.pallas_call(
        taps_grad_kernel,
        grid=(chunks,),
        in_specs=[blk(rows), blk(3), blk(3), blk(rows), k],
        out_specs=[k, blk(rows)],
        out_shape=[jax.ShapeDtypeStruct((7, 7, width), F32), jax.ShapeDtypeStruct((rows, cols, width), F32)],
        scratch_shapes=[
            pltpu.VMEM((rows + 6, cols + 2 * PAD, LANES), F32),
            pltpu.VMEM((rows, cols + 2 * PAD, LANES), F32),
            pltpu.VMEM((49, TILE, LANES), F32),
        ],
        compiler_params=params("arbitrary"),
        name="taps_grad",
    )(feat, above, below, grad, kernel)


def conv_back_kernel(part, above, below, k_ref, upstream, weight, out, xs, taps):
    fill_padded(xs, above, 0)
    fill_padded(xs, below, 3)
    spread_taps(taps, k_ref, True)
    cols = part.shape[1]
    for start in range(0, cols, GROUP * TILE):
        acc = [[None] * GROUP for _ in range(4)]
        for o in range(4):
            for b in range(GROUP):
                at = slice(start + TILE * b, start + TILE * (b + 1))
                acc[o][b] = part[o, at, :] + upstream[o, at, :].astype(F32) * weight[o, at, :]
        acc = taps_group(xs, taps, halo_pairs(), start, acc)
        for o in range(4):
            for b in range(GROUP):
                out[o, start + TILE * b : start + TILE * (b + 1), :] = acc[o][b]


def conv_back(part, above, below, kernel, upstream, weight):
    rows, cols, width = part.shape
    chunks = pl.cdiv(width, LANES)
    blk = lambda r: pl.BlockSpec((r, cols, LANES), lambda c: (0, 0, c))
    k = pl.BlockSpec((7, 7, LANES), lambda c: (0, 0, c))
    return pl.pallas_call(
        conv_back_kernel,
        grid=(chunks,),
        in_specs=[blk(rows), blk(3), blk(3), k, blk(rows), pl.BlockSpec((rows, cols, LANES), lambda c: (0, 0, 0))],
        out_specs=blk(rows),
        out_shape=jax.ShapeDtypeStruct((rows, cols, width), F32),
        scratch_shapes=[
            pltpu.VMEM((6, cols + 2 * PAD, LANES), F32),
            pltpu.VMEM((49, TILE, LANES), F32),
        ],
        compiler_params=params("arbitrary"),
        name="conv_back",
    )(part, above, below, kernel, upstream, weight)


def body(
    features, kernel, norm_gain, w_up, grn_gamma, grn_beta, w_down, upstream, labels, class_weight
):
    crops, rows, cols, width = features.shape
    feat, up = features[0], upstream[0]
    space = lax.axis_size("space")
    dp = lax.axis_size("dp")
    hid = w_up.shape[0] * dp
    pixels = rows * cols
    rising = [(i, i + 1) for i in range(space - 1)]
    falling = [(j, i) for i, j in rising]
    above = lax.ppermute(feat[rows - 3 :], "space", rising)
    below = lax.ppermute(feat[:3], "space", falling)
    w_up_all = lax.all_gather(w_up, "dp", axis=0, tiled=True)
    w_down_all = lax.all_gather(w_down, "dp", axis=0, tiled=True)

    classes = jnp.arange(class_weight.shape[0], dtype=jnp.int32)
    pixel_weight = jnp.sum(jnp.where(labels[0][..., None] == classes, class_weight, 0.0), axis=-1)
    weight = jnp.broadcast_to(pixel_weight[..., None], (rows, cols, LANES))
    weighted = (up.astype(F32) * pixel_weight[..., None]).astype(BF16).reshape(pixels, width)

    part = conv_own(feat, kernel, False)
    normed, xhat, rstd = conv_norm(part, above, below, kernel, norm_gain)
    act, slope, gm, local = up_project(normed, weighted, w_up_all, w_down_all)
    sums = lax.psum(local[:3], "space")
    sums = jnp.concatenate([sums, jnp.zeros((5, hid), F32)], axis=0)
    gamma, beta = grn_gamma.reshape(1, hid), grn_beta.reshape(1, hid)
    down_term, ratio, twice, parts = down_grad(act, weighted, sums, gamma, beta)
    up_term, grad_conv, grad_ends, gain_part = hidden_grad(
        act, slope, gm, w_up_all, normed, ratio, twice, gamma, norm_gain, xhat, rstd
    )
    grad_conv = grad_conv.reshape(rows, cols, width)
    ends = grad_ends.reshape(rows, cols, width)
    g_above = lax.ppermute(ends[rows - 3 :], "space", rising)
    g_below = lax.ppermute(ends[:3], "space", falling)
    kernel_part, back = taps_grad(feat, above, below, grad_conv, kernel)
    grad_features = conv_back(back, g_above, g_below, kernel, up, weight)

    scale = 1.0 / math.sqrt(dp * space * pixels)
    partial_rows = lax.psum_scatter(
        jnp.concatenate([up_term, down_term], axis=1), "dp", scatter_dimension=0, tiled=True
    )
    summed = lax.psum(partial_rows.astype(F32), "space")
    kernel_sum, gain_sum = lax.psum((kernel_part, jnp.sum(gain_part, axis=0)), ("dp", "space"))
    gamma_sum, beta_sum = lax.psum((parts[0], parts[1]), "dp")
    return (
        grad_features[None],
        scale * kernel_sum,
        scale * gain_sum,
        scale * summed[:, :width],
        scale * gamma_sum,
        scale * beta_sum,
        scale * summed[:, width:],
    )


def solution(mesh):
    return jax.shard_map(
        body,
        mesh=mesh,
        in_specs=(
            P("dp", "space", None, None),
            P(),
            P(),
            P("dp", None),
            P(),
            P(),
            P("dp", None),
            P("dp", "space", None, None),
            P("dp", "space", None),
            P(),
        ),
        out_specs=(P("dp", "space", None, None), P(), P(), P("dp", None), P(), P(), P("dp", None)),
        check_vma=False,
    )
```

time: 627 us -> 539 us (0.86); the launches traced: 619 us -> 538 us
  other arithmetic: 114 us -> 14.4 us
  Pallas kernels: 0 us -> 76 us
  blocking collectives: 163 us -> 223 us
  waiting for transfers between devices: 241 us -> 182 us
  matrix products: 42 us -> 0 us
  local copies, waits for them, and re-layouts: 33.5 us -> 20.1 us
    unnamed x6 -> x4, waiting for transfers between devices: 141 us -> 1.41 us
    reduce_scatter x0 -> x1, waiting for transfers between devices: none -> 83.7 us  [body(): lax.psum_scatter(jnp.concatenate([up_term, down_term], axis=1), 'dp', sca...]
    pallas_call x0 -> x7, Pallas kernels: none -> 76 us  [the longest x1 18.6 us: hidden_grad(): pl.pallas_call(functools.partial(hidden_kernel, n), grid=(n,), in_specs=[...]
    all_gather x2, waiting for transfers between devices: 23.1 us -> 84.2 us  [the longest x1 56.3 us: body(): w_down_all = lax.all_gather(w_down, 'dp', axis=0, tiled=True)]
    psum x3 -> x4, blocking collectives: 163 us -> 223 us  [the longest x1 73.5 us: body(): lax.psum((kernel_part, jnp.sum(gain_part, axis=0)), ('dp', 'space'))]
    psum x2 -> x1, waiting for transfers between devices: 54.1 us -> 0.01 us  [body(): lax.psum((kernel_part, jnp.sum(gain_part, axis=0)), ('dp', 'space'))]
    add x1 -> x0, other arithmetic: 45.2 us -> none  [body(): grad_features = pixel_grad + conv_back]
    dot_general x5 -> x0, matrix products: 42 us -> none  [the longest x1 17.9 us: body(): lax.dot_general(normed, lax.all_gather(w_up, 'dp', axis=0, tiled=True), (...]
  transfers between devices with their start and end apart: 9 -> 8, of which waited for: 6 -> 4; matrix products, arithmetic and copies ran while one was open for 20% -> 6% of each run, Pallas kernels for 0% -> 4%
where the time goes in v1:
time: 539 us; the launch traced here: 538 us
  blocking collectives  223 us (41%)
  waiting for transfers between devices  182 us (34%)
  Pallas kernels  76 us (14%)
  local copies, waits for them, and re-layouts  20.1 us (4%)
  other arithmetic  14.4 us (3%)
  between operations  13.9 us (3%)
  starting transfers between devices  7.64 us (1%)
    reduce_scatter x1, waiting for transfers between devices, body(): lax.psum_scatter(jnp.concatenate([up_term, down_term], axis=1), 'dp', sca...  83.7 us
    psum x1, blocking collectives, body(): lax.psum((kernel_part, jnp.sum(gain_part, axis=0)), ('dp', 'space'))  73.5 us
    psum x1, blocking collectives, body(): gamma_sum, beta_sum = lax.psum((parts[0], parts[1]), 'dp')  66 us
    all_gather x1, waiting for transfers between devices, body(): w_down_all = lax.all_gather(w_down, 'dp', axis=0, tiled=True)  56.3 us
    psum x1, blocking collectives, body(): summed = lax.psum(partial_rows.astype(F32), 'space')  50.2 us
    psum x1, blocking collectives, body(): sums = lax.psum(local[:3], 'space')  33.6 us
    all_gather x1, waiting for transfers between devices, body(): w_up_all = lax.all_gather(w_up, 'dp', axis=0, tiled=True)  28 us
    pallas_call x1, Pallas kernels, hidden_grad(): pl.pallas_call(functools.partial(hidden_kernel, n), grid=(n,), in_specs=[...  18.6 us
  transfers between devices with their start and end apart: 8, of which 4 were waited for; matrix products, arithmetic and copies ran while one was open for 6% of the time, Pallas kernels for 4%

profile of v1, /device:TPU:0, one launch (start us, length us, event | category | flops | bytes accessed | tf_op | source)
XLA Modules:
  0.0 537.6 jit_solution(16806145964951548178)
XLA Ops:
  8.7 2.3 slice_bitcast_fusion
  11.0 3.6 collective-permute-start
  14.6 1.3 collective-permute-start.1
  15.9 2.3 copy.35
  18.2 1.3 reshape.40.gain
  21.0 5.8 %conv_own.1.part = f32[4,128,704]{2,1,0:T(8,128)} custom-call(bf16[4,128,704]{2,1,0:T(8,128)(2,1)} %bitcast.16, f32[7,7,704]{2,1,0:T(8,128)} %k_ref.7), custom_call_target="tpu_custom_call" | custom-call | tf_op jit(solution)/shard_map/conv_own/pallas_call | solution.py:78
  27.0 1.1 fusion.weighted
  28.0 12.9 %collective-permute-done = bf16[3,128,704]{1,2,0:T(8,128)(2,1)S(1)} collective-permute-done((bf16[3,128,704]{1,2,0:T(8,128)(2,1)}, bf16[3,128,704]{1,2,0:T(8,128)(2,1)S(1)}, u32[]{:S(2)}, u32[]{:S(2)}) %collective-permute-start) | collective-permute-done | bytes 540704 | tf_op jit(solution)/shard_map/ppermute | solution.py:432
  40.9 1.1 copy.39.above
  42.0 1.1 copy.40.below
  43.1 7.9 %conv_norm.1 = (bf16[512,704]{1,0:T(8,128)(2,1)}, f32[512,704]{1,0:T(8,128)}, f32[512,128]{1,0:T(8,128)}) custom-call(f32[4,128,704]{2,1,0:T(8,128)} %conv_own.1.part, bf16[3,128,704]{2,1,0:T(8,128)(2,1)} %copy.39.above, bf16[3,128,704]{2,1,0:T(8,128)(2,1)} %copy.40.below, f32[7,7,704]{2,1,0:T(8,128)} %k_ref.7, f32[1,704]{1,0:T(1,128)} %reshape.40.gain), custom_call_target="tpu_custom_call" | custom-call | tf_op jit(solution)/shard_map/conv_norm/pallas_call | solution.py:145
  51.0 28.0 %all-gather.3.cloned.1.call-done.w_up = bf16[2816,704]{1,0:T(8,128)(2,1)} async-done(((bf16[176,704]{1,0:T(8,128)(2,1)}), bf16[2816,704]{1,0:T(8,128)(2,1)}) %all-gather.3.cloned.1.call-update) | async-done | bytes 3964944 | tf_op jit(solution)/shard_map/all_gather | solution.py:434
  79.0 56.3 %all-gather.5.cloned.1.call-done.w_down = bf16[2816,704]{1,0:T(8,128)(2,1)} async-done(((bf16[176,704]{1,0:T(8,128)(2,1)}), bf16[2816,704]{1,0:T(8,128)(2,1)}) %all-gather.5.cloned.1.call-update) | async-done | bytes 3964944 | tf_op jit(solution)/shard_map/all_gather | solution.py:435
  135.2 16.0 %up_project.1 = (f32[512,2816]{1,0:T(8,128)}, f32[512,2816]{1,0:T(8,128)}, f32[512,2816]{1,0:T(8,128)}, f32[8,2816]{1,0:T(8,128)}) custom-call(bf16[512,704]{1,0:T(8,128)(2,1)} %get-tuple-element.24.normed, bf16[512,704]{1,0:T(8,128)(2,1)} %fusion.weighted, bf16[2816,704]{1,0:T(8,128)(2,1)} %all-gather.3.cloned.1.call-done.w_up, ...), custom_call_target="tpu_custom_call" | custom-call | tf_op jit(solution)/shard_map/up_project/pallas_call | solution.py:194
  152.1 33.6 %psum.42 = f32[3,2816]{1,0:T(4,128)S(1)} all-reduce(f32[3,2816]{1,0:T(4,128)S(1)} %slice.43), channel_id=1, replica_groups=mesh['dp'=16,'space'=8] {'space'}, use_global_device_ids=true, to_apply=%region_1.2 | all-reduce | flops 8448 | bytes 67584 | tf_op jit(solution)/shard_map/psum | solution.py:445
  186.4 11.0 %down_grad.1 = (bf16[2816,704]{1,0:T(8,128)(2,1)}, f32[1,2816]{1,0:T(1,128)}, f32[1,2816]{1,0:T(1,128)}, f32[8,2816]{1,0:T(8,128)}) custom-call(f32[512,2816]{1,0:T(8,128)} %get-tuple-element.25.act, bf16[512,704]{1,0:T(8,128)(2,1)} %fusion.weighted, f32[8,2816]{1,0:T(8,128)} %concatenate.6.sums, f32[1,2816]{1,0:T(1,128)} %reshape.41.gamma, ...), custom_call_target="tpu_custom_call" | custom-call | tf_op jit(solution)/shard_map/down_grad/pallas_call | solution.py:241
  197.4 18.6 %hidden_grad.1 = (bf16[2816,704]{1,0:T(8,128)(2,1)}, f32[512,704]{1,0:T(8,128)}, bf16[512,704]{1,0:T(8,128)(2,1)}, f32[8,704]{1,0:T(8,128)}) custom-call(f32[512,2816]{1,0:T(8,128)} %get-tuple-element.25.act, f32[512,2816]{1,0:T(8,128)} %get-tuple-element.26.slope, f32[512,2816]{1,0:T(8,128)} %get-tuple-element.27.gm, ...), custom_call_target="tpu_custom_call" | custom-call | tf_op jit(solution)/shard_map/hidden_grad/pallas_call | solution.py:317
  216.0 10.3 %taps_grad.1 = (f32[7,7,704]{2,1,0:T(8,128)}, f32[4,128,704]{2,1,0:T(8,128)}) custom-call(bf16[4,128,704]{2,1,0:T(8,128)(2,1)} %bitcast.17, bf16[3,128,704]{2,1,0:T(8,128)(2,1)} %copy.39.above, bf16[3,128,704]{2,1,0:T(8,128)(2,1)} %copy.40.below, f32[4,128,704]{2,1,0:T(8,128)} %bitcast.22, f32[7,7,704]{2,1,0:T(8,128)} %k_ref.7), custom_call_target="tpu_custom_call" | custom-call | tf_op jit(solution)/shard_map/taps_grad/pallas_call | solution.py:368
  226.3 9.2 %pad_maximum_fusion = bf16[2816,1408]{1,0:T(8,128)(2,1)} fusion(bf16[2816,704]{1,0:T(8,128)(2,1)} %get-tuple-element.39, bf16[2816,704]{1,0:T(8,128)(2,1)} %get-tuple-element.38), kind=kLoop, calls=%fused_computation | loop fusion | flops 15859712 | bytes 15859712 | tf_op jit(solution)/shard_map/concatenate | solution.py:461
  235.5 1.2 copy.43
  237.1 1.3 collective-permute-start.2
  238.7 1.3 collective-permute-start.3
  240.1 73.5 %psum.44 = f32[704]{0:T(1024)S(1)} all-reduce(f32[704]{0:T(1024)S(1)} %reduce_sum.19), channel_id=1, replica_groups=mesh['dp'=16,'space'=8] {'dp','space'}, use_global_device_ids=true, to_apply=%region_4.5 | all-reduce | flops 704 | bytes 5632 | tf_op jit(solution)/shard_map/psum | solution.py:464
  315.2 66.0 %all-reduce.1 = (f32[2816]{0:T(1024)S(1)}, f32[2816]{0:T(1024)S(1)}) all-reduce(f32[2816]{0:T(1024)S(1)} %get-tuple-element.63, f32[2816]{0:T(1024)S(1)} %get-tuple-element.62), channel_id=1, replica_groups=mesh['dp'=16,'space'=8] {'dp'}, use_global_device_ids=true, to_apply=%region_7.8 | all-reduce | flops 5632 | bytes 45056 | tf_op jit(solution)/shard_map/psum | solution.py:465
  381.8 1.6 broadcast_multiply_fusion
  383.4 1.1 copy.44.above
  384.5 1.1 copy.45.below
  386.4 6.5 %conv_back.1 = f32[4,128,704]{2,1,0:T(8,128)} custom-call(f32[4,128,704]{2,1,0:T(8,128)} %get-tuple-element.34.part, bf16[3,128,704]{2,1,0:T(8,128)(2,1)} %copy.44.above, bf16[3,128,704]{2,1,0:T(8,128)(2,1)} %copy.45.below, f32[7,7,704]{2,1,0:T(8,128)} %k_ref.7, bf16[4,128,704]{2,1,0:T(8,128)(2,1)} %bitcast.19, f32[4,128,128]{2,1,0:T(8,128)} %broadcast_in_dim.22.weight), custom_call_target="tpu_custom_call" | custom-call | tf_op jit(solution)/shard_map/conv_back/pallas_call | solution.py:406
  392.9 3.1 copy.46
  396.0 83.7 %reduce-scatter.2.cloned.1.call-done = bf16[176,1408]{1,0:T(8,128)(2,1)} async-done(((bf16[2816,1408]{1,0:T(8,128)(2,1)}), bf16[176,1408]{1,0:T(8,128)(2,1)}) %reduce-scatter.2.cloned.1.call-update) | async-done | bytes 495632 | tf_op jit(solution)/shard_map/reduce_scatter | solution.py:460
  479.7 50.2 %all-reduce.6 = f32[176,1408]{1,0:T(8,128)S(1)} all-reduce(bf16[176,1408]{1,0:T(8,128)(2,1)} %reduce-scatter.2.cloned.1.call-done), channel_id=1, replica_groups=mesh['dp'=16,'space'=8] {'space'}, use_global_device_ids=true, to_apply=%region_6.7 | all-reduce | flops 247808 | bytes 1486848 | tf_op jit(solution)/shard_map/psum | solution.py:463
  529.9 1.1 slice_multiply_fusion
  (40 shorter events, 8.6 us)
Async XLA Ops:
  7.2 12.3 %copy-start = (bf16[1,4,128,704]{2,3,1,0:T(8,128)(2,1)S(1)}, bf16[1,4,128,704]{2,3,1,0:T(8,128)(2,1)}, u32[]{:S(2)}) copy-start(bf16[1,4,128,704]{2,3,1,0:T(8,128)(2,1)} %param.17) | copy-start | bytes 2162692
  7.2 12.6 %copy-start.3 = (f32[2816]{0:T(1024)S(1)}, f32[2816]{0:T(1024)}, u32[]{:S(2)}) copy-start(f32[2816]{0:T(1024)} %param.14) | copy-start | bytes 33796
  7.2 13.2 %copy-start.4 = (f32[2816]{0:T(1024)S(1)}, f32[2816]{0:T(1024)}, u32[]{:S(2)}) copy-start(f32[2816]{0:T(1024)} %param.15) | copy-start | bytes 33796
  7.2 71.8 %all-gather.3.cloned.1.call-start = ((), (), s32[]{:S(2)}) async-start(), calls=%async_computation.1 | async-start | bytes 4595712 | tf_op jit(solution)/shard_map/all_gather | solution.py:434
  7.9 127.3 %all-gather.5.cloned.1.call-start = ((), (), s32[]{:S(2)}) async-start(), calls=%async_computation.2 | async-start | bytes 4595712 | tf_op jit(solution)/shard_map/all_gather | solution.py:435
  8.7 18.1 %copy-start.5 = (s32[1,4,128]{2,1,0:T(4,128)S(1)}, s32[1,4,128]{2,1,0:T(4,128)}, u32[]{:S(2)}) copy-start(s32[1,4,128]{2,1,0:T(4,128)} %param.18) | copy-start | bytes 6148
  8.7 18.1 %copy-start.6 = (f32[150]{0:T(256)S(1)}, f32[150]{0:T(256)}, u32[]{:S(2)}) copy-start(f32[150]{0:T(256)} %param.19) | copy-start | bytes 1804
  8.7 373.1 %all-reduce.5.cloned.1.call-start = ((), (), s32[]{:S(2)}) async-start(), calls=%async_computation.3 | async-start | bytes 344064 | tf_op jit(solution)/shard_map/psum | solution.py:464
  11.0 29.9 %collective-permute-start = (bf16[3,128,704]{1,2,0:T(8,128)(2,1)}, bf16[3,128,704]{1,2,0:T(8,128)(2,1)S(1)}, u32[]{:S(2)}, u32[]{:S(2)}) collective-permute-start(bf16[3,128,704]{1,2,0:T(8,128)(2,1)} %get-tuple-element.71), channel_id=1, source_target_pairs={{0,1},{1,2},{2,3},{3,4},{4,5},{5,6},{6,7},{8,9},{9,10},{10,11},{11... | collective-permute-start | bytes 1622024 | tf_op jit(solution)/shard_map/ppermute | solution.py:432
  14.6 27.4 %collective-permute-start.1 = (bf16[3,128,704]{1,2,0:T(8,128)(2,1)}, bf16[3,128,704]{1,2,0:T(8,128)(2,1)S(1)}, u32[]{:S(2)}, u32[]{:S(2)}) collective-permute-start(bf16[3,128,704]{1,2,0:T(8,128)(2,1)} %get-tuple-element.70), channel_id=1, source_target_pairs={{1,0},{2,1},{3,2},{4,3},{5,4},{6,5},{7,6},{9,8},{10,9},{11,10},{12... | collective-permute-start | bytes 1622024 | tf_op jit(solution)/shard_map/ppermute | solution.py:433
  226.3 253.5 %reduce-scatter.2.cloned.1.call-start = ((), (), s32[]{:S(2)}) async-start(), calls=%async_computation.4 | async-start | bytes 8425472 | tf_op jit(solution)/shard_map/reduce_scatter | solution.py:460
  235.5 1.2 copy-start.1
  235.5 4.5 copy-start.2
  237.1 146.3 %collective-permute-start.2 = (bf16[3,128,704]{1,2,0:T(8,128)(2,1)S(1)}, bf16[3,128,704]{1,2,0:T(8,128)(2,1)S(1)}, u32[]{:S(2)}, u32[]{:S(2)}) collective-permute-start(bf16[3,128,704]{1,2,0:T(8,128)(2,1)S(1)} %copy.41), channel_id=1, source_target_pairs={{0,1},{1,2},{2,3},{3,4},{4,5},{5,6},{6,7},{8,9},{9,10},{10,11},{11... | collective-permute-start | bytes 1622024 | tf_op jit(solution)/shard_map/ppermute | solution.py:454
  238.7 145.7 %collective-permute-start.3 = (bf16[3,128,704]{1,2,0:T(8,128)(2,1)S(1)}, bf16[3,128,704]{1,2,0:T(8,128)(2,1)S(1)}, u32[]{:S(2)}, u32[]{:S(2)}) collective-permute-start(bf16[3,128,704]{1,2,0:T(8,128)(2,1)S(1)} %copy.42), channel_id=1, source_target_pairs={{1,0},{2,1},{3,2},{4,3},{5,4},{6,5},{7,6},{9,8},{10,9},{11,10},{12... | collective-permute-start | bytes 1622024 | tf_op jit(solution)/shard_map/ppermute | solution.py:455
Sparse Core Ops, SparseCore 0:
  10.5 68.4 all-gather.2
  81.5 53.7 all-gather.4
  226.4 145.0 all-reduce.4
  376.2 103.5 reduce-scatter.1

commit v2 on v1

--- a/solution.py
+++ b/solution.py
@@ -168,23 +168,18 @@
     )(part, above, below, kernel, gain.reshape(1, width))
 
 
-def up_kernel(normed, weighted, w_up, w_down, act_ref, slope_ref, gm_ref, sums):
+def up_kernel(normed, w_up, act_ref, slope_ref, sums):
     nt = (((1,), (1,)), ((), ()))
     hidden = lax.dot_general(normed[...], w_up[...], nt, preferred_element_type=F32)
-    gm = lax.dot_general(weighted[...], w_down[...], nt, preferred_element_type=F32)
     cdf = 0.5 * (1.0 + lax.erf(hidden * (2.0**-0.5)))
     act = hidden * cdf
     slope = cdf + hidden * (jnp.exp(hidden * hidden * -0.5) * (1.0 / math.sqrt(2.0 * math.pi)))
     act_ref[...] = act
     slope_ref[...] = slope
-    gm_ref[...] = gm
-    sums[0:1, :] = jnp.sum(act * act, axis=0, keepdims=True)
-    sums[1:2, :] = jnp.sum(gm * act, axis=0, keepdims=True)
-    sums[2:3, :] = jnp.sum(gm, axis=0, keepdims=True)
-    sums[3:8, :] = jnp.zeros((5, sums.shape[1]), F32)
-
-
-def up_project(normed, weighted, w_up, w_down, block=256):
+    sums[...] = jnp.sum((act * act).reshape(-1, 8, act.shape[1]), axis=0)
+
+
+def up_project(normed, w_up, block=256):
     pixels, width = normed.shape
     hid = w_up.shape[0]
     whole = pl.BlockSpec((pixels, width), lambda h: (0, 0))
@@ -194,12 +189,40 @@
     return pl.pallas_call(
         up_kernel,
         grid=(hid // block,),
-        in_specs=[whole, whole, rows, rows],
-        out_specs=[cols, cols, cols, pl.BlockSpec((8, block), lambda h: (0, h))],
-        out_shape=[big, big, big, jax.ShapeDtypeStruct((8, hid), F32)],
+        in_specs=[whole, rows],
+        out_specs=[cols, cols, pl.BlockSpec((8, block), lambda h: (0, h))],
+        out_shape=[big, big, jax.ShapeDtypeStruct((8, hid), F32)],
         compiler_params=params("arbitrary"),
         name="up_project",
-    )(normed, weighted, w_up, w_down)
+    )(normed, w_up)
+
+
+def mixed_kernel(weighted, w_down, act_ref, sq, gm_ref, sums):
+    nt = (((1,), (1,)), ((), ()))
+    gm = lax.dot_general(weighted[...], w_down[...], nt, preferred_element_type=F32)
+    gm_ref[...] = gm
+    act = act_ref[...]
+    sums[0:1, :] = jnp.sum(sq[...], axis=0, keepdims=True)
+    sums[1:2, :] = jnp.sum(gm * act, axis=0, keepdims=True)
+    sums[2:3, :] = jnp.sum(gm, axis=0, keepdims=True)
+    sums[3:4, :] = jnp.zeros((1, sums.shape[1]), F32)
+
+
+def mixed_grad(weighted, w_down, act, sq, block=256):
+    pixels, width = weighted.shape
+    hid = w_down.shape[0]
+    whole = pl.BlockSpec((pixels, width), lambda h: (0, 0))
+    rows = pl.BlockSpec((block, width), lambda h: (h, 0))
+    cols = pl.BlockSpec((pixels, block), lambda h: (0, h))
+    return pl.pallas_call(
+        mixed_kernel,
+        grid=(hid // block,),
+        in_specs=[whole, rows, cols, pl.BlockSpec((8, block), lambda h: (0, h))],
+        out_specs=[cols, pl.BlockSpec((4, block), lambda h: (0, h))],
+        out_shape=[jax.ShapeDtypeStruct((pixels, hid), F32), jax.ShapeDtypeStruct((4, hid), F32)],
+        compiler_params=params("arbitrary"),
+        name="mixed_grad",
+    )(weighted, w_down, act, sq)
 
 
 def ratio_of(sums, gamma):
@@ -213,18 +236,17 @@
     return ratio, grad_energy / energy
 
 
-def down_kernel(act, weighted, sums, gamma, beta, down_term, ratio, twice, parts):
+def down_kernel(act, weighted, sums, local, gamma, beta, down_term, ratio, twice, parts):
     h = pl.program_id(0)
     block = act.shape[1]
 
     @pl.when(h == 0)
     def _():
-        r, t = ratio_of(sums, gamma[...])
+        r, t = ratio_of(jnp.sum(sums[...], axis=0), gamma[...])
         ratio[...] = r
         twice[...] = t
-        parts[0:1, :] = sums[1:2, :] * r
-        parts[1:2, :] = sums[2:3, :]
-        parts[2:8, :] = jnp.zeros((6, r.shape[1]), F32)
+        parts[0:1, :] = local[1:2, :] * r
+        parts[1:2, :] = local[2:3, :]
 
     here = pl.ds(pl.multiple_of(h * block, block), block)
     a = act[...]
@@ -234,7 +256,7 @@
     ).astype(BF16)
 
 
-def down_grad(act, weighted, sums, gamma, beta, block=256):
+def down_grad(act, weighted, sums, local, gamma, beta, block=256):
     pixels, hid = act.shape
     width = weighted.shape[1]
     whole = lambda *s: pl.BlockSpec(s, lambda h: (0,) * len(s))
@@ -244,7 +266,8 @@
         in_specs=[
             pl.BlockSpec((pixels, block), lambda h: (0, h)),
             whole(pixels, width),
-            whole(8, hid),
+            whole(*sums.shape),
+            whole(4, hid),
             whole(1, hid),
             whole(1, hid),
         ],
@@ -252,17 +275,17 @@
             pl.BlockSpec((block, width), lambda h: (h, 0)),
             whole(1, hid),
             whole(1, hid),
-            whole(8, hid),
+            whole(2, hid),
         ],
         out_shape=[
             jax.ShapeDtypeStruct((hid, width), BF16),
             jax.ShapeDtypeStruct((1, hid), F32),
             jax.ShapeDtypeStruct((1, hid), F32),
-            jax.ShapeDtypeStruct((8, hid), F32),
+            jax.ShapeDtypeStruct((2, hid), F32),
         ],
         compiler_params=params("arbitrary"),
         name="down_grad",
-    )(act, weighted, sums, gamma, beta)
+    )(act, weighted, sums, local, gamma, beta)
 
 
 def hidden_kernel(
@@ -418,6 +441,62 @@
     )(part, above, below, kernel, upstream, weight)
 
 
+BOTH = ("dp", "space")
+STEPS = ((1, 0), (3, 0), (0, 1), (2, 0), (1, 1), (3, 1), (2, 1))
+
+
+def pairs_of(move):
+    pairs = []
+    for d in range(16):
+        for s in range(8):
+            y, z, c, x, low = move(d // 8, d // 2 % 4, d % 2, s // 2, s % 2)
+            pairs.append((d * 8 + s, (y * 8 + z * 2 + c) * 8 + x * 2 + low))
+    return pairs
+
+
+def to_other_core(value):
+    return lax.ppermute(value, BOTH, pairs_of(lambda y, z, c, x, low: (y, z, 1 - c, x, low)))
+
+
+def by_step(value, dz, dy):
+    return lax.ppermute(
+        value, BOTH, pairs_of(lambda y, z, c, x, low: ((y + dy) % 2, (z + dz) % 4, c, x, (low + dy) % 2))
+    )
+
+
+def gather_rows(shard):
+    mine = jnp.concatenate([shard] + [by_step(shard, dz, dy) for dz, dy in STEPS], axis=0)
+    return jnp.concatenate([mine, to_other_core(mine)], axis=0)
+
+
+def block_order():
+    dp = lax.axis_index("dp")
+    y, z, c = dp // 8, dp // 2 % 4, dp % 2
+    owners = [
+        ((y + dy) % 2) * 8 + ((z - dz) % 4) * 2 + core for core in (c, 1 - c) for dz, dy in ((0, 0),) + STEPS
+    ]
+    return jnp.stack(owners)
+
+
+def reduce_rows(term):
+    half = term.shape[0] // 2
+    other = to_other_core(term[half:])
+    chip = (term[:half].astype(F32) + other.astype(F32)).astype(BF16)
+    rows = half // 8
+    total = chip[:rows].astype(F32)
+    for n, (dz, dy) in enumerate(STEPS, 1):
+        total = total + by_step(chip[n * rows : (n + 1) * rows], -dz, dy).astype(F32)
+    return total
+
+
+def exchange(value, axis):
+    return lax.all_to_all(value, axis, 0, 0)
+
+
+def everyone(value, axis):
+    return exchange(jnp.broadcast_to(value, (lax.axis_size(axis),) + value.shape), axis)
+
+
 def body(
     features, kernel, norm_gain, w_up, grn_gamma, grn_beta, w_down, upstream, labels, class_weight
 ):
@@ -425,14 +504,18 @@
     feat, up = features[0], upstream[0]
     space = lax.axis_size("space")
     dp = lax.axis_size("dp")
-    hid = w_up.shape[0] * dp
+    owned = w_up.shape[0]
+    hid = owned * dp
     pixels = rows * cols
     rising = [(i, i + 1) for i in range(space - 1)]
     falling = [(j, i) for i, j in rising]
     above = lax.ppermute(feat[rows - 3 :], "space", rising)
     below = lax.ppermute(feat[:3], "space", falling)
-    w_up_all = lax.all_gather(w_up, "dp", axis=0, tiled=True)
-    w_down_all = lax.all_gather(w_down, "dp", axis=0, tiled=True)
+    w_up_all = gather_rows(w_up)
+    w_down_all = gather_rows(w_down)
+    order = block_order()
+    gamma = jnp.take(grn_gamma.reshape(dp, owned), order, axis=0).reshape(1, hid)
+    beta = jnp.take(grn_beta.reshape(dp, owned), order, axis=0).reshape(1, hid)
 
     classes = jnp.arange(class_weight.shape[0], dtype=jnp.int32)
     pixel_weight = jnp.sum(jnp.where(labels[0][..., None] == classes, class_weight, 0.0), axis=-1)
@@ -441,11 +524,10 @@
 
     part = conv_own(feat, kernel, False)
     normed, xhat, rstd = conv_norm(part, above, below, kernel, norm_gain)
-    act, slope, gm, local = up_project(normed, weighted, w_up_all, w_down_all)
-    sums = lax.psum(local[:3], "space")
-    sums = jnp.concatenate([sums, jnp.zeros((5, hid), F32)], axis=0)
-    gamma, beta = grn_gamma.reshape(1, hid), grn_beta.reshape(1, hid)
-    down_term, ratio, twice, parts = down_grad(act, weighted, sums, gamma, beta)
+    act, slope, sq = up_project(normed, w_up_all)
+    gm, local = mixed_grad(weighted, w_down_all, act, sq)
+    sums = everyone(local, "space")
+    down_term, ratio, twice, parts = down_grad(act, weighted, sums, local, gamma, beta)
     up_term, grad_conv, grad_ends, gain_part = hidden_grad(
         act, slope, gm, w_up_all, normed, ratio, twice, gamma, norm_gain, xhat, rstd
     )
@@ -457,20 +539,36 @@
     grad_features = conv_back(back, g_above, g_below, kernel, up, weight)
 
     scale = 1.0 / math.sqrt(dp * space * pixels)
-    partial_rows = lax.psum_scatter(
-        jnp.concatenate([up_term, down_term], axis=1), "dp", scatter_dimension=0, tiled=True
+    down_rows = reduce_rows(down_term)
+    up_rows = reduce_rows(up_term)
+
+    places = jnp.arange(dp)
+    place = jnp.sum(jnp.where(order[None, :] == places[:, None], places[None, :], 0), axis=1)
+    spread = jnp.take(parts.reshape(2, dp, owned), place, axis=1)
+    vector = jnp.concatenate(
+        [kernel_part.reshape(49, width), jnp.sum(gain_part, axis=0, keepdims=True), spread.reshape(-1, width)], axis=0
     )
-    summed = lax.psum(partial_rows.astype(F32), "space")
-    kernel_sum, gain_sum = lax.psum((kernel_part, jnp.sum(gain_part, axis=0)), ("dp", "space"))
-    gamma_sum, beta_sum = lax.psum((parts[0], parts[1]), "dp")
+    lines = vector.shape[0]
+    vector = jnp.pad(vector, ((0, -lines % (8 * space)), (0, 0)))
+    piece = jnp.sum(exchange(vector.reshape(space, -1, width), "space"), axis=0)
+    piece = jnp.sum(everyone(piece, "dp"), axis=0)
+    vector = scale * everyone(piece, "space").reshape(-1, width)
+    kernel_sum = vector[:49].reshape(7, 7, width)
+    gain_sum = vector[49]
+    gamma_sum, beta_sum = vector[50:lines].reshape(2, hid)
+
+    block = jnp.concatenate([up_rows, down_rows], axis=1)
+    block = block.reshape(space, owned // space, 2 * width).astype(BF16)
+    block = scale * jnp.sum(exchange(block, "space").astype(F32), axis=0)
+    block = everyone(block.astype(BF16), "space").astype(F32).reshape(owned, 2 * width)
     return (
         grad_features[None],
-        scale * kernel_sum,
-        scale * gain_sum,
-        scale * summed[:, :width],
-        scale * gamma_sum,
-        scale * beta_sum,
-        scale * summed[:, width:],
+        kernel_sum,
+        gain_sum,
+        block[:, :width],
+        gamma_sum,
+        beta_sum,
+        block[:, width:],
     )
 
 

time: 539 us -> 344 us (0.64)
  blocking collectives: 223 us -> 0 us
  waiting for transfers between devices: 182 us -> 61.6 us
  starting transfers between devices: 7.64 us -> 98 us
  local copies, waits for them, and re-layouts: 20.1 us -> 80.8 us
  between operations: 13.9 us -> 1.24 us
  Pallas kernels: 76 us -> 84.3 us
    psum x4 -> x0, blocking collectives: 223 us -> none  [the longest x1 73.5 us: body(): lax.psum((kernel_part, jnp.sum(gain_part, axis=0)), ('dp', 'space'))]
    all_gather x2 -> x0, waiting for transfers between devices: 84.2 us -> none  [the longest x1 56.3 us: body(): w_down_all = lax.all_gather(w_down, 'dp', axis=0, tiled=True)]
    reduce_scatter x1 -> x0, waiting for transfers between devices: 83.7 us -> none  [body(): lax.psum_scatter(jnp.concatenate([up_term, down_term], axis=1), 'dp', sca...]
    ppermute x0 -> x32, starting transfers between devices: none -> 62.2 us  [the longest x28 61.6 us: by_step(): lax.ppermute(value, BOTH, pairs_of(lambda y, z, c, x, low: ((y + dy) % 2,...]
    ppermute x0 -> x32, waiting for transfers between devices: none -> 31.3 us  [the longest x28 31.3 us: by_step(): lax.ppermute(value, BOTH, pairs_of(lambda y, z, c, x, low: ((y + dy) % 2,...]
    all_to_all x0 -> x6, starting transfers between devices: none -> 27.3 us  [exchange(): return lax.all_to_all(value, axis, 0, 0)]
    all_to_all x0 -> x6, waiting for transfers between devices: none -> 17.3 us  [exchange(): return lax.all_to_all(value, axis, 0, 0)]
    unnamed x17 -> x49, local copies, waits for them, and re-layouts: 6.59 us -> 21.1 us
  transfers between devices with their start and end apart: 8 -> 42, of which waited for: 4 -> 12; matrix products, arithmetic and copies ran while one was open for 6% -> 24% of each run, Pallas kernels for 4% -> 9%
where the time goes in v2:
time: 344 us; the launch traced here: 338 us
  starting transfers between devices  98 us (28%)
  Pallas kernels  84.3 us (25%)
  local copies, waits for them, and re-layouts  80.8 us (23%)
  waiting for transfers between devices  61.6 us (18%)
  other arithmetic  12.3 us (4%)
    ppermute x28, starting transfers between devices, by_step(): lax.ppermute(value, BOTH, pairs_of(lambda y, z, c, x, low: ((y + dy) % 2,...  61.6 us
    ppermute x28, waiting for transfers between devices, by_step(): lax.ppermute(value, BOTH, pairs_of(lambda y, z, c, x, low: ((y + dy) % 2,...  31.3 us
    all_to_all x6, starting transfers between devices, exchange(): return lax.all_to_all(value, axis, 0, 0)  27.3 us
    unnamed x49, local copies, waits for them, and re-layouts  21.1 us
    pallas_call x1, Pallas kernels, hidden_grad(): pl.pallas_call(functools.partial(hidden_kernel, n), grid=(n,), in_specs=[...  18.6 us
    all_to_all x6, waiting for transfers between devices, exchange(): return lax.all_to_all(value, axis, 0, 0)  17.3 us
    ppermute x4, local copies, waits for them, and re-layouts, to_other_core(): lax.ppermute(value, BOTH, pairs_of(lambda y, z, c, x, low: (y, z, 1 - c,...  13.5 us
    ppermute x1, waiting for transfers between devices, body(): above = lax.ppermute(feat[rows - 3:], 'space', rising)  13 us
  transfers between devices with their start and end apart: 42, of which 12 were waited for; matrix products, arithmetic and copies ran while one was open for 24% of the time, Pallas kernels for 9%

profile of v2, /device:TPU:0, one launch (start us, length us, event | category | flops | bytes accessed | tf_op | source)
XLA Modules:
  0.0 338.3 jit_solution(2088711362526477290)
XLA Ops:
  13.9 4.7 %collective-permute-start.15 = (bf16[176,704]{1,0:T(8,128)(2,1)}, bf16[176,704]{1,0:T(8,128)(2,1)S(1)}, u32[]{:S(2)}, u32[]{:S(2)}) collective-permute-start(bf16[176,704]{1,0:T(8,128)(2,1)} %param.18), channel_id=1, source_target_pairs={{0,113},{1,112},{2,115},{3,114},{4,117},{5,116},{6,119},{7,118},{8... | collective-permute-start | bytes 743432 | tf_op jit(solution)/shard_map/ppermute | solution.py:462
  19.5 8.3 %collective-permute-start.16 = (bf16[176,704]{1,0:T(8,128)(2,1)S(1)}, bf16[176,704]{1,0:T(8,128)(2,1)S(1)}, u32[]{:S(2)}, u32[]{:S(2)}) collective-permute-start(bf16[176,704]{1,0:T(8,128)(2,1)S(1)} %copy-done.7), channel_id=1, source_target_pairs={{0,97},{1,96},{2,99},{3,98},{4,101},{5,100},{6,103},{7,102},{8,105... | collective-permute-start | bytes 743432 | tf_op jit(solution)/shard_map/ppermute | solution.py:462
  29.5 3.2 collective-permute-start.3
  38.2 3.5 %collective-permute-start.6 = (bf16[176,704]{1,0:T(8,128)(2,1)S(1)}, bf16[176,704]{1,0:T(8,128)(2,1)}, u32[]{:S(2)}, u32[]{:S(2)}) collective-permute-start(bf16[176,704]{1,0:T(8,128)(2,1)S(1)} %copy-done.8), channel_id=1, source_target_pairs={{0,81},{1,80},{2,83},{3,82},{4,85},{5,84},{6,87},{7,86},{8,89},{9,... | collective-permute-start | bytes 743432 | tf_op jit(solution)/shard_map/ppermute | solution.py:462
  42.5 4.1 %copy.66 = bf16[1408,704]{0,1:T(8,128)(2,1)} copy(bf16[1408,704]{1,0:T(8,128)(2,1)} %get-tuple-element.99) | data formatting | bytes 3964928 | tf_op jit(solution)/shard_map/concatenate | solution.py:468
  46.6 4.7 %collective-permute-done.2 = bf16[176,704]{1,0:T(8,128)(2,1)S(1)} collective-permute-done((bf16[176,704]{1,0:T(8,128)(2,1)S(1)}, bf16[176,704]{1,0:T(8,128)(2,1)S(1)}, u32[]{:S(2)}, u32[]{:S(2)}) %collective-permute-start.2) | collective-permute-done | bytes 247840 | tf_op jit(solution)/shard_map/ppermute | solution.py:462
  66.5 3.7 %collective-permute-start = (bf16[3,128,704]{1,2,0:T(8,128)(2,1)}, bf16[3,128,704]{1,2,0:T(8,128)(2,1)S(1)}, u32[]{:S(2)}, u32[]{:S(2)}) collective-permute-start(bf16[3,128,704]{1,2,0:T(8,128)(2,1)} %get-tuple-element.98), channel_id=1, source_target_pairs={{0,1},{1,2},{2,3},{3,4},{4,5},{5,6},{6,7},{8,9},{9,10},{10,11},{11... | collective-permute-start | bytes 1622024 | tf_op jit(solution)/shard_map/ppermute | solution.py:512
  74.4 5.8 %conv_own.1.part = f32[4,128,704]{2,1,0:T(8,128)} custom-call(bf16[4,128,704]{2,1,0:T(8,128)(2,1)} %bitcast.42, f32[7,7,704]{2,1,0:T(8,128)} %k_ref.7), custom_call_target="tpu_custom_call" | custom-call | tf_op jit(solution)/shard_map/conv_own/pallas_call | solution.py:78
  81.3 13.0 %collective-permute-done = bf16[3,128,704]{1,2,0:T(8,128)(2,1)S(1)} collective-permute-done((bf16[3,128,704]{1,2,0:T(8,128)(2,1)}, bf16[3,128,704]{1,2,0:T(8,128)(2,1)S(1)}, u32[]{:S(2)}, u32[]{:S(2)}) %collective-permute-start) | collective-permute-done | bytes 540704 | tf_op jit(solution)/shard_map/ppermute | solution.py:512
  96.4 7.9 %conv_norm.1 = (bf16[512,704]{1,0:T(8,128)(2,1)}, f32[512,704]{1,0:T(8,128)}, f32[512,128]{1,0:T(8,128)}) custom-call(f32[4,128,704]{2,1,0:T(8,128)} %conv_own.1.part, bf16[3,128,704]{2,1,0:T(8,128)(2,1)} %copy.68.above, bf16[3,128,704]{2,1,0:T(8,128)(2,1)} %copy.69.below, f32[7,7,704]{2,1,0:T(8,128)} %k_ref.7, f32[1,704]{1,0:T(1,128)} %reshape.103.gain), custom_call_target="tpu_custom_call" | custom-call | tf_op jit(solution)/shard_map/conv_norm/pallas_call | solution.py:145
  112.9 12.3 %up_project.1 = (f32[512,2816]{1,0:T(8,128)}, f32[512,2816]{1,0:T(8,128)}, f32[8,2816]{1,0:T(8,128)}) custom-call(bf16[512,704]{1,0:T(8,128)(2,1)} %get-tuple-element.26.normed, bf16[2816,704]{1,0:T(8,128)(2,1)} %constant_dynamic-update-slice_fusion.8.w_up), custom_call_target="tpu_custom_call" | custom-call | tf_op jit(solution)/shard_map/up_project/pallas_call | solution.py:189
  125.2 12.1 %mixed_grad.1 = (f32[512,2816]{1,0:T(8,128)}, f32[4,2816]{1,0:T(4,128)}) custom-call(bf16[512,704]{1,0:T(8,128)(2,1)} %fusion.weighted, bf16[2816,704]{1,0:T(8,128)(2,1)} %constant_dynamic-update-slice_fusion.25.w_down, f32[512,2816]{1,0:T(8,128)} %get-tuple-element.27.act_ref.act, f32[8,2816]{1,0:T(8,128)} %get-tuple-element.29.sq), custom_call_target="tpu_custom_call" | custom-call | tf_op jit(solution)/shard_map/mixed_grad/pallas_call | solution.py:217
  138.8 6.1 %all-to-all-start = ((f32[8,4,2816]{2,1,0:T(4,128)}), f32[8,4,2816]{2,1,0:T(4,128)S(1)}, u32[]{:S(2)}, u32[]{:S(2)}) async-start(f32[8,4,2816]{2,1,0:T(4,128)} %broadcast_in_dim.70), calls=%async_computation | async-start | bytes 720896 | tf_op jit(solution)/shard_map/all_to_all | solution.py:493
  147.5 5.2 %all-to-all-done.sums = f32[8,4,2816]{2,1,0:T(4,128)S(1)} async-done(((f32[8,4,2816]{2,1,0:T(4,128)}), f32[8,4,2816]{2,1,0:T(4,128)S(1)}, u32[]{:S(2)}, u32[]{:S(2)}) %all-to-all-start) | async-done | bytes 360480 | tf_op jit(solution)/shard_map/all_to_all | solution.py:493
  153.5 11.1 %down_grad.1 = (bf16[2816,704]{1,0:T(8,128)(2,1)}, f32[1,2816]{1,0:T(1,128)}, f32[1,2816]{1,0:T(1,128)}, f32[2,2816]{1,0:T(2,128)}) custom-call(f32[512,2816]{1,0:T(8,128)} %get-tuple-element.27.act_ref.act, bf16[512,704]{1,0:T(8,128)(2,1)} %fusion.weighted, f32[8,4,2816]{2,1,0:T(4,128)} %copy-done.4, f32[4,2816]{1,0:T(4,128)} %get-tuple-element.31.local, ...), custom_call_target="tpu_custom_call" | custom-call | tf_op jit(solution)/shard_map/down_grad/pallas_call | solution.py:263
  164.6 18.6 %hidden_grad.1 = (bf16[2816,704]{1,0:T(8,128)(2,1)}, f32[512,704]{1,0:T(8,128)}, bf16[512,704]{1,0:T(8,128)(2,1)}, f32[8,704]{1,0:T(8,128)}) custom-call(f32[512,2816]{1,0:T(8,128)} %get-tuple-element.27.act_ref.act, f32[512,2816]{1,0:T(8,128)} %get-tuple-element.28.slope, f32[512,2816]{1,0:T(8,128)} %get-tuple-element.30.gm, ...), custom_call_target="tpu_custom_call" | custom-call | tf_op jit(solution)/shard_map/hidden_grad/pallas_call | solution.py:340
  192.8 10.3 %taps_grad.1 = (f32[7,7,704]{2,1,0:T(8,128)}, f32[4,128,704]{2,1,0:T(8,128)}) custom-call(bf16[4,128,704]{2,1,0:T(8,128)(2,1)} %bitcast.43, bf16[3,128,704]{2,1,0:T(8,128)(2,1)} %copy.68.above, bf16[3,128,704]{2,1,0:T(8,128)(2,1)} %copy.69.below, f32[4,128,704]{2,1,0:T(8,128)} %bitcast.48, f32[7,7,704]{2,1,0:T(8,128)} %k_ref.7), custom_call_target="tpu_custom_call" | custom-call | tf_op jit(solution)/shard_map/taps_grad/pallas_call | solution.py:391
  204.8 4.0 %all-to-all-start.1 = ((f32[8,8,704]{2,1,0:T(8,128)}), f32[8,8,704]{2,1,0:T(8,128)}, u32[]{:S(2)}, u32[]{:S(2)}) async-start(f32[8,8,704]{2,1,0:T(8,128)} %fusion.1), calls=%async_computation.1 | async-start | bytes 393216 | tf_op jit(solution)/shard_map/all_to_all | solution.py:493
  208.8 4.0 %copy.78 = bf16[1408,704]{1,0:T(8,128)(2,1)} copy(bf16[1408,704]{0,1:T(8,128)(2,1)} %collective-permute-done.20) | data formatting | bytes 3964928 | tf_op jit(solution)/shard_map/ppermute | solution.py:458
  216.9 3.3 collective-permute-start.21
  226.2 4.0 %copy.80 = bf16[1408,704]{1,0:T(8,128)(2,1)} copy(bf16[1408,704]{0,1:T(8,128)(2,1)} %collective-permute-done.28) | data formatting | bytes 3964928 | tf_op jit(solution)/shard_map/ppermute | solution.py:458
  234.2 3.8 %collective-permute-done.21 = bf16[176,704]{1,0:T(8,128)(2,1)S(1)} collective-permute-done((bf16[176,704]{1,0:T(8,128)(2,1)}, bf16[176,704]{1,0:T(8,128)(2,1)S(1)}, u32[]{:S(2)}, u32[]{:S(2)}) %collective-permute-start.21) | collective-permute-done | bytes 247840 | tf_op jit(solution)/shard_map/ppermute | solution.py:462
  241.1 4.2 %collective-permute-start.27 = (bf16[176,704]{1,0:T(8,128)(2,1)}, bf16[176,704]{1,0:T(8,128)(2,1)}, u32[]{:S(2)}, u32[]{:S(2)}) collective-permute-start(bf16[176,704]{1,0:T(8,128)(2,1)} %get-tuple-element.80), channel_id=1, source_target_pairs={{0,97},{1,96},{2,99},{3,98},{4,101},{5,100},{6,103},{7,102},{8,105... | collective-permute-start | bytes 743432 | tf_op jit(solution)/shard_map/ppermute | solution.py:462
  253.0 3.6 %all-to-all-start.2 = ((f32[16,8,704]{2,1,0:T(8,128)}), f32[16,8,704]{2,1,0:T(8,128)S(1)}, u32[]{:S(2)}, u32[]{:S(2)}) async-start(f32[16,8,704]{2,1,0:T(8,128)} %broadcast_in_dim.78), calls=%async_computation.2 | async-start | bytes 786432 | tf_op jit(solution)/shard_map/all_to_all | solution.py:493
  277.9 7.0 %collective-permute-done.34 = bf16[176,704]{1,0:T(8,128)(2,1)S(1)} collective-permute-done((bf16[176,704]{1,0:T(8,128)(2,1)}, bf16[176,704]{1,0:T(8,128)(2,1)S(1)}, u32[]{:S(2)}, u32[]{:S(2)}) %collective-permute-start.34) | collective-permute-done | bytes 247840 | tf_op jit(solution)/shard_map/ppermute | solution.py:462
  285.0 6.0 %collective-permute-done.35 = bf16[176,704]{1,0:T(8,128)(2,1)S(1)} collective-permute-done((bf16[176,704]{1,0:T(8,128)(2,1)}, bf16[176,704]{1,0:T(8,128)(2,1)S(1)}, u32[]{:S(2)}, u32[]{:S(2)}) %collective-permute-start.35) | collective-permute-done | bytes 247840 | tf_op jit(solution)/shard_map/ppermute | solution.py:462
  293.5 4.4 %all-to-all-start.4 = ((bf16[8,22,1408]{2,1,0:T(8,128)(2,1)}), bf16[8,22,1408]{2,1,0:T(8,128)(2,1)S(1)}, u32[]{:S(2)}, u32[]{:S(2)}) async-start(bf16[8,22,1408]{2,1,0:T(8,128)(2,1)} %convert_element_type.115), calls=%async_computation.4 | async-start | bytes 1081344 | tf_op jit(solution)/shard_map/all_to_all | solution.py:493
  302.1 6.3 %conv_back.1 = f32[4,128,704]{2,1,0:T(8,128)} custom-call(f32[4,128,704]{2,1,0:T(8,128)} %get-tuple-element.37.part, bf16[3,128,704]{2,1,0:T(8,128)(2,1)} %copy.73.above, bf16[3,128,704]{2,1,0:T(8,128)(2,1)} %copy.74.below, f32[7,7,704]{2,1,0:T(8,128)} %k_ref.7, bf16[4,128,704]{2,1,0:T(8,128)(2,1)} %bitcast.45, f32[4,128,128]{2,1,0:T(8,128)} %broadcast_in_dim.71.weight), custom_call_target="tpu_custom_call" | custom-call | tf_op jit(solution)/shard_map/conv_back/pallas_call | solution.py:429
  312.1 5.7 %all-to-all-start.3 = ((f32[8,8,704]{2,1,0:T(8,128)}), f32[8,8,704]{2,1,0:T(8,128)S(1)}, u32[]{:S(2)}, u32[]{:S(2)}) async-start(f32[8,8,704]{2,1,0:T(8,128)} %broadcast_in_dim.79), calls=%async_computation.3 | async-start | bytes 393216 | tf_op jit(solution)/shard_map/all_to_all | solution.py:493
  317.9 6.6 %all-to-all-done.3 = f32[8,8,704]{2,1,0:T(8,128)S(1)} async-done(((f32[8,8,704]{2,1,0:T(8,128)}), f32[8,8,704]{2,1,0:T(8,128)S(1)}, u32[]{:S(2)}, u32[]{:S(2)}) %all-to-all-start.3) | async-done | bytes 180256 | tf_op jit(solution)/shard_map/all_to_all | solution.py:493
  325.3 3.5 %all-to-all-start.5 = ((bf16[8,22,1408]{2,1,0:T(8,128)(2,1)}), bf16[8,22,1408]{2,1,0:T(8,128)(2,1)S(1)}, u32[]{:S(2)}, u32[]{:S(2)}) async-start(bf16[8,22,1408]{2,1,0:T(8,128)(2,1)} %broadcast_in_dim.80), calls=%async_computation.5 | async-start | bytes 1081344 | tf_op jit(solution)/shard_map/all_to_all | solution.py:493
  331.5 5.5 %all-to-all-done.5 = bf16[8,22,1408]{2,1,0:T(8,128)(2,1)S(1)} async-done(((bf16[8,22,1408]{2,1,0:T(8,128)(2,1)}), bf16[8,22,1408]{2,1,0:T(8,128)(2,1)S(1)}, u32[]{:S(2)}, u32[]{:S(2)}) %all-to-all-start.5) | async-done | bytes 495648 | tf_op jit(solution)/shard_map/all_to_all | solution.py:493
  (185 shorter events, 130.6 us)
Async XLA Ops:
  4.9 23.7 %collective-permute-start.12 = (bf16[176,704]{1,0:T(8,128)(2,1)}, bf16[176,704]{1,0:T(8,128)(2,1)S(1)}, u32[]{:S(2)}, u32[]{:S(2)}) collective-permute-start(bf16[176,704]{1,0:T(8,128)(2,1)} %param.18), channel_id=1, source_target_pairs={{0,65},{1,64},{2,67},{3,66},{4,69},{5,68},{6,71},{7,70},{8,73},{9,... | collective-permute-start | bytes 743432 | tf_op jit(solution)/shard_map/ppermute | solution.py:462
  7.9 21.5 %collective-permute-start.13 = (bf16[176,704]{1,0:T(8,128)(2,1)}, bf16[176,704]{1,0:T(8,128)(2,1)S(1)}, u32[]{:S(2)}, u32[]{:S(2)}) collective-permute-start(bf16[176,704]{1,0:T(8,128)(2,1)} %param.18), channel_id=1, source_target_pairs={{0,32},{1,33},{2,34},{3,35},{4,36},{5,37},{6,38},{7,39},{8,40},{9,... | collective-permute-start | bytes 743432 | tf_op jit(solution)/shard_map/ppermute | solution.py:462
  9.7 23.8 %collective-permute-start.14 = (bf16[176,704]{1,0:T(8,128)(2,1)}, bf16[176,704]{1,0:T(8,128)(2,1)S(1)}, u32[]{:S(2)}, u32[]{:S(2)}) collective-permute-start(bf16[176,704]{1,0:T(8,128)(2,1)} %param.18), channel_id=1, source_target_pairs={{0,81},{1,80},{2,83},{3,82},{4,85},{5,84},{6,87},{7,86},{8,89},{9,... | collective-permute-start | bytes 743432 | tf_op jit(solution)/shard_map/ppermute | solution.py:462
  13.9 22.5 %collective-permute-start.15 = (bf16[176,704]{1,0:T(8,128)(2,1)}, bf16[176,704]{1,0:T(8,128)(2,1)S(1)}, u32[]{:S(2)}, u32[]{:S(2)}) collective-permute-start(bf16[176,704]{1,0:T(8,128)(2,1)} %param.18), channel_id=1, source_target_pairs={{0,113},{1,112},{2,115},{3,114},{4,117},{5,116},{6,119},{7,118},{8... | collective-permute-start | bytes 743432 | tf_op jit(solution)/shard_map/ppermute | solution.py:462
  19.5 18.7 %collective-permute-start.16 = (bf16[176,704]{1,0:T(8,128)(2,1)S(1)}, bf16[176,704]{1,0:T(8,128)(2,1)S(1)}, u32[]{:S(2)}, u32[]{:S(2)}) collective-permute-start(bf16[176,704]{1,0:T(8,128)(2,1)S(1)} %copy-done.7), channel_id=1, source_target_pairs={{0,97},{1,96},{2,99},{3,98},{4,101},{5,100},{6,103},{7,102},{8,105... | collective-permute-start | bytes 743432 | tf_op jit(solution)/shard_map/ppermute | solution.py:462
  28.6 22.7 %collective-permute-start.2 = (bf16[176,704]{1,0:T(8,128)(2,1)S(1)}, bf16[176,704]{1,0:T(8,128)(2,1)S(1)}, u32[]{:S(2)}, u32[]{:S(2)}) collective-permute-start(bf16[176,704]{1,0:T(8,128)(2,1)S(1)} %copy-done.8), channel_id=1, source_target_pairs={{0,16},{1,17},{2,18},{3,19},{4,20},{5,21},{6,22},{7,23},{8,24},{9,... | collective-permute-start | bytes 743432 | tf_op jit(solution)/shard_map/ppermute | solution.py:462
  29.5 22.6 %collective-permute-start.3 = (bf16[176,704]{1,0:T(8,128)(2,1)S(1)}, bf16[176,704]{1,0:T(8,128)(2,1)S(1)}, u32[]{:S(2)}, u32[]{:S(2)}) collective-permute-start(bf16[176,704]{1,0:T(8,128)(2,1)S(1)} %copy-done.8), channel_id=1, source_target_pairs={{0,48},{1,49},{2,50},{3,51},{4,52},{5,53},{6,54},{7,55},{8,56},{9,... | collective-permute-start | bytes 743432 | tf_op jit(solution)/shard_map/ppermute | solution.py:462
  33.5 19.3 %collective-permute-start.4 = (bf16[176,704]{1,0:T(8,128)(2,1)S(1)}, bf16[176,704]{1,0:T(8,128)(2,1)S(1)}, u32[]{:S(2)}, u32[]{:S(2)}) collective-permute-start(bf16[176,704]{1,0:T(8,128)(2,1)S(1)} %copy-done.8), channel_id=1, source_target_pairs={{0,65},{1,64},{2,67},{3,66},{4,69},{5,68},{6,71},{7,70},{8,73},{9,... | collective-permute-start | bytes 743432 | tf_op jit(solution)/shard_map/ppermute | solution.py:462
  36.5 17.1 %collective-permute-start.5 = (bf16[176,704]{1,0:T(8,128)(2,1)S(1)}, bf16[176,704]{1,0:T(8,128)(2,1)}, u32[]{:S(2)}, u32[]{:S(2)}) collective-permute-start(bf16[176,704]{1,0:T(8,128)(2,1)S(1)} %copy-done.8), channel_id=1, source_target_pairs={{0,32},{1,33},{2,34},{3,35},{4,36},{5,37},{6,38},{7,39},{8,40},{9,... | collective-permute-start | bytes 743432 | tf_op jit(solution)/shard_map/ppermute | solution.py:462
  38.2 17.1 %collective-permute-start.6 = (bf16[176,704]{1,0:T(8,128)(2,1)S(1)}, bf16[176,704]{1,0:T(8,128)(2,1)}, u32[]{:S(2)}, u32[]{:S(2)}) collective-permute-start(bf16[176,704]{1,0:T(8,128)(2,1)S(1)} %copy-done.8), channel_id=1, source_target_pairs={{0,81},{1,80},{2,83},{3,82},{4,85},{5,84},{6,87},{7,86},{8,89},{9,... | collective-permute-start | bytes 743432 | tf_op jit(solution)/shard_map/ppermute | solution.py:462
  52.8 51.5 %collective-permute-start.17 = (bf16[1408,704]{0,1:T(8,128)(2,1)}, bf16[1408,704]{0,1:T(8,128)(2,1)}, u32[]{:S(2)}, u32[]{:S(2)}) collective-permute-start(bf16[1408,704]{0,1:T(8,128)(2,1)} %copy.66), channel_id=1, source_target_pairs={{0,8},{1,9},{2,10},{3,11},{4,12},{5,13},{6,14},{7,15},{8,0},{9,1},... | collective-permute-start | bytes 5947400 | tf_op jit(solution)/shard_map/ppermute | solution.py:458
  65.3 43.3 %collective-permute-start.9 = (bf16[1408,704]{0,1:T(8,128)(2,1)}, bf16[1408,704]{0,1:T(8,128)(2,1)}, u32[]{:S(2)}, u32[]{:S(2)}) collective-permute-start(bf16[1408,704]{0,1:T(8,128)(2,1)} %copy.63), channel_id=1, source_target_pairs={{0,8},{1,9},{2,10},{3,11},{4,12},{5,13},{6,14},{7,15},{8,0},{9,1},... | collective-permute-start | bytes 5947400 | tf_op jit(solution)/shard_map/ppermute | solution.py:458
  66.5 27.8 %collective-permute-start = (bf16[3,128,704]{1,2,0:T(8,128)(2,1)}, bf16[3,128,704]{1,2,0:T(8,128)(2,1)S(1)}, u32[]{:S(2)}, u32[]{:S(2)}) collective-permute-start(bf16[3,128,704]{1,2,0:T(8,128)(2,1)} %get-tuple-element.98), channel_id=1, source_target_pairs={{0,1},{1,2},{2,3},{3,4},{4,5},{5,6},{6,7},{8,9},{9,10},{10,11},{11... | collective-permute-start | bytes 1622024 | tf_op jit(solution)/shard_map/ppermute | solution.py:512
  70.3 25.1 %collective-permute-start.1 = (bf16[3,128,704]{1,2,0:T(8,128)(2,1)}, bf16[3,128,704]{1,2,0:T(8,128)(2,1)S(1)}, u32[]{:S(2)}, u32[]{:S(2)}) collective-permute-start(bf16[3,128,704]{1,2,0:T(8,128)(2,1)} %get-tuple-element.97), channel_id=1, source_target_pairs={{1,0},{2,1},{3,2},{4,3},{5,4},{6,5},{7,6},{9,8},{10,9},{11,10},{12... | collective-permute-start | bytes 1622024 | tf_op jit(solution)/shard_map/ppermute | solution.py:513
  187.3 21.6 %collective-permute-start.20 = (bf16[1408,704]{0,1:T(8,128)(2,1)}, bf16[1408,704]{0,1:T(8,128)(2,1)}, u32[]{:S(2)}, u32[]{:S(2)}) collective-permute-start(bf16[1408,704]{0,1:T(8,128)(2,1)} %copy.77), channel_id=1, source_target_pairs={{0,8},{1,9},{2,10},{3,11},{4,12},{5,13},{6,14},{7,15},{8,0},{9,1},... | collective-permute-start | bytes 5947400 | tf_op jit(solution)/shard_map/ppermute | solution.py:458
  191.4 32.4 %collective-permute-start.28 = (bf16[1408,704]{0,1:T(8,128)(2,1)}, bf16[1408,704]{0,1:T(8,128)(2,1)}, u32[]{:S(2)}, u32[]{:S(2)}) collective-permute-start(bf16[1408,704]{0,1:T(8,128)(2,1)} %copy.79), channel_id=1, source_target_pairs={{0,8},{1,9},{2,10},{3,11},{4,12},{5,13},{6,14},{7,15},{8,0},{9,1},... | collective-permute-start | bytes 5947400 | tf_op jit(solution)/shard_map/ppermute | solution.py:458
  204.8 46.5 %all-to-all-start.1 = ((f32[8,8,704]{2,1,0:T(8,128)}), f32[8,8,704]{2,1,0:T(8,128)}, u32[]{:S(2)}, u32[]{:S(2)}) async-start(f32[8,8,704]{2,1,0:T(8,128)} %fusion.1), calls=%async_computation.1 | async-start | bytes 393216 | tf_op jit(solution)/shard_map/all_to_all | solution.py:493
  216.9 21.1 %collective-permute-start.21 = (bf16[176,704]{1,0:T(8,128)(2,1)}, bf16[176,704]{1,0:T(8,128)(2,1)S(1)}, u32[]{:S(2)}, u32[]{:S(2)}) collective-permute-start(bf16[176,704]{1,0:T(8,128)(2,1)} %get-tuple-element.79), channel_id=1, source_target_pairs={{0,48},{1,49},{2,50},{3,51},{4,52},{5,53},{6,54},{7,55},{8,56},{9,... | collective-permute-start | bytes 743432 | tf_op jit(solution)/shard_map/ppermute | solution.py:462
  220.2 20.8 %collective-permute-start.22 = (bf16[176,704]{1,0:T(8,128)(2,1)}, bf16[176,704]{1,0:T(8,128)(2,1)S(1)}, u32[]{:S(2)}, u32[]{:S(2)}) collective-permute-start(bf16[176,704]{1,0:T(8,128)(2,1)} %get-tuple-element.85), channel_id=1, source_target_pairs={{0,16},{1,17},{2,18},{3,19},{4,20},{5,21},{6,22},{7,23},{8,24},{9,... | collective-permute-start | bytes 743432 | tf_op jit(solution)/shard_map/ppermute | solution.py:462
  220.2 25.0 %collective-permute-start.23 = (bf16[176,704]{1,0:T(8,128)(2,1)}, bf16[176,704]{1,0:T(8,128)(2,1)}, u32[]{:S(2)}, u32[]{:S(2)}) collective-permute-start(bf16[176,704]{1,0:T(8,128)(2,1)} %get-tuple-element.84), channel_id=1, source_target_pairs={{0,65},{1,64},{2,67},{3,66},{4,69},{5,68},{6,71},{7,70},{8,73},{9,... | collective-permute-start | bytes 743432 | tf_op jit(solution)/shard_map/ppermute | solution.py:462
  221.7 23.5 %collective-permute-start.24 = (bf16[176,704]{1,0:T(8,128)(2,1)}, bf16[176,704]{1,0:T(8,128)(2,1)}, u32[]{:S(2)}, u32[]{:S(2)}) collective-permute-start(bf16[176,704]{1,0:T(8,128)(2,1)} %get-tuple-element.83), channel_id=1, source_target_pairs={{0,32},{1,33},{2,34},{3,35},{4,36},{5,37},{6,38},{7,39},{8,40},{9,... | collective-permute-start | bytes 743432 | tf_op jit(solution)/shard_map/ppermute | solution.py:462
  223.8 32.8 %collective-permute-start.25 = (bf16[176,704]{1,0:T(8,128)(2,1)}, bf16[176,704]{1,0:T(8,128)(2,1)}, u32[]{:S(2)}, u32[]{:S(2)}) collective-permute-start(bf16[176,704]{1,0:T(8,128)(2,1)} %get-tuple-element.82), channel_id=1, source_target_pairs={{0,113},{1,112},{2,115},{3,114},{4,117},{5,116},{6,119},{7,118},{8... | collective-permute-start | bytes 743432 | tf_op jit(solution)/shard_map/ppermute | solution.py:462
  238.1 21.5 %collective-permute-start.26 = (bf16[176,704]{1,0:T(8,128)(2,1)}, bf16[176,704]{1,0:T(8,128)(2,1)}, u32[]{:S(2)}, u32[]{:S(2)}) collective-permute-start(bf16[176,704]{1,0:T(8,128)(2,1)} %get-tuple-element.81), channel_id=1, source_target_pairs={{0,81},{1,80},{2,83},{3,82},{4,85},{5,84},{6,87},{7,86},{8,89},{9,... | collective-permute-start | bytes 743432 | tf_op jit(solution)/shard_map/ppermute | solution.py:462
  241.1 21.5 %collective-permute-start.27 = (bf16[176,704]{1,0:T(8,128)(2,1)}, bf16[176,704]{1,0:T(8,128)(2,1)}, u32[]{:S(2)}, u32[]{:S(2)}) collective-permute-start(bf16[176,704]{1,0:T(8,128)(2,1)} %get-tuple-element.80), channel_id=1, source_target_pairs={{0,97},{1,96},{2,99},{3,98},{4,101},{5,100},{6,103},{7,102},{8,105... | collective-permute-start | bytes 743432 | tf_op jit(solution)/shard_map/ppermute | solution.py:462
  245.2 18.6 %collective-permute-start.29 = (bf16[176,704]{1,0:T(8,128)(2,1)}, bf16[176,704]{1,0:T(8,128)(2,1)}, u32[]{:S(2)}, u32[]{:S(2)}) collective-permute-start(bf16[176,704]{1,0:T(8,128)(2,1)} %get-tuple-element.86), channel_id=1, source_target_pairs={{0,48},{1,49},{2,50},{3,51},{4,52},{5,53},{6,54},{7,55},{8,56},{9,... | collective-permute-start | bytes 743432 | tf_op jit(solution)/shard_map/ppermute | solution.py:462
  245.2 21.5 %collective-permute-start.30 = (bf16[176,704]{1,0:T(8,128)(2,1)}, bf16[176,704]{1,0:T(8,128)(2,1)}, u32[]{:S(2)}, u32[]{:S(2)}) collective-permute-start(bf16[176,704]{1,0:T(8,128)(2,1)} %get-tuple-element.92), channel_id=1, source_target_pairs={{0,16},{1,17},{2,18},{3,19},{4,20},{5,21},{6,22},{7,23},{8,24},{9,... | collective-permute-start | bytes 743432 | tf_op jit(solution)/shard_map/ppermute | solution.py:462
  253.0 40.4 %all-to-all-start.2 = ((f32[16,8,704]{2,1,0:T(8,128)}), f32[16,8,704]{2,1,0:T(8,128)S(1)}, u32[]{:S(2)}, u32[]{:S(2)}) async-start(f32[16,8,704]{2,1,0:T(8,128)} %broadcast_in_dim.78), calls=%async_computation.2 | async-start | bytes 786432 | tf_op jit(solution)/shard_map/all_to_all | solution.py:493
  263.8 21.1 %collective-permute-start.34 = (bf16[176,704]{1,0:T(8,128)(2,1)}, bf16[176,704]{1,0:T(8,128)(2,1)S(1)}, u32[]{:S(2)}, u32[]{:S(2)}) collective-permute-start(bf16[176,704]{1,0:T(8,128)(2,1)} %get-tuple-element.88), channel_id=1, source_target_pairs={{0,81},{1,80},{2,83},{3,82},{4,85},{5,84},{6,87},{7,86},{8,89},{9,... | collective-permute-start | bytes 743432 | tf_op jit(solution)/shard_map/ppermute | solution.py:462
  266.7 24.2 %collective-permute-start.35 = (bf16[176,704]{1,0:T(8,128)(2,1)}, bf16[176,704]{1,0:T(8,128)(2,1)S(1)}, u32[]{:S(2)}, u32[]{:S(2)}) collective-permute-start(bf16[176,704]{1,0:T(8,128)(2,1)} %get-tuple-element.87), channel_id=1, source_target_pairs={{0,97},{1,96},{2,99},{3,98},{4,101},{5,100},{6,103},{7,102},{8,105... | collective-permute-start | bytes 743432 | tf_op jit(solution)/shard_map/ppermute | solution.py:462
  271.2 27.8 %collective-permute-start.18 = (bf16[3,128,704]{1,2,0:T(8,128)(2,1)}, bf16[3,128,704]{1,2,0:T(8,128)(2,1)S(1)}, u32[]{:S(2)}, u32[]{:S(2)}) collective-permute-start(bf16[3,128,704]{1,2,0:T(8,128)(2,1)} %copy.70), channel_id=1, source_target_pairs={{0,1},{1,2},{2,3},{3,4},{4,5},{5,6},{6,7},{8,9},{9,10},{10,11},{11... | collective-permute-start | bytes 1622024 | tf_op jit(solution)/shard_map/ppermute | solution.py:536
  273.5 26.6 %collective-permute-start.19 = (bf16[3,128,704]{1,2,0:T(8,128)(2,1)}, bf16[3,128,704]{1,2,0:T(8,128)(2,1)S(1)}, u32[]{:S(2)}, u32[]{:S(2)}) collective-permute-start(bf16[3,128,704]{1,2,0:T(8,128)(2,1)} %copy.71), channel_id=1, source_target_pairs={{1,0},{2,1},{3,2},{4,3},{5,4},{6,5},{7,6},{9,8},{10,9},{11,10},{12... | collective-permute-start | bytes 1622024 | tf_op jit(solution)/shard_map/ppermute | solution.py:537
  293.5 17.9 %all-to-all-start.4 = ((bf16[8,22,1408]{2,1,0:T(8,128)(2,1)}), bf16[8,22,1408]{2,1,0:T(8,128)(2,1)S(1)}, u32[]{:S(2)}, u32[]{:S(2)}) async-start(bf16[8,22,1408]{2,1,0:T(8,128)(2,1)} %convert_element_type.115), calls=%async_computation.4 | async-start | bytes 1081344 | tf_op jit(solution)/shard_map/all_to_all | solution.py:493
  (26 other events, 286.9 us)

commit v3 on v1

v3 whole, which is shorter than its diff:
```python
import functools
import math

import jax
import jax.numpy as jnp
from jax import lax
from jax.experimental import pallas as pl
from jax.experimental.pallas import tpu as pltpu
from jax.sharding import PartitionSpec as P

EPS_NORM = 1e-06
F32 = jnp.float32
BF16 = jnp.bfloat16
VMEM_LIMIT = 56 * 1024 * 1024
LANES = 128
PAD = 8
TILE = 8
GROUP = 4
CHUNKS = 3


def params(*semantics):
    return pltpu.CompilerParams(dimension_semantics=semantics, vmem_limit_bytes=VMEM_LIMIT)


def cost(micros):
    return pl.CostEstimate(flops=int(micros * 0.4e9), transcendentals=0, bytes_accessed=0)


def fill_padded(dst, src, first, lanes):
    rows, cols, _ = src.shape
    zeros = jnp.zeros((rows, PAD, LANES), F32)
    dst[first : first + rows, 0:PAD, :] = zeros
    dst[first : first + rows, PAD + cols : PAD + cols + PAD, :] = zeros
    dst[first : first + rows, PAD : PAD + cols, :] = src[:, :, lanes].astype(F32)


def spread_taps(dst, k_ref, flip, lanes):
    for i in range(7):
        for j in range(7):
            tap = k_ref[6 - i, 6 - j : 7 - j, lanes] if flip else k_ref[i, j : j + 1, lanes]
            dst[i * 7 + j] = jnp.broadcast_to(tap, (TILE, LANES))


def taps_group(src, taps, pairs, start, acc):
    rows = sorted({r for r, _, _ in pairs})
    for j in range(7):
        for r in rows:
            todo = [(o, i) for rr, o, i in pairs if rr == r]
            at = [start + TILE * b + PAD - 3 + j for b in range(GROUP)]
            xs = [src[r, p : p + TILE, :] for p in at]
            for o, i in todo:
                tap = taps[i * 7 + j]
                for b in range(GROUP):
                    acc[o][b] = acc[o][b] + xs[b] * tap
    return acc


def own_pairs():
    return [(s, o, s - o + 3) for s in range(4) for o in range(4)]


def halo_pairs():
    above = [(s, o, s - o) for s in range(3) for o in range(4) if 0 <= s - o <= 6]
    below = [(3 + s, o, s + 7 - o) for s in range(3) for o in range(4) if 0 <= s + 7 - o <= 6]
    return above + below


def each_chunk(body):
    def one(n, carry):
        body(n, pl.ds(pl.multiple_of(n * LANES, LANES), LANES))
        return carry

    lax.fori_loop(0, CHUNKS, one, 0)


def tile_rows(start, b):
    return slice(start + TILE * b, start + TILE * (b + 1))


def conv_own_kernel(feat, k_ref, out, xs, taps):
    cols = feat.shape[1]

    def chunk(n, lanes):
        fill_padded(xs, feat, 0, lanes)
        spread_taps(taps, k_ref, False, lanes)
        for start in range(0, cols, GROUP * TILE):
            acc = [[jnp.zeros((TILE, LANES), F32) for _ in range(GROUP)] for _ in range(4)]
            acc = taps_group(xs, taps, own_pairs(), start, acc)
            for o in range(4):
                for b in range(GROUP):
                    out[o, tile_rows(start, b), lanes] = acc[o][b]

    each_chunk(chunk)


def lane_blocks(rows, cols):
    return pl.BlockSpec((rows, cols, CHUNKS * LANES), lambda c: (0, 0, c))


def whole_block(*shape):
    return pl.BlockSpec(shape, lambda c: (0,) * len(shape))


def conv_own(feat, kernel):
    rows, cols, width = feat.shape
    return pl.pallas_call(
        conv_own_kernel,
        grid=(pl.cdiv(width, CHUNKS * LANES),),
        in_specs=[lane_blocks(rows, cols), lane_blocks(7, 7)],
        out_specs=lane_blocks(rows, cols),
        out_shape=jax.ShapeDtypeStruct((rows, cols, width), F32),
        scratch_shapes=[
            pltpu.VMEM((rows, cols + 2 * PAD, LANES), F32),
            pltpu.VMEM((49, TILE, LANES), F32),
        ],
        compiler_params=params("arbitrary"),
        cost_estimate=cost(5),
        name="conv_own",
    )(feat, kernel)


def conv_norm_kernel(width, steps, part, above, below, k_ref, gain, normed, xhat, rstd, xs, taps, conv):
    c = pl.program_id(0)
    cols = part.shape[1]

    def chunk(n, lanes):
        fill_padded(xs, above, 0, lanes)
        fill_padded(xs, below, 3, lanes)
        spread_taps(taps, k_ref, False, lanes)
        for start in range(0, cols, GROUP * TILE):
            acc = [[part[o, tile_rows(start, b), lanes] for b in range(GROUP)] for o in range(4)]
            acc = taps_group(xs, taps, halo_pairs(), start, acc)
            for o in range(4):
                for b in range(GROUP):
                    conv[c * CHUNKS + n, tile_rows(o * cols + start, b), :] = acc[o][b]

    each_chunk(chunk)

    @pl.when(c == steps - 1)
    def _():
        chunks = pl.cdiv(width, LANES)
        last = width - (chunks - 1) * LANES
        block = 64

        def one(t, carry):
            at = pl.multiple_of(t * block, block)
            parts = [conv[n, pl.ds(at, block), :] for n in range(chunks)]
            lane = lax.broadcasted_iota(jnp.int32, (block, LANES), 1)
            inside = lane < last
            parts[-1] = jnp.where(inside, parts[-1], 0.0)
            mean = jnp.sum(sum(parts[1:], parts[0]), axis=-1, keepdims=True) / width
            centred = [p - mean for p in parts]
            centred[-1] = jnp.where(inside, centred[-1], 0.0)
            squares = [p * p for p in centred]
            var = jnp.sum(sum(squares[1:], squares[0]), axis=-1, keepdims=True) / width
            scale = lax.rsqrt(var + EPS_NORM)
            rstd[pl.ds(at, block), :] = jnp.broadcast_to(scale, (block, LANES))
            for n in range(chunks):
                w = min(LANES, width - n * LANES)
                hat = centred[n] * scale
                g = gain[:, n * LANES : n * LANES + w]
                xhat[pl.ds(at, block), n * LANES : n * LANES + w] = hat[:, :w]
                normed[pl.ds(at, block), n * LANES : n * LANES + w] = (hat[:, :w] * g).astype(BF16)
            return carry

        lax.fori_loop(0, (4 * cols) // block, one, 0)


def conv_norm(part, above, below, kernel, gain):
    rows, cols, width = part.shape
    steps = pl.cdiv(width, CHUNKS * LANES)
    pixels = rows * cols
    return pl.pallas_call(
        functools.partial(conv_norm_kernel, width, steps),
        grid=(steps,),
        in_specs=[
            lane_blocks(rows, cols),
            lane_blocks(3, cols),
            lane_blocks(3, cols),
            lane_blocks(7, 7),
            whole_block(1, width),
        ],
        out_specs=[whole_block(pixels, width), whole_block(pixels, width), whole_block(pixels, LANES)],
        out_shape=[
            jax.ShapeDtypeStruct((pixels, width), BF16),
            jax.ShapeDtypeStruct((pixels, width), F32),
            jax.ShapeDtypeStruct((pixels, LANES), F32),
        ],
        scratch_shapes=[
            pltpu.VMEM((6, cols + 2 * PAD, LANES), F32),
            pltpu.VMEM((49, TILE, LANES), F32),
            pltpu.VMEM((steps * CHUNKS, pixels, LANES), F32),
        ],
        compiler_params=params("arbitrary"),
        cost_estimate=cost(7),
        name="conv_norm",
    )(part, above, below, kernel, gain.reshape(1, width))


def with_rows(h, mine, other, step):
    pl.when(h < 2)(lambda: step(mine))
    pl.when(h >= 2)(lambda: step(other))


def half_rows(block, width):
    mine = pl.BlockSpec((block, width), lambda h: (jnp.minimum(h, 1), 0))
    other = pl.BlockSpec((block, width), lambda h: (jnp.maximum(h - 2, 0), 0))
    return mine, other


def up_kernel(normed, w_mine, w_other, act_ref, slope_ref, sums):
    def step(w):
        nt = (((1,), (1,)), ((), ()))
        hidden = lax.dot_general(normed[...], w[...], nt, preferred_element_type=F32)
        cdf = 0.5 * (1.0 + lax.erf(hidden * (2.0**-0.5)))
        act = hidden * cdf
        slope_ref[0] = cdf + hidden * (jnp.exp(hidden * hidden * -0.5) * (1.0 / math.sqrt(2.0 * math.pi)))
        act_ref[0] = act
        sums[0] = jnp.sum((act * act).reshape(-1, 8, act.shape[1]), axis=0)

    with_rows(pl.program_id(0), w_mine, w_other, step)


def up_project(normed, w_up):
    pixels, width = normed.shape
    block = w_up[0].shape[0] // 2
    cols = pl.BlockSpec((1, pixels, block), lambda h: (h, 0, 0))
    big = jax.ShapeDtypeStruct((4, pixels, block), F32)
    return pl.pallas_call(
        up_kernel,
        grid=(4,),
        in_specs=[whole_block(pixels, width), *half_rows(block, width)],
        out_specs=[cols, cols, pl.BlockSpec((1, 8, block), lambda h: (h, 0, 0))],
        out_shape=[big, big, jax.ShapeDtypeStruct((4, 8, block), F32)],
        compiler_params=params("arbitrary"),
        cost_estimate=cost(9),
        name="up_project",
    )(normed, *w_up)


def mixed_kernel(weighted, w_mine, w_other, act_ref, sq, gm_ref, sums):
    def step(w):
        nt = (((1,), (1,)), ((), ()))
        gm = lax.dot_general(weighted[...], w[...], nt, preferred_element_type=F32)
        gm_ref[0] = gm
        act = act_ref[0]
        sums[0, 0:1, :] = jnp.sum(sq[0], axis=0, keepdims=True)
        sums[0, 1:2, :] = jnp.sum(gm * act, axis=0, keepdims=True)
        sums[0, 2:3, :] = jnp.sum(gm, axis=0, keepdims=True)
        sums[0, 3:4, :] = jnp.zeros((1, act.shape[1]), F32)

    with_rows(pl.program_id(0), w_mine, w_other, step)


def mixed_grad(weighted, w_down, act, sq):
    pixels, width = weighted.shape
    block = w_down[0].shape[0] // 2
    cols = pl.BlockSpec((1, pixels, block), lambda h: (h, 0, 0))
    return pl.pallas_call(
        mixed_kernel,
        grid=(4,),
        in_specs=[
            whole_block(pixels, width),
            *half_rows(block, width),
            cols,
            pl.BlockSpec((1, 8, block), lambda h: (h, 0, 0)),
        ],
        out_specs=[cols, pl.BlockSpec((1, 4, block), lambda h: (h, 0, 0))],
        out_shape=[jax.ShapeDtypeStruct((4, pixels, block), F32), jax.ShapeDtypeStruct((4, 4, block), F32)],
        compiler_params=params("arbitrary"),
        cost_estimate=cost(8),
        name="mixed_grad",
    )(weighted, *w_down, act, sq)


def ratio_of(sq, dot, gamma):
    energy = jnp.sqrt(sq)
    hid = energy.shape[0] * energy.shape[1]
    total = lambda x: jnp.sum(jnp.sum(x, axis=1, keepdims=True), axis=0, keepdims=True)
    mean = total(energy) / hid + EPS_NORM
    grad_ratio = gamma * dot
    shared = total(grad_ratio * energy) / (mean * mean) / hid
    return energy / mean, (grad_ratio / mean - shared) / energy


def outer(left, right):
    return lax.dot_general(left, right, (((0,), (0,)), ((), ())), preferred_element_type=F32).astype(BF16)


def mixed_of(a, gamma, ratio, beta):
    return (gamma * a * ratio + beta + a).astype(BF16)


def down_other_kernel(act, weighted, sums, local, gamma, beta, other, ratio, twice, parts):
    h = pl.program_id(0)

    @pl.when(h == 0)
    def _():
        crop = jnp.sum(sums[...], axis=0)
        sq = jnp.concatenate([crop[n, 0:1] for n in range(4)], axis=0)
        dot = jnp.concatenate([crop[n, 1:2] for n in range(4)], axis=0)
        r, t = ratio_of(sq, dot, gamma[...])
        ratio[...] = r
        twice[...] = t
        for n in range(4):
            parts[0, n : n + 1, :] = local[n, 1:2] * r[n : n + 1]
            parts[1, n : n + 1, :] = local[n, 2:3]

    row = pl.ds(h + 2, 1)
    other[...] = outer(mixed_of(act[0], gamma[row, :], ratio[row, :], beta[row, :]), weighted[...])


def down_other(act, weighted, sums, local, gamma, beta):
    _, pixels, block = act.shape
    width = weighted.shape[1]
    vec = jax.ShapeDtypeStruct((4, block), F32)
    return pl.pallas_call(
        down_other_kernel,
        grid=(2,),
        in_specs=[
            pl.BlockSpec((1, pixels, block), lambda h: (h + 2, 0, 0)),
            whole_block(pixels, width),
            whole_block(*sums.shape),
            whole_block(*local.shape),
            whole_block(4, block),
            whole_block(4, block),
        ],
        out_specs=[
            pl.BlockSpec((block, width), lambda h: (h, 0)),
            whole_block(4, block),
            whole_block(4, block),
            whole_block(2, 4, block),
        ],
        out_shape=[
            jax.ShapeDtypeStruct((2 * block, width), BF16),
            vec,
            vec,
            jax.ShapeDtypeStruct((2, 4, block), F32),
        ],
        compiler_params=params("arbitrary"),
        cost_estimate=cost(4),
        name="down_other",
    )(act, weighted, sums, local, gamma, beta)


def down_mine_kernel(act, weighted, ratio, gamma, beta, mine):
    row = pl.ds(pl.program_id(0), 1)
    mine[...] = outer(mixed_of(act[0], gamma[row, :], ratio[row, :], beta[row, :]), weighted[...])


def down_mine(act, weighted, ratio, gamma, beta):
    _, pixels, block = act.shape
    width = weighted.shape[1]
    return pl.pallas_call(
        down_mine_kernel,
        grid=(2,),
        in_specs=[
            pl.BlockSpec((1, pixels, block), lambda h: (h, 0, 0)),
            whole_block(pixels, width),
            whole_block(4, block),
            whole_block(4, block),
            whole_block(4, block),
        ],
        out_specs=pl.BlockSpec((block, width), lambda h: (h, 0)),
        out_shape=jax.ShapeDtypeStruct((2 * block, width), BF16),
        compiler_params=params("arbitrary"),
        cost_estimate=cost(4),
        name="down_mine",
    )(act, weighted, ratio, gamma, beta)


def hidden_kernel(
    act, slope, gm, w_mine, w_other, normed, ratio, twice, gamma, gain, xhat, rstd,
    mine, other, grad_conv, first, last, gain_part, total,
):
    h = pl.program_id(0)
    row = pl.ds(h, 1)
    grad_act = gm[0] * (gamma[row, :] * ratio[row, :] + 1.0) + act[0] * twice[row, :]
    grad_hidden = (grad_act * slope[0]).astype(BF16)
    term = outer(grad_hidden, normed[...])

    @pl.when(h == 0)
    def _():
        total[...] = jnp.dot(grad_hidden, w_mine[...], preferred_element_type=F32)
        mine[...] = term

    @pl.when(h == 1)
    def _():
        total[...] += jnp.dot(grad_hidden, w_mine[...], preferred_element_type=F32)
        mine[...] = term

    @pl.when(h >= 2)
    def _():
        total[...] += jnp.dot(grad_hidden, w_other[...], preferred_element_type=F32)
        other[...] = term

    @pl.when(h == 3)
    def _():
        pixels, width = total.shape
        block = 64

        def one(t, carry):
            at = pl.ds(pl.multiple_of(t * block, block), block)
            g = total[at, :]
            hat = xhat[at, :]
            carry = carry + jnp.sum((g * hat).reshape(block // 8, 8, width), axis=0)
            g = g * gain[...]
            mean_g = jnp.sum(g, axis=-1, keepdims=True) / width
            mean_gh = jnp.sum(g * hat, axis=-1, keepdims=True) / width
            out = rstd[at, 0:1] * (g - mean_g - hat * mean_gh)
            grad_conv[at, :] = out

            @pl.when(t * block < first.shape[0])
            def _():
                first[at, :] = out.astype(BF16)

            @pl.when(t * block >= pixels - last.shape[0])
            def _():
                last[pl.ds(pl.multiple_of(t * block - (pixels - last.shape[0]), block), block), :] = out.astype(BF16)

            return carry

        gain_part[...] = lax.fori_loop(0, pixels // block, one, jnp.zeros((8, width), F32))


def hidden_grad(act, slope, gm, w_up, normed, ratio, twice, gamma, gain, xhat, rstd, edge):
    _, pixels, block = act.shape
    width = normed.shape[1]
    cols = pl.BlockSpec((1, pixels, block), lambda h: (h, 0, 0))
    vec = whole_block(4, block)
    mine, other = half_rows(block, width)
    term = jax.ShapeDtypeStruct((2 * block, width), BF16)
    return pl.pallas_call(
        hidden_kernel,
        grid=(4,),
        in_specs=[
            cols, cols, cols, mine, other, whole_block(pixels, width), vec, vec, vec,
            whole_block(1, width), whole_block(pixels, width), whole_block(pixels, LANES),
        ],
        out_specs=[
            mine, other, whole_block(pixels, width), whole_block(edge, width), whole_block(edge, width),
            whole_block(8, width),
        ],
        out_shape=[
            term,
            term,
            jax.ShapeDtypeStruct((pixels, width), F32),
            jax.ShapeDtypeStruct((edge, width), BF16),
            jax.ShapeDtypeStruct((edge, width), BF16),
            jax.ShapeDtypeStruct((8, width), F32),
        ],
        scratch_shapes=[pltpu.VMEM((pixels, width), F32)],
        compiler_params=params("arbitrary"),
        cost_estimate=cost(14),
        name="hidden_grad",
    )(act, slope, gm, *w_up, normed, ratio, twice, gamma, gain.reshape(1, width), xhat, rstd)


def taps_grad_kernel(feat, above, below, grad, k_ref, ktaps, part, xs, gs, taps):
    cols = feat.shape[1]

    def chunk(n, lanes):
        fill_padded(xs, above, 0, lanes)
        fill_padded(xs, feat, 3, lanes)
        fill_padded(xs, below, 7, lanes)
        fill_padded(gs, grad, 0, lanes)
        spread_taps(taps, k_ref, True, lanes)
        for start in range(0, cols, GROUP * TILE):
            acc = [[jnp.zeros((TILE, LANES), F32) for _ in range(GROUP)] for _ in range(4)]
            acc = taps_group(gs, taps, own_pairs(), start, acc)
            for o in range(4):
                for b in range(GROUP):
                    part[o, tile_rows(start, b), lanes] = acc[o][b]
        for j in range(7):
            sums = [jnp.zeros((TILE, LANES), F32) for _ in range(7)]
            for start in range(0, cols, TILE):
                g = [gs[o, PAD + start : PAD + start + TILE, :] for o in range(4)]
                for r in range(10):
                    x = xs[r, PAD - 3 + j + start : PAD - 3 + j + start + TILE, :]
                    for o in range(4):
                        if 0 <= r - o <= 6:
                            sums[r - o] = sums[r - o] + x * g[o]
            for i in range(7):
                ktaps[i, j : j + 1, lanes] = jnp.sum(sums[i], axis=0, keepdims=True)

    each_chunk(chunk)


def taps_grad(feat, above, below, grad, kernel):
    rows, cols, width = feat.shape
    return pl.pallas_call(
        taps_grad_kernel,
        grid=(pl.cdiv(width, CHUNKS * LANES),),
        in_specs=[
            lane_blocks(rows, cols),
            lane_blocks(3, cols),
            lane_blocks(3, cols),
            lane_blocks(rows, cols),
            lane_blocks(7, 7),
        ],
        out_specs=[lane_blocks(7, 7), lane_blocks(rows, cols)],
        out_shape=[jax.ShapeDtypeStruct((7, 7, width), F32), jax.ShapeDtypeStruct((rows, cols, width), F32)],
        scratch_shapes=[
            pltpu.VMEM((rows + 6, cols + 2 * PAD, LANES), F32),
            pltpu.VMEM((rows, cols + 2 * PAD, LANES), F32),
            pltpu.VMEM((49, TILE, LANES), F32),
        ],
        compiler_params=params("arbitrary"),
        cost_estimate=cost(9),
        name="taps_grad",
    )(feat, above, below, grad, kernel)


def conv_back_kernel(part, above, below, k_ref, upstream, weight, out, xs, taps):
    cols = part.shape[1]

    def chunk(n, lanes):
        fill_padded(xs, above, 0, lanes)
        fill_padded(xs, below, 3, lanes)
        spread_taps(taps, k_ref, True, lanes)
        for start in range(0, cols, GROUP * TILE):
            acc = [[None] * GROUP for _ in range(4)]
            for o in range(4):
                for b in range(GROUP):
                    at = tile_rows(start, b)
                    acc[o][b] = part[o, at, lanes] + upstream[o, at, lanes].astype(F32) * weight[o, at, :]
            acc = taps_group(xs, taps, halo_pairs(), start, acc)
            for o in range(4):
                for b in range(GROUP):
                    out[o, tile_rows(start, b), lanes] = acc[o][b]

    each_chunk(chunk)


def conv_back(part, above, below, kernel, upstream, weight):
    rows, cols, width = part.shape
    return pl.pallas_call(
        conv_back_kernel,
        grid=(pl.cdiv(width, CHUNKS * LANES),),
        in_specs=[
            lane_blocks(rows, cols),
            lane_blocks(3, cols),
            lane_blocks(3, cols),
            lane_blocks(7, 7),
            lane_blocks(rows, cols),
            whole_block(rows, cols, LANES),
        ],
        out_specs=lane_blocks(rows, cols),
        out_shape=jax.ShapeDtypeStruct((rows, cols, width), F32),
        scratch_shapes=[
            pltpu.VMEM((6, cols + 2 * PAD, LANES), F32),
            pltpu.VMEM((49, TILE, LANES), F32),
        ],
        compiler_params=params("arbitrary"),
        cost_estimate=cost(5),
        name="conv_back",
    )(part, above, below, kernel, upstream, weight)


def chip_kernel(mine, other, vector, out):
    for q in range(mine.shape[0]):
        high = (mine[q, :128, :].astype(F32) + other[q, :128, :].astype(F32)).astype(BF16)
        low = mine[q, 128:, :].astype(F32) + other[q, 128:, :].astype(F32)
        for s in range(8):
            out[q * 8 + s, :16, :] = high[16 * s : 16 * (s + 1), :]
            rest = low[6 * s : 6 * (s + 1), :]
            if vector is not None:
                rest = jnp.concatenate([rest, vector[s]], axis=0)
            out[q * 8 + s, 16:, :] = rest.astype(BF16)


def chip_sum(mine, other, vector=None):
    owners, owned, width = mine.shape
    piece = owned // 8 + (0 if vector is None else vector.shape[1])
    rows = pl.BlockSpec((owners // 2, owned, width), lambda q: (q, 0, 0))
    given = [] if vector is None else [vector]
    kernel = chip_kernel if given else lambda mine, other, out: chip_kernel(mine, other, None, out)
    return pl.pallas_call(
        kernel,
        grid=(2,),
        in_specs=[rows, rows] + [whole_block(*v.shape) for v in given],
        out_specs=pl.BlockSpec((owners * 4, piece, width), lambda q: (q, 0, 0)),
        out_shape=jax.ShapeDtypeStruct((owners * 8, piece, width), BF16),
        compiler_params=params("arbitrary"),
        cost_estimate=cost(3),
        name="chip_sum",
    )(mine, other, *given)


BOTH = ("dp", "space")


def device(y, z, c, x, low):
    return (y * 8 + z * 2 + c) * 8 + x * 2 + low


OWNERS = [
    [device(y, z, c, x, low ^ y) for y in range(2) for z in range(4)]
    for c in range(2)
    for x in range(4)
    for low in range(2)
]
CORES = [
    [device(y, z, c, x, low) for y in range(2) for z in range(4) for x in range(4) for low in range(2)]
    for c in range(2)
]

SWAP = [
    (device(y, z, c, x, low), device(y, z, 1 - c, x, low))
    for y in range(2)
    for z in range(4)
    for c in range(2)
    for x in range(4)
    for low in range(2)
]


def to_other_core(value):
    return lax.ppermute(value, BOTH, SWAP)


def gather_mine(shard):
    return lax.all_to_all(jnp.broadcast_to(shard, (8,) + shard.shape), BOTH, 0, 0, axis_index_groups=OWNERS)


def with_other(mine):
    other = to_other_core(mine)
    return mine.reshape(-1, mine.shape[2]), other.reshape(-1, mine.shape[2])


def local_order(vector, owned):
    first, second = core_halves(vector.reshape(8, 2, owned), 1)
    return jnp.concatenate([first.reshape(2, -1), second.reshape(2, -1)], axis=0)


def core_halves(value, axis):
    c = lax.axis_index("dp") % 2
    low, high = lax.index_in_dim(value, 0, axis, False), lax.index_in_dim(value, 1, axis, False)
    return jnp.where(c == 0, low, high), jnp.where(c == 0, high, low)


def global_order(blocks, owned):
    n = blocks.shape[0]
    low, high = core_halves(blocks.reshape(n, 2, 8, owned), 1)
    return jnp.stack([low, high], axis=2).reshape(n, -1)


def sum_blocks(blocks):
    return jnp.sum(lax.all_to_all(blocks, BOTH, 0, 0, axis_index_groups=CORES).astype(F32), axis=0)


def exchange(value, axis):
    return lax.all_to_all(value, axis, 0, 0)


def everyone(value, axis):
    return exchange(jnp.broadcast_to(value, (lax.axis_size(axis),) + value.shape), axis)


def shift(rows, pairs):
    flat = rows.reshape(-1, 16, rows.shape[-1])
    return lax.ppermute(flat, "space", pairs).reshape(rows.shape)


def body(
    features, kernel, norm_gain, w_up, grn_gamma, grn_beta, w_down, upstream, labels, class_weight
):
    crops, rows, cols, width = features.shape
    feat, up = features[0], upstream[0]
    space = lax.axis_size("space")
    dp = lax.axis_size("dp")
    owned = w_up.shape[0]
    hid = owned * dp
    pixels = rows * cols
    rising = [(i, i + 1) for i in range(space - 1)]
    falling = [(j, i) for i, j in rising]
    above = shift(feat[rows - 3 :], rising)
    below = shift(feat[:3], falling)
    part = conv_own(feat, kernel)
    mine = gather_mine(jnp.concatenate([w_up, w_down], axis=0))
    w_up_mine, w_down_mine = mine[:, :owned], mine[:, owned:]
    gamma, beta = local_order(grn_gamma, owned), local_order(grn_beta, owned)

    classes = jnp.arange(class_weight.shape[0], dtype=jnp.int32)
    pixel_weight = jnp.sum(jnp.where(labels[0][..., None] == classes, class_weight, 0.0), axis=-1)
    weight = jnp.broadcast_to(pixel_weight[..., None], (rows, cols, LANES))
    weighted = (up.astype(F32) * pixel_weight[..., None]).astype(BF16).reshape(pixels, width)

    normed, xhat, rstd = conv_norm(part, above, below, kernel, norm_gain)
    w_up_mine, w_down_mine, rstd = lax.optimization_barrier((w_up_mine, w_down_mine, rstd))
    w_up_all = with_other(w_up_mine)
    act, slope, sq = up_project(normed, w_up_all)
    w_down_mine, sq = lax.optimization_barrier((w_down_mine, sq))
    w_down_all = with_other(w_down_mine)
    gm, local = mixed_grad(weighted, w_down_all, act, sq)
    sums = everyone(local, "space")
    down_other_term, ratio, twice, parts = down_other(act, weighted, sums, local, gamma, beta)
    by_owner = lambda rows: rows.reshape(8, owned, width)
    came = to_other_core(by_owner(down_other_term))
    down_blocks = chip_sum(by_owner(down_mine(act, weighted, ratio, gamma, beta)), came)
    ratio, down_blocks = lax.optimization_barrier((ratio, down_blocks))
    down_rows = sum_blocks(down_blocks)
    up_mine, up_other, grad_conv, g_first, g_last, gain_part = hidden_grad(
        act, slope, gm, w_up_all, normed, ratio, twice, gamma, norm_gain, xhat, rstd, 3 * cols
    )
    grad_conv = grad_conv.reshape(rows, cols, width)
    g_above = shift(g_last.reshape(3, cols, width), rising)
    g_below = shift(g_first.reshape(3, cols, width), falling)
    kernel_part, back = taps_grad(feat, above, below, grad_conv, kernel)

    scale = 1.0 / math.sqrt(dp * space * pixels)
    vector = jnp.concatenate(
        [
            kernel_part.reshape(49, width),
            jnp.sum(gain_part, axis=0, keepdims=True),
            global_order(parts, owned).reshape(-1, width),
        ],
        axis=0,
    )
    lines = vector.shape[0]
    vector = jnp.pad(vector, ((0, -lines % 64), (0, 0)))
    vector, g_above, g_below = lax.optimization_barrier((vector, g_above, g_below))
    vector = (vector + to_other_core(vector)).reshape(8, 8, width)
    up_blocks = chip_sum(by_owner(up_mine), to_other_core(by_owner(up_other)), vector)
    up_blocks, down_rows = lax.optimization_barrier((up_blocks, down_rows))
    up_rows = sum_blocks(up_blocks)
    grad_features = conv_back(back, g_above, g_below, kernel, up, weight)
    up_rows, grad_features = lax.optimization_barrier((up_rows, grad_features))

    piece = owned // space
    block = jnp.concatenate([up_rows[:piece], down_rows], axis=1)
    block = jnp.concatenate([block, up_rows[piece:].reshape(4, 2 * width)], axis=0)
    block = everyone((scale * block).astype(BF16), "space").astype(F32)
    vector = block[:, piece:].reshape(8 * space, width)
    kernel_sum = vector[:49].reshape(7, 7, width)
    gain_sum = vector[49]
    gamma_sum, beta_sum = vector[50:lines].reshape(2, hid)
    block = jnp.concatenate([block[:, :16].reshape(-1, 2 * width), block[:, 16:piece].reshape(-1, 2 * width)], axis=0)
    return (
        grad_features[None],
        kernel_sum,
        gain_sum,
        block[:, :width],
        gamma_sum,
        beta_sum,
        block[:, width:],
    )


def solution(mesh):
    return jax.shard_map(
        body,
        mesh=mesh,
        in_specs=(
            P("dp", "space", None, None),
            P(),
            P(),
            P("dp", None),
            P(),
            P(),
            P("dp", None),
            P("dp", "space", None, None),
            P("dp", "space", None),
            P(),
        ),
        out_specs=(P("dp", "space", None, None), P(), P(), P("dp", None), P(), P(), P("dp", None)),
        check_vma=False,
    )
```

time: 539 us -> 264 us (0.49)
  blocking collectives: 223 us -> 0 us
  waiting for transfers between devices: 182 us -> 109 us
  starting transfers between devices: 7.64 us -> 43.4 us
  between operations: 13.9 us -> 0.99 us
  other arithmetic: 14.4 us -> 6.62 us
    psum x4 -> x0, blocking collectives: 223 us -> none  [the longest x1 73.5 us: body(): lax.psum((kernel_part, jnp.sum(gain_part, axis=0)), ('dp', 'space'))]
    all_gather x2 -> x0, waiting for transfers between devices: 84.2 us -> none  [the longest x1 56.3 us: body(): w_down_all = lax.all_gather(w_down, 'dp', axis=0, tiled=True)]
    reduce_scatter x1 -> x0, waiting for transfers between devices: 83.7 us -> none  [body(): lax.psum_scatter(jnp.concatenate([up_term, down_term], axis=1), 'dp', sca...]
    all_to_all x0 -> x5, waiting for transfers between devices: none -> 63.6 us  [the longest x2 33 us: sum_blocks(): lax.all_to_all(blocks, BOTH, 0, 0, axis_index_groups=CORES).astype(F32)]
    all_to_all x0 -> x5, starting transfers between devices: none -> 35 us  [the longest x2 18.2 us: sum_blocks(): lax.all_to_all(blocks, BOTH, 0, 0, axis_index_groups=CORES).astype(F32)]
    ppermute x4 -> x9, waiting for transfers between devices: 12.9 us -> 45.3 us  [the longest x4 36.9 us: shift(): return lax.ppermute(flat, 'space', pairs).reshape(rows.shape)]
    concatenate x1 -> x5, other arithmetic: 9.18 us -> 3.46 us  [the longest x2 1.22 us: local_order(): jnp.concatenate([first.reshape(2, -1), second.reshape(2, -1)], axis=0)]
    pallas_call x7 -> x11, Pallas kernels: 76 us -> 78.9 us  [the longest x1 16.4 us: hidden_grad(): pl.pallas_call(hidden_kernel, grid=(4,), in_specs=[cols, cols, cols, mine...]
  transfers between devices with their start and end apart: 8 -> 14, of which waited for: 4 -> 10; matrix products, arithmetic and copies ran while one was open for 6% -> 4% of each run, Pallas kernels for 4% -> 19%
where the time goes in v3:
time: 264 us; the launch traced here: 263 us
  waiting for transfers between devices  109 us (41%)
  Pallas kernels  78.9 us (30%)
  starting transfers between devices  43.4 us (16%)
  local copies, waits for them, and re-layouts  24.1 us (9%)
  other arithmetic  6.62 us (3%)
    ppermute x4, waiting for transfers between devices, shift(): return lax.ppermute(flat, 'space', pairs).reshape(rows.shape)  36.9 us
    all_to_all x2, waiting for transfers between devices, sum_blocks(): lax.all_to_all(blocks, BOTH, 0, 0, axis_index_groups=CORES).astype(F32)  33 us
    all_to_all x2, starting transfers between devices, sum_blocks(): lax.all_to_all(blocks, BOTH, 0, 0, axis_index_groups=CORES).astype(F32)  18.2 us
    pallas_call x1, Pallas kernels, hidden_grad(): pl.pallas_call(hidden_kernel, grid=(4,), in_specs=[cols, cols, cols, mine...  16.4 us
    all_to_all x2, waiting for transfers between devices, exchange(): return lax.all_to_all(value, axis, 0, 0)  15.9 us
    all_to_all x1, waiting for transfers between devices, gather_mine(): lax.all_to_all(jnp.broadcast_to(shard, (8,) + shard.shape), BOTH, 0, 0, a...  14.7 us
    pallas_call x1, Pallas kernels, taps_grad(): pl.pallas_call(taps_grad_kernel, grid=(pl.cdiv(width, CHUNKS * LANES),),...  10.9 us
    pallas_call x1, Pallas kernels, up_project(): pl.pallas_call(up_kernel, grid=(4,), in_specs=[whole_block(pixels, width)...  9.63 us
  transfers between devices with their start and end apart: 14, of which 10 were waited for; matrix products, arithmetic and copies ran while one was open for 4% of the time, Pallas kernels for 19%

profile of v3, /device:TPU:0, one launch (start us, length us, event | category | flops | bytes accessed | tf_op | source)
XLA Modules:
  0.0 263.0 jit_solution(2031261916499668853)
XLA Ops:
  1.7 2.3 broadcast_in_dim.31
  4.1 8.0 %all-to-all-start = ((bf16[8,352,704]{2,1,0:T(8,128)(2,1)}), bf16[8,352,704]{2,1,0:T(8,128)(2,1)}, u32[]{:S(2)}, u32[]{:S(2)}) async-start(bf16[8,352,704]{2,1,0:T(8,128)(2,1)} %broadcast_in_dim.31), calls=%async_computation | async-start | bytes 8650752 | tf_op jit(solution)/shard_map/all_to_all | solution.py:624
  12.5 2.1 collective-permute-start
  16.4 4.9 %conv_own.1.part = f32[4,128,704]{2,1,0:T(8,128)} custom-call(bf16[4,128,704]{2,1,0:T(8,128)(2,1)} %bitcast.46, f32[7,7,704]{2,1,0:T(8,128)} %k_ref.7), custom_call_target="tpu_custom_call" | custom-call | flops 2000000000 | tf_op jit(solution)/shard_map/conv_own/pallas_call | solution.py:107
  21.4 18.1 %collective-permute-done = bf16[24,16,704]{2,1,0:T(8,128)(2,1)S(1)} collective-permute-done((bf16[24,16,704]{2,1,0:T(8,128)(2,1)S(1)}, bf16[24,16,704]{2,1,0:T(8,128)(2,1)S(1)}, u32[]{:S(2)}, u32[]{:S(2)}) %collective-permute-start) | collective-permute-done | bytes 540704 | tf_op jit(solution)/shard_map/ppermute | solution.py:663
  40.5 7.0 %conv_norm.1 = (bf16[512,704]{1,0:T(8,128)(2,1)}, f32[512,704]{1,0:T(8,128)}, f32[512,128]{1,0:T(8,128)}) custom-call(f32[4,128,704]{2,1,0:T(8,128)} %conv_own.1.part, bf16[3,128,704]{2,1,0:T(8,128)(2,1)} %bitcast.62, bf16[3,128,704]{2,1,0:T(8,128)(2,1)} %bitcast.64, f32[7,7,704]{2,1,0:T(8,128)} %k_ref.7, f32[1,704]{1,0:T(1,128)} %reshape.172.gain), custom_call_target="tpu_custom_call" | custom-call | flops 2800000000 | tf_op jit(solution)/shard_map/conv_norm/pallas_call | solution.py:174
  47.5 14.7 %all-to-all-done = bf16[8,352,704]{2,1,0:T(8,128)(2,1)} async-done(((bf16[8,352,704]{2,1,0:T(8,128)(2,1)}), bf16[8,352,704]{2,1,0:T(8,128)(2,1)}, u32[]{:S(2)}, u32[]{:S(2)}) %all-to-all-start) | async-done | bytes 3964960 | tf_op jit(solution)/shard_map/all_to_all | solution.py:624
  62.2 3.9 %fusion.10 = (bf16[8,176,704]{2,1,0:T(8,128)(2,1)}, bf16[8,176,704]{2,1,0:T(8,128)(2,1)S(1)}) fusion(bf16[8,352,704]{2,1,0:T(8,128)(2,1)} %all-to-all-done), kind=kLoop, calls=%fused_computation.34 | loop fusion | bytes 7929856 | tf_op jit(solution)/shard_map/slice | solution.py:682
  66.0 4.3 %collective-permute-done.2 = bf16[8,176,704]{2,1,0:T(8,128)(2,1)S(1)} collective-permute-done((bf16[8,176,704]{2,1,0:T(8,128)(2,1)S(1)}, bf16[8,176,704]{2,1,0:T(8,128)(2,1)S(1)}, u32[]{:S(2)}, u32[]{:S(2)}) %collective-permute-start.2) | collective-permute-done | bytes 1982496 | tf_op jit(solution)/shard_map/ppermute | solution.py:620
  71.7 9.6 %up_project.1 = (f32[4,512,704]{2,1,0:T(8,128)}, f32[4,512,704]{2,1,0:T(8,128)}, f32[4,8,704]{2,1,0:T(8,128)}) custom-call(bf16[512,704]{1,0:T(8,128)(2,1)} %get-tuple-element.41.normed, bf16[1408,704]{1,0:T(8,128)(2,1)} %bitcast.43, bf16[1408,704]{1,0:T(8,128)(2,1)} %bitcast.49), custom_call_target="tpu_custom_call" | custom-call | flops 3600000000 | tf_op jit(solution)/shard_map/up_project/pallas_call | solution.py:230
  83.6 2.5 collective-permute-done.3
  86.0 8.5 %mixed_grad.1 = (f32[4,512,704]{2,1,0:T(8,128)}, f32[4,4,704]{2,1,0:T(4,128)}) custom-call(bf16[512,704]{1,0:T(8,128)(2,1)} %fusion.weighted, bf16[1408,704]{1,0:T(8,128)(2,1)} %bitcast.52, bf16[1408,704]{1,0:T(8,128)(2,1)} %bitcast.11.w_other, f32[4,512,704]{2,1,0:T(8,128)} %get-tuple-element.44.act_ref.act, f32[4,8,704]{2,1,0:T(8,128)} %get-tuple-element.49.sq), custom_call_target="tpu_custom_call" | custom-call | flops 3200000000 | tf_op jit(solution)/shard_map/mixed_grad/pallas_call | solution.py:260
  94.6 1.6 broadcast_in_dim.34
  96.2 4.3 %all-to-all-start.1 = ((f32[8,4,4,704]{3,2,1,0:T(4,128)}), f32[8,4,4,704]{3,2,1,0:T(4,128)S(1)}, u32[]{:S(2)}, u32[]{:S(2)}) async-start(f32[8,4,4,704]{3,2,1,0:T(4,128)} %broadcast_in_dim.34), calls=%async_computation.1 | async-start | bytes 786432 | tf_op jit(solution)/shard_map/all_to_all | solution.py:654
  102.2 6.8 %all-to-all-done.1.sums = f32[8,4,4,704]{3,2,1,0:T(4,128)S(1)} async-done(((f32[8,4,4,704]{3,2,1,0:T(4,128)}), f32[8,4,4,704]{3,2,1,0:T(4,128)S(1)}, u32[]{:S(2)}, u32[]{:S(2)}) %all-to-all-start.1) | async-done | bytes 360480 | tf_op jit(solution)/shard_map/all_to_all | solution.py:654
  109.7 4.6 %down_other.1 = (bf16[1408,704]{1,0:T(8,128)(2,1)}, f32[4,704]{1,0:T(4,128)}, f32[4,704]{1,0:T(4,128)}, f32[2,4,704]{2,1,0:T(4,128)}) custom-call(f32[4,512,704]{2,1,0:T(8,128)} %get-tuple-element.44.act_ref.act, bf16[512,704]{1,0:T(8,128)(2,1)} %fusion.weighted, f32[8,4,4,704]{3,2,1,0:T(4,128)} %copy-done.5, f32[4,4,704]{2,1,0:T(4,128)} %get-tuple-element.51.local, ...), custom_call_target="tpu_custom_call" | custom-call | flops 1600000000 | tf_op jit(solution)/shard_map/down_other/pallas_call | solution.py:318
  114.3 4.3 %down_mine.1 = bf16[1408,704]{1,0:T(8,128)(2,1)} custom-call(f32[4,512,704]{2,1,0:T(8,128)} %get-tuple-element.44.act_ref.act, bf16[512,704]{1,0:T(8,128)(2,1)} %fusion.weighted, f32[4,704]{1,0:T(4,128)} %get-tuple-element.54.ratio, f32[4,704]{1,0:T(4,128)} %pad_maximum_fusion.4.gamma, f32[4,704]{1,0:T(4,128)} %pad_maximum_fusion.5.beta), custom_call_target="tpu_custom_call" | custom-call | flops 1600000000 | tf_op jit(solution)/shard_map/down_mine/pallas_call | solution.py:355
  118.8 1.4 copy-done.4
  120.2 3.5 %chip_sum.2 = bf16[64,22,704]{2,1,0:T(8,128)(2,1)} custom-call(bf16[8,176,704]{2,1,0:T(8,128)(2,1)} %bitcast.45, bf16[8,176,704]{2,1,0:T(8,128)(2,1)} %copy-done.4), custom_call_target="tpu_custom_call" | custom-call | flops 1200000000 | tf_op jit(solution)/shard_map/chip_sum/pallas_call | solution.py:579
  123.8 7.8 %all-to-all-start.2 = ((bf16[64,22,704]{2,1,0:T(8,128)(2,1)}), bf16[64,22,704]{2,1,0:T(8,128)(2,1)S(1)}, u32[]{:S(2)}, u32[]{:S(2)}) async-start(bf16[64,22,704]{2,1,0:T(8,128)(2,1)} %chip_sum.2), calls=%async_computation.2 | async-start | bytes 4718592 | tf_op jit(solution)/shard_map/all_to_all | solution.py:650
  131.5 16.4 %hidden_grad.1 = (bf16[1408,704]{1,0:T(8,128)(2,1)}, bf16[1408,704]{1,0:T(8,128)(2,1)}, f32[512,704]{1,0:T(8,128)}, bf16[384,704]{1,0:T(8,128)(2,1)}, bf16[384,704]{1,0:T(8,128)(2,1)}, /*index=5*/f32[8,704]{1,0:T(8,128)}) custom-call(f32[4,512,704]{2,1,0:T(8,128)} %get-tuple-element.44.act_ref.act, f32[4,512,704]{2,1,0:T(8,128)} %get-tuple-element.45.slope, ...), custom_call_target="tpu_custom_call" | custom-call | flops 5600000000 | tf_op jit(solution)/shard_map/hidden_grad/pallas_call | solution.py:434
  148.2 3.3 %collective-permute-start.6 = (bf16[24,16,704]{2,1,0:T(8,128)(2,1)}, bf16[24,16,704]{2,1,0:T(8,128)(2,1)S(1)}, u32[]{:S(2)}, u32[]{:S(2)}) collective-permute-start(bf16[24,16,704]{2,1,0:T(8,128)(2,1)} %bitcast.68), channel_id=1, source_target_pairs={{0,1},{1,2},{2,3},{3,4},{4,5},{5,6},{6,7},{8,9},{9,10},{10,11},{11... | collective-permute-start | bytes 1622024 | tf_op jit(solution)/shard_map/ppermute | solution.py:663
  153.0 10.9 %taps_grad.1 = (f32[7,7,704]{2,1,0:T(8,128)}, f32[4,128,704]{2,1,0:T(8,128)}) custom-call(bf16[4,128,704]{2,1,0:T(8,128)(2,1)} %bitcast.47, bf16[3,128,704]{2,1,0:T(8,128)(2,1)} %bitcast.63, bf16[3,128,704]{2,1,0:T(8,128)(2,1)} %bitcast.65, f32[4,128,704]{2,1,0:T(8,128)} %bitcast.61, f32[7,7,704]{2,1,0:T(8,128)} %k_ref.7), custom_call_target="tpu_custom_call" | custom-call | flops 3600000000 | tf_op jit(solution)/shard_map/taps_grad/pallas_call | solution.py:492
  164.9 18.9 %collective-permute-done.6 = bf16[24,16,704]{2,1,0:T(8,128)(2,1)S(1)} collective-permute-done((bf16[24,16,704]{2,1,0:T(8,128)(2,1)}, bf16[24,16,704]{2,1,0:T(8,128)(2,1)S(1)}, u32[]{:S(2)}, u32[]{:S(2)}) %collective-permute-start.6) | collective-permute-done | bytes 540704 | tf_op jit(solution)/shard_map/ppermute | solution.py:663
  186.4 3.8 %chip_sum.3 = bf16[64,30,704]{2,1,0:T(8,128)(2,1)} custom-call(bf16[8,176,704]{2,1,0:T(8,128)(2,1)} %bitcast.51, bf16[8,176,704]{2,1,0:T(8,128)(2,1)} %collective-permute-done.5.other, f32[8,8,704]{2,1,0:T(8,128)} %add_bitcast_fusion.vector), custom_call_target="tpu_custom_call" | custom-call | flops 1200000000 | tf_op jit(solution)/shard_map/chip_sum/pallas_call | solution.py:579
  190.2 10.5 %all-to-all-start.3 = ((bf16[64,30,704]{2,1,0:T(8,128)(2,1)}), bf16[64,30,704]{2,1,0:T(8,128)(2,1)S(1)}, u32[]{:S(2)}, u32[]{:S(2)}) async-start(bf16[64,30,704]{2,1,0:T(8,128)(2,1)} %chip_sum.3), calls=%async_computation.3 | async-start | bytes 6291456 | tf_op jit(solution)/shard_map/all_to_all | solution.py:650
  200.6 2.3 copy.46
  203.7 5.2 %conv_back.1 = f32[4,128,704]{2,1,0:T(8,128)} custom-call(f32[4,128,704]{2,1,0:T(8,128)} %get-tuple-element.69.part, bf16[3,128,704]{2,1,0:T(8,128)(2,1)} %bitcast.66, bf16[3,128,704]{2,1,0:T(8,128)(2,1)} %bitcast.25.below, f32[7,7,704]{2,1,0:T(8,128)} %k_ref.7, bf16[4,128,704]{2,1,0:T(8,128)(2,1)} %bitcast.54, f32[4,128,128]{2,1,0:T(8,128)} %broadcast_in_dim.36.weight), custom_call_target="tpu_custom_call" | custom-call | flops 2000000000 | tf_op jit(solution)/shard_map/conv_back/pallas_call | solution.py:538
  209.0 33.0 %all-to-all-done.3 = bf16[64,30,704]{2,1,0:T(8,128)(2,1)S(1)} async-done(((bf16[64,30,704]{2,1,0:T(8,128)(2,1)}), bf16[64,30,704]{2,1,0:T(8,128)(2,1)S(1)}, u32[]{:S(2)}, u32[]{:S(2)}) %all-to-all-start.3) | async-done | bytes 2703392 | tf_op jit(solution)/shard_map/all_to_all | solution.py:650
  243.7 4.5 %all-to-all-start.4 = ((bf16[8,26,1408]{2,1,0:T(8,128)(2,1)}), bf16[8,26,1408]{2,1,0:T(8,128)(2,1)S(1)}, u32[]{:S(2)}, u32[]{:S(2)}) async-start(bf16[8,26,1408]{2,1,0:T(8,128)(2,1)} %broadcast_in_dim.38), calls=%async_computation.4 | async-start | bytes 1441792 | tf_op jit(solution)/shard_map/all_to_all | solution.py:654
  248.2 1.6 copy.47
  249.7 9.1 %all-to-all-done.4 = bf16[8,26,1408]{2,1,0:T(8,128)(2,1)S(1)} async-done(((bf16[8,26,1408]{2,1,0:T(8,128)(2,1)}), bf16[8,26,1408]{2,1,0:T(8,128)(2,1)S(1)}, u32[]{:S(2)}, u32[]{:S(2)}) %all-to-all-start.4) | async-done | bytes 585760 | tf_op jit(solution)/shard_map/all_to_all | solution.py:654
  (95 shorter events, 22.3 us)
Async XLA Ops:
  4.1 8.0 %copy-start.7 = (bf16[1,4,128,704]{2,3,1,0:T(8,128)(2,1)S(1)}, bf16[1,4,128,704]{2,3,1,0:T(8,128)(2,1)}, u32[]{:S(2)}) copy-start(bf16[1,4,128,704]{2,3,1,0:T(8,128)(2,1)} %param.10) | copy-start | bytes 2162692
  4.1 58.1 %all-to-all-start = ((bf16[8,352,704]{2,1,0:T(8,128)(2,1)}), bf16[8,352,704]{2,1,0:T(8,128)(2,1)}, u32[]{:S(2)}, u32[]{:S(2)}) async-start(bf16[8,352,704]{2,1,0:T(8,128)(2,1)} %broadcast_in_dim.31), calls=%async_computation | async-start | bytes 8650752 | tf_op jit(solution)/shard_map/all_to_all | solution.py:624
  12.1 3.8 %copy-start.12 = (f32[704]{0:T(1024)S(1)}, f32[704]{0:T(1024)}, u32[]{:S(2)}) copy-start(f32[704]{0:T(1024)} %param.12) | copy-start | bytes 8452
  12.4 4.1 %copy-start.1 = (bf16[1,4,128,704]{3,2,1,0:T(8,128)(2,1)}, bf16[1,4,128,704]{3,2,1,0:T(8,128)(2,1)S(1)}, u32[]{:S(2)}) copy-start(bf16[1,4,128,704]{3,2,1,0:T(8,128)(2,1)S(1)} %copy.37) | copy-start | bytes 2162692
  12.5 27.0 %collective-permute-start = (bf16[24,16,704]{2,1,0:T(8,128)(2,1)S(1)}, bf16[24,16,704]{2,1,0:T(8,128)(2,1)S(1)}, u32[]{:S(2)}, u32[]{:S(2)}) collective-permute-start(bf16[24,16,704]{2,1,0:T(8,128)(2,1)S(1)} %bitcast.56), channel_id=1, source_target_pairs={{0,1},{1,2},{2,3},{3,4},{4,5},{5,6},{6,7},{8,9},{9,10},{10,11},{11... | collective-permute-start | bytes 1622024 | tf_op jit(solution)/shard_map/ppermute | solution.py:663
  14.5 24.9 %collective-permute-start.1 = (bf16[24,16,704]{2,1,0:T(8,128)(2,1)S(1)}, bf16[24,16,704]{2,1,0:T(8,128)(2,1)S(1)}, u32[]{:S(2)}, u32[]{:S(2)}) collective-permute-start(bf16[24,16,704]{2,1,0:T(8,128)(2,1)S(1)} %bitcast.55), channel_id=1, source_target_pairs={{1,0},{2,1},{3,2},{4,3},{5,4},{6,5},{7,6},{9,8},{10,9},{11,10},{12... | collective-permute-start | bytes 1622024 | tf_op jit(solution)/shard_map/ppermute | solution.py:663
  39.4 0.8 copy-start.15
  39.4 1.0 copy-start.16
  66.0 4.3 %copy-start = (bf16[8,176,704]{2,1,0:T(8,128)(2,1)}, bf16[8,176,704]{2,1,0:T(8,128)(2,1)S(1)}, u32[]{:S(2)}) copy-start(bf16[8,176,704]{2,1,0:T(8,128)(2,1)S(1)} %get-tuple-element.43) | copy-start | bytes 5947396
  66.0 4.3 %collective-permute-start.2 = (bf16[8,176,704]{2,1,0:T(8,128)(2,1)S(1)}, bf16[8,176,704]{2,1,0:T(8,128)(2,1)S(1)}, u32[]{:S(2)}, u32[]{:S(2)}) collective-permute-start(bf16[8,176,704]{2,1,0:T(8,128)(2,1)S(1)} %get-tuple-element.43), channel_id=1, source_target_pairs={{0,8},{1,9},{2,10},{3,11},{4,12},{5,13},{6,14},{7,15},{8,0},{9,1},... | collective-permute-start | bytes 5947400 | tf_op jit(solution)/shard_map/ppermute | solution.py:620
  70.3 1.4 copy-start.3
  71.7 9.9 %copy-start.2 = (bf16[1,4,128,704]{2,3,1,0:T(8,128)(2,1)S(1)}, bf16[1,4,128,704]{2,3,1,0:T(8,128)(2,1)}, u32[]{:S(2)}) copy-start(bf16[1,4,128,704]{2,3,1,0:T(8,128)(2,1)} %param.17) | copy-start | bytes 2162692
  81.3 0.7 copy-start.10
  81.3 0.8 copy-start.11
  81.3 0.9 copy-start.13
  81.4 0.9 copy-start.14
  81.4 4.7 %collective-permute-start.3 = (bf16[8,176,704]{2,1,0:T(8,128)(2,1)}, bf16[8,176,704]{2,1,0:T(8,128)(2,1)}, u32[]{:S(2)}, u32[]{:S(2)}) collective-permute-start(bf16[8,176,704]{2,1,0:T(8,128)(2,1)} %get-tuple-element.48), channel_id=1, source_target_pairs={{0,8},{1,9},{2,10},{3,11},{4,12},{5,13},{6,14},{7,15},{8,0},{9,1},... | collective-permute-start | bytes 5947400 | tf_op jit(solution)/shard_map/ppermute | solution.py:620
  96.2 12.8 %all-to-all-start.1 = ((f32[8,4,4,704]{3,2,1,0:T(4,128)}), f32[8,4,4,704]{3,2,1,0:T(4,128)S(1)}, u32[]{:S(2)}, u32[]{:S(2)}) async-start(f32[8,4,4,704]{3,2,1,0:T(4,128)} %broadcast_in_dim.34), calls=%async_computation.1 | async-start | bytes 786432 | tf_op jit(solution)/shard_map/all_to_all | solution.py:654
  109.0 0.7 copy-start.5
  114.3 4.5 %collective-permute-start.4 = (bf16[8,176,704]{2,1,0:T(8,128)(2,1)}, bf16[8,176,704]{2,1,0:T(8,128)(2,1)S(1)}, u32[]{:S(2)}, u32[]{:S(2)}) collective-permute-start(bf16[8,176,704]{2,1,0:T(8,128)(2,1)} %bitcast.60), channel_id=1, source_target_pairs={{0,8},{1,9},{2,10},{3,11},{4,12},{5,13},{6,14},{7,15},{8,0},{9,1},... | collective-permute-start | bytes 5947400 | tf_op jit(solution)/shard_map/ppermute | solution.py:620
  118.8 1.4 copy-start.4
  123.8 62.2 %all-to-all-start.2 = ((bf16[64,22,704]{2,1,0:T(8,128)(2,1)}), bf16[64,22,704]{2,1,0:T(8,128)(2,1)S(1)}, u32[]{:S(2)}, u32[]{:S(2)}) async-start(bf16[64,22,704]{2,1,0:T(8,128)(2,1)} %chip_sum.2), calls=%async_computation.2 | async-start | bytes 4718592 | tf_op jit(solution)/shard_map/all_to_all | solution.py:650
  131.5 16.6 %copy-start.8 = (f32[2,4,704]{2,1,0:T(4,128)S(1)}, f32[2,4,704]{2,1,0:T(4,128)}, u32[]{:S(2)}) copy-start(f32[2,4,704]{2,1,0:T(4,128)} %get-tuple-element.63) | copy-start | bytes 67588
  148.0 38.4 %collective-permute-start.5 = (bf16[8,176,704]{2,1,0:T(8,128)(2,1)}, bf16[8,176,704]{2,1,0:T(8,128)(2,1)}, u32[]{:S(2)}, u32[]{:S(2)}) collective-permute-start(bf16[8,176,704]{2,1,0:T(8,128)(2,1)} %bitcast.59), channel_id=1, source_target_pairs={{0,8},{1,9},{2,10},{3,11},{4,12},{5,13},{6,14},{7,15},{8,0},{9,1},... | collective-permute-start | bytes 5947400 | tf_op jit(solution)/shard_map/ppermute | solution.py:620
  148.2 35.6 %collective-permute-start.6 = (bf16[24,16,704]{2,1,0:T(8,128)(2,1)}, bf16[24,16,704]{2,1,0:T(8,128)(2,1)S(1)}, u32[]{:S(2)}, u32[]{:S(2)}) collective-permute-start(bf16[24,16,704]{2,1,0:T(8,128)(2,1)} %bitcast.68), channel_id=1, source_target_pairs={{0,1},{1,2},{2,3},{3,4},{4,5},{5,6},{6,7},{8,9},{9,10},{10,11},{11... | collective-permute-start | bytes 1622024 | tf_op jit(solution)/shard_map/ppermute | solution.py:663
  151.6 32.2 %collective-permute-start.7 = (bf16[24,16,704]{2,1,0:T(8,128)(2,1)}, bf16[24,16,704]{2,1,0:T(8,128)(2,1)}, u32[]{:S(2)}, u32[]{:S(2)}) collective-permute-start(bf16[24,16,704]{2,1,0:T(8,128)(2,1)} %bitcast.67), channel_id=1, source_target_pairs={{1,0},{2,1},{3,2},{4,3},{5,4},{6,5},{7,6},{9,8},{10,9},{11,10},{12... | collective-permute-start | bytes 1622024 | tf_op jit(solution)/shard_map/ppermute | solution.py:663
  153.0 11.9 %copy-start.9 = (f32[8,704]{1,0:T(8,128)S(1)}, f32[8,704]{1,0:T(8,128)}, u32[]{:S(2)}) copy-start(f32[8,704]{1,0:T(8,128)} %get-tuple-element.62) | copy-start | bytes 67588
  183.8 2.1 copy-start.17
  183.8 1.4 collective-permute-start.8
  190.2 51.8 %all-to-all-start.3 = ((bf16[64,30,704]{2,1,0:T(8,128)(2,1)}), bf16[64,30,704]{2,1,0:T(8,128)(2,1)S(1)}, u32[]{:S(2)}, u32[]{:S(2)}) async-start(bf16[64,30,704]{2,1,0:T(8,128)(2,1)} %chip_sum.3), calls=%async_computation.3 | async-start | bytes 6291456 | tf_op jit(solution)/shard_map/all_to_all | solution.py:650
  242.5 5.6 %copy-start.6 = (f32[4,128,704]{2,1,0:T(8,128)S(1)}, f32[4,128,704]{2,1,0:T(8,128)}, u32[]{:S(2)}) copy-start(f32[4,128,704]{2,1,0:T(8,128)} %conv_back.1) | copy-start | bytes 4325380
  243.7 15.2 %all-to-all-start.4 = ((bf16[8,26,1408]{2,1,0:T(8,128)(2,1)}), bf16[8,26,1408]{2,1,0:T(8,128)(2,1)S(1)}, u32[]{:S(2)}, u32[]{:S(2)}) async-start(bf16[8,26,1408]{2,1,0:T(8,128)(2,1)} %broadcast_in_dim.38), calls=%async_computation.4 | async-start | bytes 1441792 | tf_op jit(solution)/shard_map/all_to_all | solution.py:654

commit v4 on v3

--- a/solution.py
+++ b/solution.py
@@ -239,7 +239,7 @@
     )(normed, *w_up)
 
 
-def mixed_kernel(weighted, w_mine, w_other, act_ref, sq, gm_ref, sums):
+def mixed_kernel(weighted, w_mine, w_other, act_ref, sq, gm_ref, sums, gm_sum):
     def step(w):
         nt = (((1,), (1,)), ((), ()))
         gm = lax.dot_general(weighted[...], w[...], nt, preferred_element_type=F32)
@@ -247,8 +247,7 @@
         act = act_ref[0]
         sums[0, 0:1, :] = jnp.sum(sq[0], axis=0, keepdims=True)
         sums[0, 1:2, :] = jnp.sum(gm * act, axis=0, keepdims=True)
-        sums[0, 2:3, :] = jnp.sum(gm, axis=0, keepdims=True)
-        sums[0, 3:4, :] = jnp.zeros((1, act.shape[1]), F32)
+        gm_sum[0] = jnp.sum(gm, axis=0, keepdims=True)
 
     with_rows(pl.program_id(0), w_mine, w_other, step)
 
@@ -266,8 +265,16 @@
             cols,
             pl.BlockSpec((1, 8, block), lambda h: (h, 0, 0)),
         ],
-        out_specs=[cols, pl.BlockSpec((1, 4, block), lambda h: (h, 0, 0))],
-        out_shape=[jax.ShapeDtypeStruct((4, pixels, block), F32), jax.ShapeDtypeStruct((4, 4, block), F32)],
+        out_specs=[
+            cols,
+            pl.BlockSpec((1, 2, block), lambda h: (h, 0, 0)),
+            pl.BlockSpec((1, 1, block), lambda h: (h, 0, 0)),
+        ],
+        out_shape=[
+            jax.ShapeDtypeStruct((4, pixels, block), F32),
+            jax.ShapeDtypeStruct((4, 2, block), F32),
+            jax.ShapeDtypeStruct((4, 1, block), F32),
+        ],
         compiler_params=params("arbitrary"),
         cost_estimate=cost(8),
         name="mixed_grad",
@@ -292,7 +299,7 @@
     return (gamma * a * ratio + beta + a).astype(BF16)
 
 
-def down_other_kernel(act, weighted, sums, local, gamma, beta, other, ratio, twice, parts):
+def down_other_kernel(act, weighted, sums, local, gm_sum, gamma, beta, other, ratio, twice, parts):
     h = pl.program_id(0)
 
     @pl.when(h == 0)
@@ -305,13 +312,13 @@
         twice[...] = t
         for n in range(4):
             parts[0, n : n + 1, :] = local[n, 1:2] * r[n : n + 1]
-            parts[1, n : n + 1, :] = local[n, 2:3]
+            parts[1, n : n + 1, :] = gm_sum[n]
 
     row = pl.ds(h + 2, 1)
     other[...] = outer(mixed_of(act[0], gamma[row, :], ratio[row, :], beta[row, :]), weighted[...])
 
 
-def down_other(act, weighted, sums, local, gamma, beta):
+def down_other(act, weighted, sums, local, gm_sum, gamma, beta):
     _, pixels, block = act.shape
     width = weighted.shape[1]
     vec = jax.ShapeDtypeStruct((4, block), F32)
@@ -323,6 +330,7 @@
             whole_block(pixels, width),
             whole_block(*sums.shape),
             whole_block(*local.shape),
+            whole_block(*gm_sum.shape),
             whole_block(4, block),
             whole_block(4, block),
         ],
@@ -341,7 +349,7 @@
         compiler_params=params("arbitrary"),
         cost_estimate=cost(4),
         name="down_other",
-    )(act, weighted, sums, local, gamma, beta)
+    )(act, weighted, sums, local, gm_sum, gamma, beta)
 
 
 def down_mine_kernel(act, weighted, ratio, gamma, beta, mine):
@@ -457,25 +465,18 @@
     )(act, slope, gm, *w_up, normed, ratio, twice, gamma, gain.reshape(1, width), xhat, rstd)
 
 
-def taps_grad_kernel(feat, above, below, grad, k_ref, ktaps, part, xs, gs, taps):
+def taps_grad_kernel(feat, above, below, grad, ktaps, xs, gs):
     cols = feat.shape[1]
 
     def chunk(n, lanes):
         fill_padded(xs, above, 0, lanes)
         fill_padded(xs, feat, 3, lanes)
         fill_padded(xs, below, 7, lanes)
-        fill_padded(gs, grad, 0, lanes)
-        spread_taps(taps, k_ref, True, lanes)
-        for start in range(0, cols, GROUP * TILE):
-            acc = [[jnp.zeros((TILE, LANES), F32) for _ in range(GROUP)] for _ in range(4)]
-            acc = taps_group(gs, taps, own_pairs(), start, acc)
-            for o in range(4):
-                for b in range(GROUP):
-                    part[o, tile_rows(start, b), lanes] = acc[o][b]
+        gs[...] = grad[:, :, lanes]
         for j in range(7):
             sums = [jnp.zeros((TILE, LANES), F32) for _ in range(7)]
             for start in range(0, cols, TILE):
-                g = [gs[o, PAD + start : PAD + start + TILE, :] for o in range(4)]
+                g = [gs[o, start : start + TILE, :] for o in range(4)]
                 for r in range(10):
                     x = xs[r, PAD - 3 + j + start : PAD - 3 + j + start + TILE, :]
                     for o in range(4):
@@ -487,7 +488,7 @@
     each_chunk(chunk)
 
 
-def taps_grad(feat, above, below, grad, kernel):
+def taps_grad(feat, above, below, grad):
     rows, cols, width = feat.shape
     return pl.pallas_call(
         taps_grad_kernel,
@@ -497,35 +498,38 @@
             lane_blocks(3, cols),
             lane_blocks(3, cols),
             lane_blocks(rows, cols),
-            lane_blocks(7, 7),
-        ],
-        out_specs=[lane_blocks(7, 7), lane_blocks(rows, cols)],
-        out_shape=[jax.ShapeDtypeStruct((7, 7, width), F32), jax.ShapeDtypeStruct((rows, cols, width), F32)],
+        ],
+        out_specs=lane_blocks(7, 7),
+        out_shape=jax.ShapeDtypeStruct((7, 7, width), F32),
         scratch_shapes=[
             pltpu.VMEM((rows + 6, cols + 2 * PAD, LANES), F32),
-            pltpu.VMEM((rows, cols + 2 * PAD, LANES), F32),
-            pltpu.VMEM((49, TILE, LANES), F32),
-        ],
-        compiler_params=params("arbitrary"),
-        cost_estimate=cost(9),
+            pltpu.VMEM((rows, cols, LANES), F32),
+        ],
+        compiler_params=params("arbitrary"),
+        cost_estimate=cost(1),
         name="taps_grad",
-    )(feat, above, below, grad, kernel)
-
-
-def conv_back_kernel(part, above, below, k_ref, upstream, weight, out, xs, taps):
-    cols = part.shape[1]
+    )(feat, above, below, grad)
+
+
+def all_pairs():
+    return [(r, o, r - o) for r in range(10) for o in range(4) if 0 <= r - o <= 6]
+
+
+def conv_back_kernel(grad, above, below, k_ref, upstream, weight, out, xs, taps):
+    cols = grad.shape[1]
 
     def chunk(n, lanes):
         fill_padded(xs, above, 0, lanes)
-        fill_padded(xs, below, 3, lanes)
+        fill_padded(xs, grad, 3, lanes)
+        fill_padded(xs, below, 7, lanes)
         spread_taps(taps, k_ref, True, lanes)
         for start in range(0, cols, GROUP * TILE):
             acc = [[None] * GROUP for _ in range(4)]
             for o in range(4):
                 for b in range(GROUP):
                     at = tile_rows(start, b)
-                    acc[o][b] = part[o, at, lanes] + upstream[o, at, lanes].astype(F32) * weight[o, at, :]
-            acc = taps_group(xs, taps, halo_pairs(), start, acc)
+                    acc[o][b] = upstream[o, at, lanes].astype(F32) * weight[o, at, :]
+            acc = taps_group(xs, taps, all_pairs(), start, acc)
             for o in range(4):
                 for b in range(GROUP):
                     out[o, tile_rows(start, b), lanes] = acc[o][b]
@@ -533,8 +537,8 @@
     each_chunk(chunk)
 
 
-def conv_back(part, above, below, kernel, upstream, weight):
-    rows, cols, width = part.shape
+def conv_back(grad, above, below, kernel, upstream, weight):
+    rows, cols, width = grad.shape
     return pl.pallas_call(
         conv_back_kernel,
         grid=(pl.cdiv(width, CHUNKS * LANES),),
@@ -549,13 +553,13 @@
         out_specs=lane_blocks(rows, cols),
         out_shape=jax.ShapeDtypeStruct((rows, cols, width), F32),
         scratch_shapes=[
-            pltpu.VMEM((6, cols + 2 * PAD, LANES), F32),
+            pltpu.VMEM((rows + 6, cols + 2 * PAD, LANES), F32),
             pltpu.VMEM((49, TILE, LANES), F32),
         ],
         compiler_params=params("arbitrary"),
-        cost_estimate=cost(5),
+        cost_estimate=cost(60),
         name="conv_back",
-    )(part, above, below, kernel, upstream, weight)
+    )(grad, above, below, kernel, upstream, weight)
 
 
 def chip_kernel(mine, other, vector, out):
@@ -583,7 +587,7 @@
         out_specs=pl.BlockSpec((owners * 4, piece, width), lambda q: (q, 0, 0)),
         out_shape=jax.ShapeDtypeStruct((owners * 8, piece, width), BF16),
         compiler_params=params("arbitrary"),
-        cost_estimate=cost(3),
+        cost_estimate=cost(0.3),
         name="chip_sum",
     )(mine, other, *given)
 
@@ -678,8 +682,9 @@
     above = shift(feat[rows - 3 :], rising)
     below = shift(feat[:3], falling)
     part = conv_own(feat, kernel)
-    mine = gather_mine(jnp.concatenate([w_up, w_down], axis=0))
-    w_up_mine, w_down_mine = mine[:, :owned], mine[:, owned:]
+    w_up_mine = gather_mine(w_up)
+    w_up_mine, w_down, part, above, below = lax.optimization_barrier((w_up_mine, w_down, part, above, below))
+    w_down_mine = gather_mine(w_down)
     gamma, beta = local_order(grn_gamma, owned), local_order(grn_beta, owned)
 
     classes = jnp.arange(class_weight.shape[0], dtype=jnp.int32)
@@ -688,14 +693,13 @@
     weighted = (up.astype(F32) * pixel_weight[..., None]).astype(BF16).reshape(pixels, width)
 
     normed, xhat, rstd = conv_norm(part, above, below, kernel, norm_gain)
-    w_up_mine, w_down_mine, rstd = lax.optimization_barrier((w_up_mine, w_down_mine, rstd))
     w_up_all = with_other(w_up_mine)
     act, slope, sq = up_project(normed, w_up_all)
     w_down_mine, sq = lax.optimization_barrier((w_down_mine, sq))
     w_down_all = with_other(w_down_mine)
-    gm, local = mixed_grad(weighted, w_down_all, act, sq)
+    gm, local, gm_sum = mixed_grad(weighted, w_down_all, act, sq)
     sums = everyone(local, "space")
-    down_other_term, ratio, twice, parts = down_other(act, weighted, sums, local, gamma, beta)
+    down_other_term, ratio, twice, parts = down_other(act, weighted, sums, local, gm_sum, gamma, beta)
     by_owner = lambda rows: rows.reshape(8, owned, width)
     came = to_other_core(by_owner(down_other_term))
     down_blocks = chip_sum(by_owner(down_mine(act, weighted, ratio, gamma, beta)), came)
@@ -707,7 +711,7 @@
     grad_conv = grad_conv.reshape(rows, cols, width)
     g_above = shift(g_last.reshape(3, cols, width), rising)
     g_below = shift(g_first.reshape(3, cols, width), falling)
-    kernel_part, back = taps_grad(feat, above, below, grad_conv, kernel)
+    kernel_part = taps_grad(feat, above, below, grad_conv)
 
     scale = 1.0 / math.sqrt(dp * space * pixels)
     vector = jnp.concatenate(
@@ -720,12 +724,11 @@
     )
     lines = vector.shape[0]
     vector = jnp.pad(vector, ((0, -lines % 64), (0, 0)))
-    vector, g_above, g_below = lax.optimization_barrier((vector, g_above, g_below))
     vector = (vector + to_other_core(vector)).reshape(8, 8, width)
     up_blocks = chip_sum(by_owner(up_mine), to_other_core(by_owner(up_other)), vector)
     up_blocks, down_rows = lax.optimization_barrier((up_blocks, down_rows))
     up_rows = sum_blocks(up_blocks)
-    grad_features = conv_back(back, g_above, g_below, kernel, up, weight)
+    grad_features = conv_back(grad_conv, g_above, g_below, kernel, up, weight)
     up_rows, grad_features = lax.optimization_barrier((up_rows, grad_features))
 
     piece = owned // space

time: 264 us -> 244 us (0.924)
  waiting for transfers between devices: 109 us -> 82 us
  starting transfers between devices: 43.4 us -> 54.6 us
  local copies, waits for them, and re-layouts: 24.1 us -> 21.4 us
    all_to_all x2, waiting for transfers between devices: 33 us -> 7.84 us  [sum_blocks(): lax.all_to_all(blocks, BOTH, 0, 0, axis_index_groups=CORES).astype(F32)]
    all_to_all x1 -> x2, starting transfers between devices: 7.98 us -> 17 us  [gather_mine(): lax.all_to_all(jnp.broadcast_to(shard, (8,) + shard.shape), BOTH, 0, 0, a...]
    ppermute x4, waiting for transfers between devices: 36.9 us -> 45.7 us  [shift(): return lax.ppermute(flat, 'space', pairs).reshape(rows.shape)]
    ppermute x5, waiting for transfers between devices: 8.35 us -> 2.67 us  [to_other_core(): return lax.ppermute(value, BOTH, SWAP)]
    all_to_all x1 -> x2, waiting for transfers between devices: 14.7 us -> 10.1 us  [gather_mine(): lax.all_to_all(jnp.broadcast_to(shard, (8,) + shard.shape), BOTH, 0, 0, a...]
    slice x1 -> x0, local copies, waits for them, and re-layouts: 3.87 us -> none  [body(): w_up_mine, w_down_mine = (mine[:, :owned], mine[:, owned:])]
    pallas_call x1, Pallas kernels: 10.9 us -> 7.75 us  [taps_grad(): pl.pallas_call(taps_grad_kernel, grid=(pl.cdiv(width, CHUNKS * LANES),),...]
    pallas_call x1, Pallas kernels: 5.25 us -> 8.04 us  [conv_back(): pl.pallas_call(conv_back_kernel, grid=(pl.cdiv(width, CHUNKS * LANES),),...]
  transfers between devices with their start and end apart: 14 -> 15, of which waited for: 10 -> 9; matrix products, arithmetic and copies ran while one was open for 4% -> 6% of each run, Pallas kernels for 19% -> 25%
where the time goes in v4:
time: 244 us; the launch traced here: 243 us
  waiting for transfers between devices  82 us (34%)
  Pallas kernels  78.7 us (32%)
  starting transfers between devices  54.6 us (22%)
  local copies, waits for them, and re-layouts  21.4 us (9%)
  other arithmetic  5.53 us (2%)
    ppermute x4, waiting for transfers between devices, shift(): return lax.ppermute(flat, 'space', pairs).reshape(rows.shape)  45.7 us
    all_to_all x2, starting transfers between devices, sum_blocks(): lax.all_to_all(blocks, BOTH, 0, 0, axis_index_groups=CORES).astype(F32)  18.8 us
    all_to_all x2, starting transfers between devices, gather_mine(): lax.all_to_all(jnp.broadcast_to(shard, (8,) + shard.shape), BOTH, 0, 0, a...  17 us
    pallas_call x1, Pallas kernels, hidden_grad(): pl.pallas_call(hidden_kernel, grid=(4,), in_specs=[cols, cols, cols, mine...  16.4 us
    all_to_all x2, waiting for transfers between devices, exchange(): return lax.all_to_all(value, axis, 0, 0)  15.7 us
    all_to_all x2, waiting for transfers between devices, gather_mine(): lax.all_to_all(jnp.broadcast_to(shard, (8,) + shard.shape), BOTH, 0, 0, a...  10.1 us
    pallas_call x1, Pallas kernels, up_project(): pl.pallas_call(up_kernel, grid=(4,), in_specs=[whole_block(pixels, width)...  9.69 us
    all_to_all x2, starting transfers between devices, exchange(): return lax.all_to_all(value, axis, 0, 0)  9.28 us
  transfers between devices with their start and end apart: 15, of which 9 were waited for; matrix products, arithmetic and copies ran while one was open for 6% of the time, Pallas kernels for 25%

profile of v4, /device:TPU:0, one launch (start us, length us, event | category | flops | bytes accessed | tf_op | source)
XLA Modules:
  0.0 243.2 jit_solution(5287292962040660230)
XLA Ops:
  0.6 2.4 %broadcast_in_dim.34 = bf16[8,176,704]{2,1,0:T(8,128)(2,1)} broadcast(bf16[176,704]{1,0:T(8,128)(2,1)} %param.13), dimensions={1,2} | broadcast | bytes 2230272 | tf_op jit(solution)/shard_map/broadcast_in_dim | solution.py:628
  3.1 7.8 %all-to-all-start = ((bf16[8,176,704]{2,1,0:T(8,128)(2,1)}), bf16[8,176,704]{2,1,0:T(8,128)(2,1)S(1)}, u32[]{:S(2)}, u32[]{:S(2)}) async-start(bf16[8,176,704]{2,1,0:T(8,128)(2,1)} %broadcast_in_dim.34), calls=%async_computation | async-start | bytes 4325376 | tf_op jit(solution)/shard_map/all_to_all | solution.py:628
  12.4 2.1 collective-permute-start
  15.8 5.0 %conv_own.1.part = f32[4,128,704]{2,1,0:T(8,128)} custom-call(bf16[4,128,704]{2,1,0:T(8,128)(2,1)} %bitcast.43, f32[7,7,704]{2,1,0:T(8,128)} %k_ref.5), custom_call_target="tpu_custom_call" | custom-call | flops 2000000000 | tf_op jit(solution)/shard_map/conv_own/pallas_call | solution.py:107
  20.8 18.6 %collective-permute-done = bf16[24,16,704]{2,1,0:T(8,128)(2,1)S(1)} collective-permute-done((bf16[24,16,704]{2,1,0:T(8,128)(2,1)S(1)}, bf16[24,16,704]{2,1,0:T(8,128)(2,1)S(1)}, u32[]{:S(2)}, u32[]{:S(2)}) %collective-permute-start) | collective-permute-done | bytes 540704 | tf_op jit(solution)/shard_map/ppermute | solution.py:667
  39.5 2.7 %broadcast_in_dim.37 = bf16[8,176,704]{2,1,0:T(8,128)(2,1)} broadcast(bf16[176,704]{1,0:T(8,128)(2,1)} %param.16), dimensions={1,2} | broadcast | bytes 2230272 | tf_op jit(solution)/shard_map/broadcast_in_dim | solution.py:628
  42.2 9.1 %all-to-all-start.1 = ((bf16[8,176,704]{2,1,0:T(8,128)(2,1)}), bf16[8,176,704]{2,1,0:T(8,128)(2,1)}, u32[]{:S(2)}, u32[]{:S(2)}) async-start(bf16[8,176,704]{2,1,0:T(8,128)(2,1)} %broadcast_in_dim.37), calls=%async_computation.1 | async-start | bytes 4325376 | tf_op jit(solution)/shard_map/all_to_all | solution.py:628
  51.9 7.0 %conv_norm.1 = (bf16[512,704]{1,0:T(8,128)(2,1)}, f32[512,704]{1,0:T(8,128)}, f32[512,128]{1,0:T(8,128)}) custom-call(f32[4,128,704]{2,1,0:T(8,128)} %conv_own.1.part, bf16[3,128,704]{2,1,0:T(8,128)(2,1)} %bitcast.54, bf16[3,128,704]{2,1,0:T(8,128)(2,1)} %bitcast.4.below, f32[7,7,704]{2,1,0:T(8,128)} %k_ref.5, f32[1,704]{1,0:T(1,128)} %reshape.172.gain), custom_call_target="tpu_custom_call" | custom-call | flops 2800000000 | tf_op jit(solution)/shard_map/conv_norm/pallas_call | solution.py:174
  58.9 9.7 %up_project.1 = (f32[4,512,704]{2,1,0:T(8,128)}, f32[4,512,704]{2,1,0:T(8,128)}, f32[4,8,704]{2,1,0:T(8,128)}) custom-call(bf16[512,704]{1,0:T(8,128)(2,1)} %get-tuple-element.42.normed, bf16[1408,704]{1,0:T(8,128)(2,1)} %bitcast.45, bf16[1408,704]{1,0:T(8,128)(2,1)} %bitcast.6.w_other), custom_call_target="tpu_custom_call" | custom-call | flops 3600000000 | tf_op jit(solution)/shard_map/up_project/pallas_call | solution.py:230
  68.6 10.1 %all-to-all-done.1 = bf16[8,176,704]{2,1,0:T(8,128)(2,1)} async-done(((bf16[8,176,704]{2,1,0:T(8,128)(2,1)}), bf16[8,176,704]{2,1,0:T(8,128)(2,1)}, u32[]{:S(2)}, u32[]{:S(2)}) %all-to-all-start.1) | async-done | bytes 1982496 | tf_op jit(solution)/shard_map/all_to_all | solution.py:628
  80.8 2.5 %collective-permute-done.3 = bf16[8,176,704]{2,1,0:T(8,128)(2,1)} collective-permute-done((bf16[8,176,704]{2,1,0:T(8,128)(2,1)}, bf16[8,176,704]{2,1,0:T(8,128)(2,1)}, u32[]{:S(2)}, u32[]{:S(2)}) %collective-permute-start.3) | collective-permute-done | bytes 1982496 | tf_op jit(solution)/shard_map/ppermute | solution.py:624
  83.3 8.6 %mixed_grad.1 = (f32[4,512,704]{2,1,0:T(8,128)}, f32[4,2,704]{2,1,0:T(2,128)}, f32[4,1,704]{2,1,0:T(1,128)}) custom-call(bf16[512,704]{1,0:T(8,128)(2,1)} %fusion.weighted, bf16[1408,704]{1,0:T(8,128)(2,1)} %bitcast.10.w_mine, bf16[1408,704]{1,0:T(8,128)(2,1)} %bitcast.11.w_other, f32[4,512,704]{2,1,0:T(8,128)} %get-tuple-element.44.act_ref.act, ...), custom_call_target="tpu_custom_call" | custom-call | flops 3200000000 | tf_op jit(solution)/shard_map/mixed_grad/pallas_call | solution.py:259
  91.8 1.5 broadcast_in_dim.38
  93.3 4.3 %all-to-all-start.2 = ((f32[8,4,2,704]{3,2,1,0:T(2,128)}), f32[8,4,2,704]{3,2,1,0:T(2,128)S(1)}, u32[]{:S(2)}, u32[]{:S(2)}) async-start(f32[8,4,2,704]{3,2,1,0:T(2,128)} %broadcast_in_dim.38), calls=%async_computation.2 | async-start | bytes 393216 | tf_op jit(solution)/shard_map/all_to_all | solution.py:658
  99.0 5.5 %all-to-all-done.2.sums = f32[8,4,2,704]{3,2,1,0:T(2,128)S(1)} async-done(((f32[8,4,2,704]{3,2,1,0:T(2,128)}), f32[8,4,2,704]{3,2,1,0:T(2,128)S(1)}, u32[]{:S(2)}, u32[]{:S(2)}) %all-to-all-start.2) | async-done | bytes 180256 | tf_op jit(solution)/shard_map/all_to_all | solution.py:658
  105.2 4.6 %down_other.1 = (bf16[1408,704]{1,0:T(8,128)(2,1)}, f32[4,704]{1,0:T(4,128)}, f32[4,704]{1,0:T(4,128)}, f32[2,4,704]{2,1,0:T(4,128)}) custom-call(f32[4,512,704]{2,1,0:T(8,128)} %get-tuple-element.44.act_ref.act, bf16[512,704]{1,0:T(8,128)(2,1)} %fusion.weighted, f32[8,4,2,704]{3,2,1,0:T(2,128)} %copy-done.5, f32[4,2,704]{2,1,0:T(2,128)} %get-tuple-element.51.local, ...), custom_call_target="tpu_custom_call" | custom-call | flops 1600000000 | tf_op jit(solution)/shard_map/down_other/pallas_call | solution.py:325
  109.8 4.3 %down_mine.1 = bf16[1408,704]{1,0:T(8,128)(2,1)} custom-call(f32[4,512,704]{2,1,0:T(8,128)} %get-tuple-element.44.act_ref.act, bf16[512,704]{1,0:T(8,128)(2,1)} %fusion.weighted, f32[4,704]{1,0:T(4,128)} %get-tuple-element.55.ratio, f32[4,704]{1,0:T(4,128)} %pad_maximum_fusion.3.gamma, f32[4,704]{1,0:T(4,128)} %pad_maximum_fusion.4.beta), custom_call_target="tpu_custom_call" | custom-call | flops 1600000000 | tf_op jit(solution)/shard_map/down_mine/pallas_call | solution.py:363
  114.3 1.4 copy-done.3
  115.7 3.5 %chip_sum.2 = bf16[64,22,704]{2,1,0:T(8,128)(2,1)} custom-call(bf16[8,176,704]{2,1,0:T(8,128)(2,1)} %bitcast.47, bf16[8,176,704]{2,1,0:T(8,128)(2,1)} %copy-done.3), custom_call_target="tpu_custom_call" | custom-call | flops 120000000 | tf_op jit(solution)/shard_map/chip_sum/pallas_call | solution.py:583
  119.2 7.5 %all-to-all-start.3 = ((bf16[64,22,704]{2,1,0:T(8,128)(2,1)}), bf16[64,22,704]{2,1,0:T(8,128)(2,1)S(1)}, u32[]{:S(2)}, u32[]{:S(2)}) async-start(bf16[64,22,704]{2,1,0:T(8,128)(2,1)} %chip_sum.2), calls=%async_computation.3 | async-start | bytes 4718592 | tf_op jit(solution)/shard_map/all_to_all | solution.py:654
  126.7 16.4 %hidden_grad.1 = (bf16[1408,704]{1,0:T(8,128)(2,1)}, bf16[1408,704]{1,0:T(8,128)(2,1)}, f32[512,704]{1,0:T(8,128)}, bf16[384,704]{1,0:T(8,128)(2,1)}, bf16[384,704]{1,0:T(8,128)(2,1)}, /*index=5*/f32[8,704]{1,0:T(8,128)}) custom-call(f32[4,512,704]{2,1,0:T(8,128)} %get-tuple-element.44.act_ref.act, f32[4,512,704]{2,1,0:T(8,128)} %get-tuple-element.45.slope, ...), custom_call_target="tpu_custom_call" | custom-call | flops 5600000000 | tf_op jit(solution)/shard_map/hidden_grad/pallas_call | solution.py:442
  143.6 7.7 %taps_grad.1 = f32[7,7,704]{2,1,0:T(8,128)} custom-call(bf16[4,128,704]{2,1,0:T(8,128)(2,1)} %bitcast.44, bf16[3,128,704]{2,1,0:T(8,128)(2,1)} %bitcast.55, bf16[3,128,704]{2,1,0:T(8,128)(2,1)} %bitcast.4.below, f32[4,128,704]{2,1,0:T(8,128)} %bitcast.50), custom_call_target="tpu_custom_call" | custom-call | flops 400000000 | tf_op jit(solution)/shard_map/taps_grad/pallas_call | solution.py:493
  152.9 4.1 %collective-permute-start.7 = (bf16[24,16,704]{2,1,0:T(8,128)(2,1)}, bf16[24,16,704]{2,1,0:T(8,128)(2,1)}, u32[]{:S(2)}, u32[]{:S(2)}) collective-permute-start(bf16[24,16,704]{2,1,0:T(8,128)(2,1)} %bitcast.23), channel_id=1, source_target_pairs={{0,1},{1,2},{2,3},{3,4},{4,5},{5,6},{6,7},{8,9},{9,10},{10,11},{11... | collective-permute-start | bytes 1622024 | tf_op jit(solution)/shard_map/ppermute | solution.py:667
  159.7 3.8 %chip_sum.3 = bf16[64,30,704]{2,1,0:T(8,128)(2,1)} custom-call(bf16[8,176,704]{2,1,0:T(8,128)(2,1)} %bitcast.49, bf16[8,176,704]{2,1,0:T(8,128)(2,1)} %collective-permute-done.5.other, f32[8,8,704]{2,1,0:T(8,128)} %add_bitcast_fusion.vector), custom_call_target="tpu_custom_call" | custom-call | flops 120000000 | tf_op jit(solution)/shard_map/chip_sum/pallas_call | solution.py:583
  163.5 11.3 %all-to-all-start.4 = ((bf16[64,30,704]{2,1,0:T(8,128)(2,1)}), bf16[64,30,704]{2,1,0:T(8,128)(2,1)S(1)}, u32[]{:S(2)}, u32[]{:S(2)}) async-start(bf16[64,30,704]{2,1,0:T(8,128)(2,1)} %chip_sum.3), calls=%async_computation.4 | async-start | bytes 6291456 | tf_op jit(solution)/shard_map/all_to_all | solution.py:654
  174.8 2.3 copy.46
  177.1 27.1 %collective-permute-done.7 = bf16[24,16,704]{2,1,0:T(8,128)(2,1)} collective-permute-done((bf16[24,16,704]{2,1,0:T(8,128)(2,1)}, bf16[24,16,704]{2,1,0:T(8,128)(2,1)}, u32[]{:S(2)}, u32[]{:S(2)}) %collective-permute-start.7) | collective-permute-done | bytes 540704 | tf_op jit(solution)/shard_map/ppermute | solution.py:667
  205.0 8.0 %conv_back.1 = f32[4,128,704]{2,1,0:T(8,128)} custom-call(f32[4,128,704]{2,1,0:T(8,128)} %bitcast.51, bf16[3,128,704]{2,1,0:T(8,128)(2,1)} %bitcast.24.above, bf16[3,128,704]{2,1,0:T(8,128)(2,1)} %bitcast.26.below, f32[7,7,704]{2,1,0:T(8,128)} %k_ref.5, bf16[4,128,704]{2,1,0:T(8,128)(2,1)} %bitcast.53, f32[4,128,128]{2,1,0:T(8,128)} %broadcast_in_dim.40.weight), custom_call_target="tpu_custom_call" | custom-call | flops 24000000000 | tf_op jit(solution)/shard_map/conv_back/pallas_call | solution.py:542
  213.0 7.6 %all-to-all-done.4 = bf16[64,30,704]{2,1,0:T(8,128)(2,1)S(1)} async-done(((bf16[64,30,704]{2,1,0:T(8,128)(2,1)}), bf16[64,30,704]{2,1,0:T(8,128)(2,1)S(1)}, u32[]{:S(2)}, u32[]{:S(2)}) %all-to-all-start.4) | async-done | bytes 2703392 | tf_op jit(solution)/shard_map/all_to_all | solution.py:654
  222.3 5.0 %all-to-all-start.5 = ((bf16[8,26,1408]{2,1,0:T(8,128)(2,1)}), bf16[8,26,1408]{2,1,0:T(8,128)(2,1)S(1)}, u32[]{:S(2)}, u32[]{:S(2)}) async-start(bf16[8,26,1408]{2,1,0:T(8,128)(2,1)} %broadcast_in_dim.42), calls=%async_computation.5 | async-start | bytes 1441792 | tf_op jit(solution)/shard_map/all_to_all | solution.py:658
  227.3 1.6 copy.47
  228.9 10.2 %all-to-all-done.5 = bf16[8,26,1408]{2,1,0:T(8,128)(2,1)S(1)} async-done(((bf16[8,26,1408]{2,1,0:T(8,128)(2,1)}), bf16[8,26,1408]{2,1,0:T(8,128)(2,1)S(1)}, u32[]{:S(2)}, u32[]{:S(2)}) %all-to-all-start.5) | async-done | bytes 585760 | tf_op jit(solution)/shard_map/all_to_all | solution.py:658
  (88 shorter events, 18.8 us)
Async XLA Ops:
  3.1 36.3 %all-to-all-start = ((bf16[8,176,704]{2,1,0:T(8,128)(2,1)}), bf16[8,176,704]{2,1,0:T(8,128)(2,1)S(1)}, u32[]{:S(2)}, u32[]{:S(2)}) async-start(bf16[8,176,704]{2,1,0:T(8,128)(2,1)} %broadcast_in_dim.34), calls=%async_computation | async-start | bytes 4325376 | tf_op jit(solution)/shard_map/all_to_all | solution.py:628
  12.3 3.5 %copy-start = (bf16[1,4,128,704]{3,2,1,0:T(8,128)(2,1)}, bf16[1,4,128,704]{3,2,1,0:T(8,128)(2,1)S(1)}, u32[]{:S(2)}) copy-start(bf16[1,4,128,704]{3,2,1,0:T(8,128)(2,1)S(1)} %copy.37) | copy-start | bytes 2162692
  12.4 27.0 %collective-permute-start = (bf16[24,16,704]{2,1,0:T(8,128)(2,1)S(1)}, bf16[24,16,704]{2,1,0:T(8,128)(2,1)S(1)}, u32[]{:S(2)}, u32[]{:S(2)}) collective-permute-start(bf16[24,16,704]{2,1,0:T(8,128)(2,1)S(1)} %bitcast.57), channel_id=1, source_target_pairs={{0,1},{1,2},{2,3},{3,4},{4,5},{5,6},{6,7},{8,9},{9,10},{10,11},{11... | collective-permute-start | bytes 1622024 | tf_op jit(solution)/shard_map/ppermute | solution.py:667
  14.5 24.9 %collective-permute-start.1 = (bf16[24,16,704]{2,1,0:T(8,128)(2,1)S(1)}, bf16[24,16,704]{2,1,0:T(8,128)(2,1)}, u32[]{:S(2)}, u32[]{:S(2)}) collective-permute-start(bf16[24,16,704]{2,1,0:T(8,128)(2,1)S(1)} %bitcast.56), channel_id=1, source_target_pairs={{1,0},{2,1},{3,2},{4,3},{5,4},{6,5},{7,6},{9,8},{10,9},{11,10},{12... | collective-permute-start | bytes 1622024 | tf_op jit(solution)/shard_map/ppermute | solution.py:667
  39.4 2.8 %copy-start.6 = (bf16[24,16,704]{2,1,0:T(8,128)(2,1)}, bf16[24,16,704]{2,1,0:T(8,128)(2,1)S(1)}, u32[]{:S(2)}) copy-start(bf16[24,16,704]{2,1,0:T(8,128)(2,1)S(1)} %collective-permute-done) | copy-start | bytes 1622020
  39.4 2.8 %copy-start.1 = (bf16[8,176,704]{2,1,0:T(8,128)(2,1)}, bf16[8,176,704]{2,1,0:T(8,128)(2,1)S(1)}, u32[]{:S(2)}) copy-start(bf16[8,176,704]{2,1,0:T(8,128)(2,1)S(1)} %all-to-all-done) | copy-start | bytes 5947396
  39.4 19.5 %collective-permute-start.2 = (bf16[8,176,704]{2,1,0:T(8,128)(2,1)S(1)}, bf16[8,176,704]{2,1,0:T(8,128)(2,1)}, u32[]{:S(2)}, u32[]{:S(2)}) collective-permute-start(bf16[8,176,704]{2,1,0:T(8,128)(2,1)S(1)} %all-to-all-done), channel_id=1, source_target_pairs={{0,8},{1,9},{2,10},{3,11},{4,12},{5,13},{6,14},{7,15},{8,0},{9,1},... | collective-permute-start | bytes 5947400 | tf_op jit(solution)/shard_map/ppermute | solution.py:624
  42.2 9.1 %copy-start.11 = (f32[704]{0:T(1024)S(1)}, f32[704]{0:T(1024)}, u32[]{:S(2)}) copy-start(f32[704]{0:T(1024)} %param.12) | copy-start | bytes 8452
  42.2 36.5 %all-to-all-start.1 = ((bf16[8,176,704]{2,1,0:T(8,128)(2,1)}), bf16[8,176,704]{2,1,0:T(8,128)(2,1)}, u32[]{:S(2)}, u32[]{:S(2)}) async-start(bf16[8,176,704]{2,1,0:T(8,128)(2,1)} %broadcast_in_dim.37), calls=%async_computation.1 | async-start | bytes 4325376 | tf_op jit(solution)/shard_map/all_to_all | solution.py:628
  58.9 19.8 %copy-start.2 = (bf16[1,4,128,704]{2,3,1,0:T(8,128)(2,1)S(1)}, bf16[1,4,128,704]{2,3,1,0:T(8,128)(2,1)}, u32[]{:S(2)}) copy-start(bf16[1,4,128,704]{2,3,1,0:T(8,128)(2,1)} %param.17) | copy-start | bytes 2162692
  68.6 10.4 %copy-start.9 = (f32[2816]{0:T(1024)S(1)}, f32[2816]{0:T(1024)}, u32[]{:S(2)}) copy-start(f32[2816]{0:T(1024)} %param.14) | copy-start | bytes 33796
  68.6 10.5 %copy-start.10 = (f32[2816]{0:T(1024)S(1)}, f32[2816]{0:T(1024)}, u32[]{:S(2)}) copy-start(f32[2816]{0:T(1024)} %param.15) | copy-start | bytes 33796
  68.6 10.9 %copy-start.12 = (s32[1,4,128]{2,1,0:T(4,128)S(1)}, s32[1,4,128]{2,1,0:T(4,128)}, u32[]{:S(2)}) copy-start(s32[1,4,128]{2,1,0:T(4,128)} %param.18) | copy-start | bytes 6148
  68.6 10.9 %copy-start.13 = (f32[150]{0:T(256)S(1)}, f32[150]{0:T(256)}, u32[]{:S(2)}) copy-start(f32[150]{0:T(256)} %param.19) | copy-start | bytes 1804
  78.7 4.6 %collective-permute-start.3 = (bf16[8,176,704]{2,1,0:T(8,128)(2,1)}, bf16[8,176,704]{2,1,0:T(8,128)(2,1)}, u32[]{:S(2)}, u32[]{:S(2)}) collective-permute-start(bf16[8,176,704]{2,1,0:T(8,128)(2,1)} %all-to-all-done.1), channel_id=1, source_target_pairs={{0,8},{1,9},{2,10},{3,11},{4,12},{5,13},{6,14},{7,15},{8,0},{9,1},... | collective-permute-start | bytes 5947400 | tf_op jit(solution)/shard_map/ppermute | solution.py:624
  93.3 11.2 %all-to-all-start.2 = ((f32[8,4,2,704]{3,2,1,0:T(2,128)}), f32[8,4,2,704]{3,2,1,0:T(2,128)S(1)}, u32[]{:S(2)}, u32[]{:S(2)}) async-start(f32[8,4,2,704]{3,2,1,0:T(2,128)} %broadcast_in_dim.38), calls=%async_computation.2 | async-start | bytes 393216 | tf_op jit(solution)/shard_map/all_to_all | solution.py:658
  104.5 0.7 copy-start.5
  109.8 4.5 %collective-permute-start.4 = (bf16[8,176,704]{2,1,0:T(8,128)(2,1)}, bf16[8,176,704]{2,1,0:T(8,128)(2,1)S(1)}, u32[]{:S(2)}, u32[]{:S(2)}) collective-permute-start(bf16[8,176,704]{2,1,0:T(8,128)(2,1)} %bitcast.61), channel_id=1, source_target_pairs={{0,8},{1,9},{2,10},{3,11},{4,12},{5,13},{6,14},{7,15},{8,0},{9,1},... | collective-permute-start | bytes 5947400 | tf_op jit(solution)/shard_map/ppermute | solution.py:624
  114.3 1.4 copy-start.3
  119.2 40.1 %all-to-all-start.3 = ((bf16[64,22,704]{2,1,0:T(8,128)(2,1)}), bf16[64,22,704]{2,1,0:T(8,128)(2,1)S(1)}, u32[]{:S(2)}, u32[]{:S(2)}) async-start(bf16[64,22,704]{2,1,0:T(8,128)(2,1)} %chip_sum.2), calls=%async_computation.3 | async-start | bytes 4718592 | tf_op jit(solution)/shard_map/all_to_all | solution.py:654
  126.7 16.6 %copy-start.7 = (f32[2,4,704]{2,1,0:T(4,128)S(1)}, f32[2,4,704]{2,1,0:T(4,128)}, u32[]{:S(2)}) copy-start(f32[2,4,704]{2,1,0:T(4,128)} %get-tuple-element.63) | copy-start | bytes 67588
  143.2 16.5 %collective-permute-start.5 = (bf16[8,176,704]{2,1,0:T(8,128)(2,1)}, bf16[8,176,704]{2,1,0:T(8,128)(2,1)}, u32[]{:S(2)}, u32[]{:S(2)}) collective-permute-start(bf16[8,176,704]{2,1,0:T(8,128)(2,1)} %bitcast.60), channel_id=1, source_target_pairs={{0,8},{1,9},{2,10},{3,11},{4,12},{5,13},{6,14},{7,15},{8,0},{9,1},... | collective-permute-start | bytes 5947400 | tf_op jit(solution)/shard_map/ppermute | solution.py:624
  143.4 8.9 %copy-start.8 = (f32[8,704]{1,0:T(8,128)S(1)}, f32[8,704]{1,0:T(8,128)}, u32[]{:S(2)}) copy-start(f32[8,704]{1,0:T(8,128)} %get-tuple-element.62) | copy-start | bytes 67588
  152.4 5.9 %collective-permute-start.6 = (f32[64,704]{1,0:T(8,128)S(1)}, f32[64,704]{1,0:T(8,128)S(1)}, u32[]{:S(2)}, u32[]{:S(2)}) collective-permute-start(f32[64,704]{1,0:T(8,128)S(1)} %select_maximum_fusion), channel_id=1, source_target_pairs={{0,8},{1,9},{2,10},{3,11},{4,12},{5,13},{6,14},{7,15},{8,0},{9,1},... | collective-permute-start | bytes 540680 | tf_op jit(solution)/shard_map/ppermute | solution.py:624
  152.9 51.3 %collective-permute-start.7 = (bf16[24,16,704]{2,1,0:T(8,128)(2,1)}, bf16[24,16,704]{2,1,0:T(8,128)(2,1)}, u32[]{:S(2)}, u32[]{:S(2)}) collective-permute-start(bf16[24,16,704]{2,1,0:T(8,128)(2,1)} %bitcast.23), channel_id=1, source_target_pairs={{0,1},{1,2},{2,3},{3,4},{4,5},{5,6},{6,7},{8,9},{9,10},{10,11},{11... | collective-permute-start | bytes 1622024 | tf_op jit(solution)/shard_map/ppermute | solution.py:667
  157.0 47.1 %collective-permute-start.8 = (bf16[24,16,704]{2,1,0:T(8,128)(2,1)}, bf16[24,16,704]{2,1,0:T(8,128)(2,1)}, u32[]{:S(2)}, u32[]{:S(2)}) collective-permute-start(bf16[24,16,704]{2,1,0:T(8,128)(2,1)} %bitcast.25), channel_id=1, source_target_pairs={{1,0},{2,1},{3,2},{4,3},{5,4},{6,5},{7,6},{9,8},{10,9},{11,10},{12... | collective-permute-start | bytes 1622024 | tf_op jit(solution)/shard_map/ppermute | solution.py:667
  163.5 57.1 %all-to-all-start.4 = ((bf16[64,30,704]{2,1,0:T(8,128)(2,1)}), bf16[64,30,704]{2,1,0:T(8,128)(2,1)S(1)}, u32[]{:S(2)}, u32[]{:S(2)}) async-start(bf16[64,30,704]{2,1,0:T(8,128)(2,1)} %chip_sum.3), calls=%async_computation.4 | async-start | bytes 6291456 | tf_op jit(solution)/shard_map/all_to_all | solution.py:654
  221.2 6.1 %copy-start.4 = (f32[4,128,704]{2,1,0:T(8,128)S(1)}, f32[4,128,704]{2,1,0:T(8,128)}, u32[]{:S(2)}) copy-start(f32[4,128,704]{2,1,0:T(8,128)} %conv_back.1) | copy-start | bytes 4325380
  222.3 16.7 %all-to-all-start.5 = ((bf16[8,26,1408]{2,1,0:T(8,128)(2,1)}), bf16[8,26,1408]{2,1,0:T(8,128)(2,1)S(1)}, u32[]{:S(2)}, u32[]{:S(2)}) async-start(bf16[8,26,1408]{2,1,0:T(8,128)(2,1)} %broadcast_in_dim.42), calls=%async_computation.5 | async-start | bytes 1441792 | tf_op jit(solution)/shard_map/all_to_all | solution.py:658

commit v5 on v4

--- a/solution.py
+++ b/solution.py
@@ -562,30 +562,36 @@
     )(grad, above, below, kernel, upstream, weight)
 
 
-def chip_kernel(mine, other, vector, out):
+def chip_kernel(mine, other, vector, edge, out):
+    width = mine.shape[2]
     for q in range(mine.shape[0]):
         high = (mine[q, :128, :].astype(F32) + other[q, :128, :].astype(F32)).astype(BF16)
         low = mine[q, 128:, :].astype(F32) + other[q, 128:, :].astype(F32)
         for s in range(8):
-            out[q * 8 + s, :16, :] = high[16 * s : 16 * (s + 1), :]
+            out[q * 8 + s, :16, :width] = high[16 * s : 16 * (s + 1), :]
             rest = low[6 * s : 6 * (s + 1), :]
             if vector is not None:
                 rest = jnp.concatenate([rest, vector[s]], axis=0)
-            out[q * 8 + s, 16:, :] = rest.astype(BF16)
-
-
-def chip_sum(mine, other, vector=None):
+                out[q * 8 + s, :16, width:] = edge[s, :16, :].astype(BF16)
+                out[q * 8 + s, 16:, width:] = edge[s, 16:, :].astype(BF16)
+            out[q * 8 + s, 16:, :width] = rest.astype(BF16)
+
+
+def chip_sum(mine, other, vector=None, edge=None):
     owners, owned, width = mine.shape
-    piece = owned // 8 + (0 if vector is None else vector.shape[1])
     rows = pl.BlockSpec((owners // 2, owned, width), lambda q: (q, 0, 0))
-    given = [] if vector is None else [vector]
-    kernel = chip_kernel if given else lambda mine, other, out: chip_kernel(mine, other, None, out)
+    if vector is None:
+        given, piece, lanes = [], owned // 8, width
+        kernel = lambda mine, other, out: chip_kernel(mine, other, None, None, out)
+    else:
+        given, piece, lanes = [vector, edge], owned // 8 + 2, width + edge.shape[2]
+        kernel = chip_kernel
     return pl.pallas_call(
         kernel,
         grid=(2,),
-        in_specs=[rows, rows] + [whole_block(*v.shape) for v in given],
-        out_specs=pl.BlockSpec((owners * 4, piece, width), lambda q: (q, 0, 0)),
-        out_shape=jax.ShapeDtypeStruct((owners * 8, piece, width), BF16),
+        in_specs=[rows, rows] + [pl.BlockSpec((8,) + v.shape[1:], lambda q: (q, 0, 0)) for v in given],
+        out_specs=pl.BlockSpec((owners * 4, piece, lanes), lambda q: (q, 0, 0)),
+        out_shape=jax.ShapeDtypeStruct((owners * 8, piece, lanes), BF16),
         compiler_params=params("arbitrary"),
         cost_estimate=cost(0.3),
         name="chip_sum",
@@ -610,18 +616,24 @@
     for c in range(2)
 ]
 
-SWAP = [
-    (device(y, z, c, x, low), device(y, z, 1 - c, x, low))
-    for y in range(2)
-    for z in range(4)
-    for c in range(2)
-    for x in range(4)
-    for low in range(2)
-]
+
+def moved(move):
+    return [
+        (device(y, z, c, x, low), device(*move(y, z, c, x, low)))
+        for y in range(2)
+        for z in range(4)
+        for c in range(2)
+        for x in range(4)
+        for low in range(2)
+    ]
 
 
 def to_other_core(value):
-    return lax.ppermute(value, BOTH, SWAP)
+    return lax.ppermute(value, BOTH, moved(lambda y, z, c, x, low: (y, z, 1 - c, x, low)))
+
+
+def to_other_half(value, cross):
+    return lax.ppermute(value, BOTH, moved(lambda y, z, c, x, low: (1 - y, z, 1 - c if cross else c, x, low)))
 
 
 def gather_mine(shard):
@@ -723,19 +735,25 @@
         axis=0,
     )
     lines = vector.shape[0]
-    vector = jnp.pad(vector, ((0, -lines % 64), (0, 0)))
-    vector = (vector + to_other_core(vector)).reshape(8, 8, width)
-    up_blocks = chip_sum(by_owner(up_mine), to_other_core(by_owner(up_other)), vector)
+    vector = jnp.pad(vector, ((0, -lines % 64), (0, 0))).reshape(16, 4, width)
+    piece = owned // space
+    lanes = 2 * width // piece
+    edge = jnp.pad(vector[:, 2:].reshape(16, piece, lanes), ((0, 0), (0, 2), (0, 0)))
+    up_blocks = chip_sum(by_owner(up_mine), to_other_core(by_owner(up_other)), vector[:, :2], edge)
     up_blocks, down_rows = lax.optimization_barrier((up_blocks, down_rows))
     up_rows = sum_blocks(up_blocks)
     grad_features = conv_back(grad_conv, g_above, g_below, kernel, up, weight)
     up_rows, grad_features = lax.optimization_barrier((up_rows, grad_features))
 
-    piece = owned // space
-    block = jnp.concatenate([up_rows[:piece], down_rows], axis=1)
-    block = jnp.concatenate([block, up_rows[piece:].reshape(4, 2 * width)], axis=0)
+    vector = jnp.concatenate([up_rows[piece:, :width], up_rows[:piece, width:].reshape(2, width)], axis=0)
+    here = vector + to_other_core(vector)
+    there = to_other_half(vector, False) + to_other_half(vector, True)
+    first = lax.axis_index("dp") < 8
+    vector = jnp.concatenate([jnp.where(first, here, there), jnp.where(first, there, here)], axis=0)
+    block = jnp.concatenate([up_rows[:piece, :width], down_rows], axis=1)
+    block = jnp.concatenate([block, vector.reshape(4, 2 * width)], axis=0)
     block = everyone((scale * block).astype(BF16), "space").astype(F32)
-    vector = block[:, piece:].reshape(8 * space, width)
+    vector = jnp.transpose(block[:, piece:].reshape(space, 2, 4, width), (1, 0, 2, 3)).reshape(8 * space, width)
     kernel_sum = vector[:49].reshape(7, 7, width)
     gain_sum = vector[49]
     gamma_sum, beta_sum = vector[50:lines].reshape(2, hid)

time: 244 us -> 241 us (0.988)
  starting transfers between devices: 54.6 us -> 50.7 us
    ppermute x4, waiting for transfers between devices: 45.7 us -> 18.6 us  [shift(): return lax.ppermute(flat, 'space', pairs).reshape(rows.shape)]
    all_to_all x2, waiting for transfers between devices: 7.84 us -> 33 us  [sum_blocks(): lax.all_to_all(blocks, BOTH, 0, 0, axis_index_groups=CORES).astype(F32)]
    all_to_all x2, starting transfers between devices: 18.8 us -> 13.2 us  [sum_blocks(): lax.all_to_all(blocks, BOTH, 0, 0, axis_index_groups=CORES).astype(F32)]
    ppermute x5 -> x7, starting transfers between devices: 0.76 us -> 3.94 us  [the longest x2 2.35 us: to_other_half(): lax.ppermute(value, BOTH, moved(lambda y, z, c, x, low: (1 - y, z, 1 - c...]
    ppermute x5 -> x7, waiting for transfers between devices: 2.67 us -> 5.6 us  [the longest x2 2.93 us: to_other_half(): lax.ppermute(value, BOTH, moved(lambda y, z, c, x, low: (1 - y, z, 1 - c...]
  transfers between devices with their start and end apart: 15 -> 17, of which waited for: 9 -> 10; matrix products, arithmetic and copies ran while one was open for 6% -> 7% of each run, Pallas kernels for 25% -> 26%
where the time goes in v5:
time: 241 us; the launch traced here: 240 us
  waiting for transfers between devices  82 us (34%)
  Pallas kernels  78.5 us (33%)
  starting transfers between devices  50.7 us (21%)
  local copies, waits for them, and re-layouts  23.1 us (10%)
  other arithmetic  4.7 us (2%)
    all_to_all x2, waiting for transfers between devices, sum_blocks(): lax.all_to_all(blocks, BOTH, 0, 0, axis_index_groups=CORES).astype(F32)  33 us
    ppermute x4, waiting for transfers between devices, shift(): return lax.ppermute(flat, 'space', pairs).reshape(rows.shape)  18.6 us
    all_to_all x2, starting transfers between devices, gather_mine(): lax.all_to_all(jnp.broadcast_to(shard, (8,) + shard.shape), BOTH, 0, 0, a...  17 us
    pallas_call x1, Pallas kernels, hidden_grad(): pl.pallas_call(hidden_kernel, grid=(4,), in_specs=[cols, cols, cols, mine...  16.4 us
    all_to_all x2, waiting for transfers between devices, exchange(): return lax.all_to_all(value, axis, 0, 0)  14.7 us
    all_to_all x2, starting transfers between devices, sum_blocks(): lax.all_to_all(blocks, BOTH, 0, 0, axis_index_groups=CORES).astype(F32)  13.2 us
    all_to_all x2, waiting for transfers between devices, gather_mine(): lax.all_to_all(jnp.broadcast_to(shard, (8,) + shard.shape), BOTH, 0, 0, a...  10.1 us
    pallas_call x1, Pallas kernels, up_project(): pl.pallas_call(up_kernel, grid=(4,), in_specs=[whole_block(pixels, width)...  9.65 us
  transfers between devices with their start and end apart: 17, of which 10 were waited for; matrix products, arithmetic and copies ran while one was open for 7% of the time, Pallas kernels for 26%

profile of v5, /device:TPU:0, one launch (start us, length us, event | category | flops | bytes accessed | tf_op | source)
XLA Modules:
  0.0 240.1 jit_solution(16131616724766397276)
XLA Ops:
  0.6 2.4 %broadcast_in_dim.34 = bf16[8,176,704]{2,1,0:T(8,128)(2,1)} broadcast(bf16[176,704]{1,0:T(8,128)(2,1)} %param.13), dimensions={1,2} | broadcast | bytes 2230272 | tf_op jit(solution)/shard_map/broadcast_in_dim | solution.py:640
  3.1 7.8 %all-to-all-start = ((bf16[8,176,704]{2,1,0:T(8,128)(2,1)}), bf16[8,176,704]{2,1,0:T(8,128)(2,1)S(1)}, u32[]{:S(2)}, u32[]{:S(2)}) async-start(bf16[8,176,704]{2,1,0:T(8,128)(2,1)} %broadcast_in_dim.34), calls=%async_computation | async-start | bytes 4325376 | tf_op jit(solution)/shard_map/all_to_all | solution.py:640
  12.4 2.1 collective-permute-start
  15.8 5.0 %conv_own.1.part = f32[4,128,704]{2,1,0:T(8,128)} custom-call(bf16[4,128,704]{2,1,0:T(8,128)(2,1)} %bitcast.43, f32[7,7,704]{2,1,0:T(8,128)} %k_ref.5), custom_call_target="tpu_custom_call" | custom-call | flops 2000000000 | tf_op jit(solution)/shard_map/conv_own/pallas_call | solution.py:107
  20.8 18.6 %collective-permute-done = bf16[24,16,704]{2,1,0:T(8,128)(2,1)S(1)} collective-permute-done((bf16[24,16,704]{2,1,0:T(8,128)(2,1)S(1)}, bf16[24,16,704]{2,1,0:T(8,128)(2,1)S(1)}, u32[]{:S(2)}, u32[]{:S(2)}) %collective-permute-start) | collective-permute-done | bytes 540704 | tf_op jit(solution)/shard_map/ppermute | solution.py:679
  39.5 2.6 %broadcast_in_dim.37 = bf16[8,176,704]{2,1,0:T(8,128)(2,1)} broadcast(bf16[176,704]{1,0:T(8,128)(2,1)} %param.16), dimensions={1,2} | broadcast | bytes 2230272 | tf_op jit(solution)/shard_map/broadcast_in_dim | solution.py:640
  42.1 9.1 %all-to-all-start.1 = ((bf16[8,176,704]{2,1,0:T(8,128)(2,1)}), bf16[8,176,704]{2,1,0:T(8,128)(2,1)}, u32[]{:S(2)}, u32[]{:S(2)}) async-start(bf16[8,176,704]{2,1,0:T(8,128)(2,1)} %broadcast_in_dim.37), calls=%async_computation.1 | async-start | bytes 4325376 | tf_op jit(solution)/shard_map/all_to_all | solution.py:640
  51.9 7.0 %conv_norm.1 = (bf16[512,704]{1,0:T(8,128)(2,1)}, f32[512,704]{1,0:T(8,128)}, f32[512,128]{1,0:T(8,128)}) custom-call(f32[4,128,704]{2,1,0:T(8,128)} %conv_own.1.part, bf16[3,128,704]{2,1,0:T(8,128)(2,1)} %bitcast.55, bf16[3,128,704]{2,1,0:T(8,128)(2,1)} %bitcast.4.below, f32[7,7,704]{2,1,0:T(8,128)} %k_ref.5, f32[1,704]{1,0:T(1,128)} %reshape.181.gain), custom_call_target="tpu_custom_call" | custom-call | flops 2800000000 | tf_op jit(solution)/shard_map/conv_norm/pallas_call | solution.py:174
  58.9 9.6 %up_project.1 = (f32[4,512,704]{2,1,0:T(8,128)}, f32[4,512,704]{2,1,0:T(8,128)}, f32[4,8,704]{2,1,0:T(8,128)}) custom-call(bf16[512,704]{1,0:T(8,128)(2,1)} %get-tuple-element.42.normed, bf16[1408,704]{1,0:T(8,128)(2,1)} %bitcast.45, bf16[1408,704]{1,0:T(8,128)(2,1)} %bitcast.6.w_other), custom_call_target="tpu_custom_call" | custom-call | flops 3600000000 | tf_op jit(solution)/shard_map/up_project/pallas_call | solution.py:230
  68.5 10.1 %all-to-all-done.1 = bf16[8,176,704]{2,1,0:T(8,128)(2,1)} async-done(((bf16[8,176,704]{2,1,0:T(8,128)(2,1)}), bf16[8,176,704]{2,1,0:T(8,128)(2,1)}, u32[]{:S(2)}, u32[]{:S(2)}) %all-to-all-start.1) | async-done | bytes 1982496 | tf_op jit(solution)/shard_map/all_to_all | solution.py:640
  80.8 2.5 %collective-permute-done.3 = bf16[8,176,704]{2,1,0:T(8,128)(2,1)} collective-permute-done((bf16[8,176,704]{2,1,0:T(8,128)(2,1)}, bf16[8,176,704]{2,1,0:T(8,128)(2,1)}, u32[]{:S(2)}, u32[]{:S(2)}) %collective-permute-start.3) | collective-permute-done | bytes 1982496 | tf_op jit(solution)/shard_map/ppermute | solution.py:632
  83.2 8.6 %mixed_grad.1 = (f32[4,512,704]{2,1,0:T(8,128)}, f32[4,2,704]{2,1,0:T(2,128)}, f32[4,1,704]{2,1,0:T(1,128)}) custom-call(bf16[512,704]{1,0:T(8,128)(2,1)} %fusion.weighted, bf16[1408,704]{1,0:T(8,128)(2,1)} %bitcast.10.w_mine, bf16[1408,704]{1,0:T(8,128)(2,1)} %bitcast.11.w_other, f32[4,512,704]{2,1,0:T(8,128)} %get-tuple-element.44.act_ref.act, ...), custom_call_target="tpu_custom_call" | custom-call | flops 3200000000 | tf_op jit(solution)/shard_map/mixed_grad/pallas_call | solution.py:259
  91.8 1.5 broadcast_in_dim.38
  93.3 4.3 %all-to-all-start.2 = ((f32[8,4,2,704]{3,2,1,0:T(2,128)}), f32[8,4,2,704]{3,2,1,0:T(2,128)S(1)}, u32[]{:S(2)}, u32[]{:S(2)}) async-start(f32[8,4,2,704]{3,2,1,0:T(2,128)} %broadcast_in_dim.38), calls=%async_computation.2 | async-start | bytes 393216 | tf_op jit(solution)/shard_map/all_to_all | solution.py:670
  99.0 5.5 %all-to-all-done.2.sums = f32[8,4,2,704]{3,2,1,0:T(2,128)S(1)} async-done(((f32[8,4,2,704]{3,2,1,0:T(2,128)}), f32[8,4,2,704]{3,2,1,0:T(2,128)S(1)}, u32[]{:S(2)}, u32[]{:S(2)}) %all-to-all-start.2) | async-done | bytes 180256 | tf_op jit(solution)/shard_map/all_to_all | solution.py:670
  105.1 4.6 %down_other.1 = (bf16[1408,704]{1,0:T(8,128)(2,1)}, f32[4,704]{1,0:T(4,128)}, f32[4,704]{1,0:T(4,128)}, f32[2,4,704]{2,1,0:T(4,128)}) custom-call(f32[4,512,704]{2,1,0:T(8,128)} %get-tuple-element.44.act_ref.act, bf16[512,704]{1,0:T(8,128)(2,1)} %fusion.weighted, f32[8,4,2,704]{3,2,1,0:T(2,128)} %copy-done.5, f32[4,2,704]{2,1,0:T(2,128)} %get-tuple-element.51.local, ...), custom_call_target="tpu_custom_call" | custom-call | flops 1600000000 | tf_op jit(solution)/shard_map/down_other/pallas_call | solution.py:325
  109.7 4.3 %down_mine.1 = bf16[1408,704]{1,0:T(8,128)(2,1)} custom-call(f32[4,512,704]{2,1,0:T(8,128)} %get-tuple-element.44.act_ref.act, bf16[512,704]{1,0:T(8,128)(2,1)} %fusion.weighted, f32[4,704]{1,0:T(4,128)} %get-tuple-element.55.ratio, f32[4,704]{1,0:T(4,128)} %pad_maximum_fusion.4.gamma, f32[4,704]{1,0:T(4,128)} %pad_maximum_fusion.5.beta), custom_call_target="tpu_custom_call" | custom-call | flops 1600000000 | tf_op jit(solution)/shard_map/down_mine/pallas_call | solution.py:363
  115.6 3.5 %chip_sum.2 = bf16[64,22,704]{2,1,0:T(8,128)(2,1)} custom-call(bf16[8,176,704]{2,1,0:T(8,128)(2,1)} %bitcast.47, bf16[8,176,704]{2,1,0:T(8,128)(2,1)} %copy-done.3), custom_call_target="tpu_custom_call" | custom-call | flops 120000000 | tf_op jit(solution)/shard_map/chip_sum/pallas_call | solution.py:589
  119.2 7.5 %all-to-all-start.3 = ((bf16[64,22,704]{2,1,0:T(8,128)(2,1)}), bf16[64,22,704]{2,1,0:T(8,128)(2,1)S(1)}, u32[]{:S(2)}, u32[]{:S(2)}) async-start(bf16[64,22,704]{2,1,0:T(8,128)(2,1)} %chip_sum.2), calls=%async_computation.3 | async-start | bytes 4718592 | tf_op jit(solution)/shard_map/all_to_all | solution.py:666
  126.7 16.4 %hidden_grad.1 = (bf16[1408,704]{1,0:T(8,128)(2,1)}, bf16[1408,704]{1,0:T(8,128)(2,1)}, f32[512,704]{1,0:T(8,128)}, bf16[384,704]{1,0:T(8,128)(2,1)}, bf16[384,704]{1,0:T(8,128)(2,1)}, /*index=5*/f32[8,704]{1,0:T(8,128)}) custom-call(f32[4,512,704]{2,1,0:T(8,128)} %get-tuple-element.44.act_ref.act, f32[4,512,704]{2,1,0:T(8,128)} %get-tuple-element.45.slope, ...), custom_call_target="tpu_custom_call" | custom-call | flops 5600000000 | tf_op jit(solution)/shard_map/hidden_grad/pallas_call | solution.py:442
  143.6 4.1 %collective-permute-start.6 = (bf16[24,16,704]{2,1,0:T(8,128)(2,1)}, bf16[24,16,704]{2,1,0:T(8,128)(2,1)}, u32[]{:S(2)}, u32[]{:S(2)}) collective-permute-start(bf16[24,16,704]{2,1,0:T(8,128)(2,1)} %bitcast.65), channel_id=1, source_target_pairs={{0,1},{1,2},{2,3},{3,4},{4,5},{5,6},{6,7},{8,9},{9,10},{10,11},{11... | collective-permute-start | bytes 1622024 | tf_op jit(solution)/shard_map/ppermute | solution.py:679
  149.0 7.8 %taps_grad.1 = f32[7,7,704]{2,1,0:T(8,128)} custom-call(bf16[4,128,704]{2,1,0:T(8,128)(2,1)} %bitcast.44, bf16[3,128,704]{2,1,0:T(8,128)(2,1)} %bitcast.56, bf16[3,128,704]{2,1,0:T(8,128)(2,1)} %bitcast.4.below, f32[4,128,704]{2,1,0:T(8,128)} %bitcast.50), custom_call_target="tpu_custom_call" | custom-call | flops 400000000 | tf_op jit(solution)/shard_map/taps_grad/pallas_call | solution.py:493
  160.3 11.3 %all-to-all-done.3 = bf16[64,22,704]{2,1,0:T(8,128)(2,1)S(1)} async-done(((bf16[64,22,704]{2,1,0:T(8,128)(2,1)}), bf16[64,22,704]{2,1,0:T(8,128)(2,1)S(1)}, u32[]{:S(2)}, u32[]{:S(2)}) %all-to-all-start.3) | async-done | bytes 1982496 | tf_op jit(solution)/shard_map/all_to_all | solution.py:666
  172.0 3.7 %chip_sum.3 = bf16[64,24,768]{2,1,0:T(8,128)(2,1)} custom-call(bf16[8,176,704]{2,1,0:T(8,128)(2,1)} %bitcast.49, bf16[8,176,704]{2,1,0:T(8,128)(2,1)} %collective-permute-done.5.other, f32[16,2,704]{2,1,0:T(2,128)} %get-tuple-element.103.vector, f32[16,24,64]{2,1,0:T(8,128)} %pad.9.edge), custom_call_target="tpu_custom_call" | custom-call | flops 120000000 | tf_op jit(solution)/shard_map/chip_sum/pallas_call | solution.py:589
  175.7 5.7 %all-to-all-start.4 = ((bf16[64,24,768]{2,1,0:T(8,128)(2,1)}), bf16[64,24,768]{2,1,0:T(8,128)(2,1)S(1)}, u32[]{:S(2)}, u32[]{:S(2)}) async-start(bf16[64,24,768]{2,1,0:T(8,128)(2,1)} %chip_sum.3), calls=%async_computation.4 | async-start | bytes 4718592 | tf_op jit(solution)/shard_map/all_to_all | solution.py:666
  183.4 8.1 %conv_back.1 = f32[4,128,704]{2,1,0:T(8,128)} custom-call(f32[4,128,704]{2,1,0:T(8,128)} %bitcast.51, bf16[3,128,704]{2,1,0:T(8,128)(2,1)} %bitcast.23.above, bf16[3,128,704]{2,1,0:T(8,128)(2,1)} %bitcast.25.below, f32[7,7,704]{2,1,0:T(8,128)} %k_ref.5, bf16[4,128,704]{2,1,0:T(8,128)(2,1)} %bitcast.53, f32[4,128,128]{2,1,0:T(8,128)} %broadcast_in_dim.40.weight), custom_call_target="tpu_custom_call" | custom-call | flops 24000000000 | tf_op jit(solution)/shard_map/conv_back/pallas_call | solution.py:542
  191.4 21.7 %all-to-all-done.4 = bf16[64,24,768]{2,1,0:T(8,128)(2,1)S(1)} async-done(((bf16[64,24,768]{2,1,0:T(8,128)(2,1)}), bf16[64,24,768]{2,1,0:T(8,128)(2,1)S(1)}, u32[]{:S(2)}, u32[]{:S(2)}) %all-to-all-start.4) | async-done | bytes 2359328 | tf_op jit(solution)/shard_map/all_to_all | solution.py:666
  215.1 2.3 collective-permute-start.9
  218.4 1.9 collective-permute-done.9
  221.4 3.5 %all-to-all-start.5 = ((bf16[8,26,1408]{2,1,0:T(8,128)(2,1)}), bf16[8,26,1408]{2,1,0:T(8,128)(2,1)S(1)}, u32[]{:S(2)}, u32[]{:S(2)}) async-start(bf16[8,26,1408]{2,1,0:T(8,128)(2,1)} %broadcast_in_dim.42), calls=%async_computation.5 | async-start | bytes 1441792 | tf_op jit(solution)/shard_map/all_to_all | solution.py:670
  225.0 1.6 copy.50
  226.6 9.2 %all-to-all-done.5 = bf16[8,26,1408]{2,1,0:T(8,128)(2,1)S(1)} async-done(((bf16[8,26,1408]{2,1,0:T(8,128)(2,1)}), bf16[8,26,1408]{2,1,0:T(8,128)(2,1)S(1)}, u32[]{:S(2)}, u32[]{:S(2)}) %all-to-all-start.5) | async-done | bytes 585760 | tf_op jit(solution)/shard_map/all_to_all | solution.py:670
  (101 shorter events, 25.1 us)
Async XLA Ops:
  3.1 36.3 %all-to-all-start = ((bf16[8,176,704]{2,1,0:T(8,128)(2,1)}), bf16[8,176,704]{2,1,0:T(8,128)(2,1)S(1)}, u32[]{:S(2)}, u32[]{:S(2)}) async-start(bf16[8,176,704]{2,1,0:T(8,128)(2,1)} %broadcast_in_dim.34), calls=%async_computation | async-start | bytes 4325376 | tf_op jit(solution)/shard_map/all_to_all | solution.py:640
  12.3 3.5 %copy-start = (bf16[1,4,128,704]{3,2,1,0:T(8,128)(2,1)}, bf16[1,4,128,704]{3,2,1,0:T(8,128)(2,1)S(1)}, u32[]{:S(2)}) copy-start(bf16[1,4,128,704]{3,2,1,0:T(8,128)(2,1)S(1)} %copy.39) | copy-start | bytes 2162692
  12.4 27.0 %collective-permute-start = (bf16[24,16,704]{2,1,0:T(8,128)(2,1)S(1)}, bf16[24,16,704]{2,1,0:T(8,128)(2,1)S(1)}, u32[]{:S(2)}, u32[]{:S(2)}) collective-permute-start(bf16[24,16,704]{2,1,0:T(8,128)(2,1)S(1)} %bitcast.58), channel_id=1, source_target_pairs={{0,1},{1,2},{2,3},{3,4},{4,5},{5,6},{6,7},{8,9},{9,10},{10,11},{11... | collective-permute-start | bytes 1622024 | tf_op jit(solution)/shard_map/ppermute | solution.py:679
  14.5 24.9 %collective-permute-start.1 = (bf16[24,16,704]{2,1,0:T(8,128)(2,1)S(1)}, bf16[24,16,704]{2,1,0:T(8,128)(2,1)}, u32[]{:S(2)}, u32[]{:S(2)}) collective-permute-start(bf16[24,16,704]{2,1,0:T(8,128)(2,1)S(1)} %bitcast.57), channel_id=1, source_target_pairs={{1,0},{2,1},{3,2},{4,3},{5,4},{6,5},{7,6},{9,8},{10,9},{11,10},{12... | collective-permute-start | bytes 1622024 | tf_op jit(solution)/shard_map/ppermute | solution.py:679
  39.4 2.8 %copy-start.6 = (bf16[24,16,704]{2,1,0:T(8,128)(2,1)}, bf16[24,16,704]{2,1,0:T(8,128)(2,1)S(1)}, u32[]{:S(2)}) copy-start(bf16[24,16,704]{2,1,0:T(8,128)(2,1)S(1)} %collective-permute-done) | copy-start | bytes 1622020
  39.4 2.7 %copy-start.1 = (bf16[8,176,704]{2,1,0:T(8,128)(2,1)}, bf16[8,176,704]{2,1,0:T(8,128)(2,1)S(1)}, u32[]{:S(2)}) copy-start(bf16[8,176,704]{2,1,0:T(8,128)(2,1)S(1)} %all-to-all-done) | copy-start | bytes 5947396
  39.4 19.4 %collective-permute-start.2 = (bf16[8,176,704]{2,1,0:T(8,128)(2,1)S(1)}, bf16[8,176,704]{2,1,0:T(8,128)(2,1)}, u32[]{:S(2)}, u32[]{:S(2)}) collective-permute-start(bf16[8,176,704]{2,1,0:T(8,128)(2,1)S(1)} %all-to-all-done), channel_id=1, source_target_pairs={{0,8},{1,9},{2,10},{3,11},{4,12},{5,13},{6,14},{7,15},{8,0},{9,1},... | collective-permute-start | bytes 5947400 | tf_op jit(solution)/shard_map/ppermute | solution.py:632
  42.1 9.1 %copy-start.11 = (f32[704]{0:T(1024)S(1)}, f32[704]{0:T(1024)}, u32[]{:S(2)}) copy-start(f32[704]{0:T(1024)} %param.12) | copy-start | bytes 8452
  42.1 36.5 %all-to-all-start.1 = ((bf16[8,176,704]{2,1,0:T(8,128)(2,1)}), bf16[8,176,704]{2,1,0:T(8,128)(2,1)}, u32[]{:S(2)}, u32[]{:S(2)}) async-start(bf16[8,176,704]{2,1,0:T(8,128)(2,1)} %broadcast_in_dim.37), calls=%async_computation.1 | async-start | bytes 4325376 | tf_op jit(solution)/shard_map/all_to_all | solution.py:640
  58.8 19.8 %copy-start.2 = (bf16[1,4,128,704]{2,3,1,0:T(8,128)(2,1)S(1)}, bf16[1,4,128,704]{2,3,1,0:T(8,128)(2,1)}, u32[]{:S(2)}) copy-start(bf16[1,4,128,704]{2,3,1,0:T(8,128)(2,1)} %param.17) | copy-start | bytes 2162692
  68.5 10.5 %copy-start.9 = (f32[2816]{0:T(1024)S(1)}, f32[2816]{0:T(1024)}, u32[]{:S(2)}) copy-start(f32[2816]{0:T(1024)} %param.14) | copy-start | bytes 33796
  68.5 10.6 %copy-start.10 = (f32[2816]{0:T(1024)S(1)}, f32[2816]{0:T(1024)}, u32[]{:S(2)}) copy-start(f32[2816]{0:T(1024)} %param.15) | copy-start | bytes 33796
  68.5 10.9 %copy-start.12 = (s32[1,4,128]{2,1,0:T(4,128)S(1)}, s32[1,4,128]{2,1,0:T(4,128)}, u32[]{:S(2)}) copy-start(s32[1,4,128]{2,1,0:T(4,128)} %param.18) | copy-start | bytes 6148
  68.5 10.9 %copy-start.13 = (f32[150]{0:T(256)S(1)}, f32[150]{0:T(256)}, u32[]{:S(2)}) copy-start(f32[150]{0:T(256)} %param.19) | copy-start | bytes 1804
  78.7 4.6 %collective-permute-start.3 = (bf16[8,176,704]{2,1,0:T(8,128)(2,1)}, bf16[8,176,704]{2,1,0:T(8,128)(2,1)}, u32[]{:S(2)}, u32[]{:S(2)}) collective-permute-start(bf16[8,176,704]{2,1,0:T(8,128)(2,1)} %all-to-all-done.1), channel_id=1, source_target_pairs={{0,8},{1,9},{2,10},{3,11},{4,12},{5,13},{6,14},{7,15},{8,0},{9,1},... | collective-permute-start | bytes 5947400 | tf_op jit(solution)/shard_map/ppermute | solution.py:632
  93.3 11.2 %all-to-all-start.2 = ((f32[8,4,2,704]{3,2,1,0:T(2,128)}), f32[8,4,2,704]{3,2,1,0:T(2,128)S(1)}, u32[]{:S(2)}, u32[]{:S(2)}) async-start(f32[8,4,2,704]{3,2,1,0:T(2,128)} %broadcast_in_dim.38), calls=%async_computation.2 | async-start | bytes 393216 | tf_op jit(solution)/shard_map/all_to_all | solution.py:670
  104.5 0.7 copy-start.5
  109.7 4.5 %collective-permute-start.4 = (bf16[8,176,704]{2,1,0:T(8,128)(2,1)}, bf16[8,176,704]{2,1,0:T(8,128)(2,1)S(1)}, u32[]{:S(2)}, u32[]{:S(2)}) collective-permute-start(bf16[8,176,704]{2,1,0:T(8,128)(2,1)} %bitcast.63), channel_id=1, source_target_pairs={{0,8},{1,9},{2,10},{3,11},{4,12},{5,13},{6,14},{7,15},{8,0},{9,1},... | collective-permute-start | bytes 5947400 | tf_op jit(solution)/shard_map/ppermute | solution.py:632
  114.2 1.4 copy-start.3
  119.2 52.5 %all-to-all-start.3 = ((bf16[64,22,704]{2,1,0:T(8,128)(2,1)}), bf16[64,22,704]{2,1,0:T(8,128)(2,1)S(1)}, u32[]{:S(2)}, u32[]{:S(2)}) async-start(bf16[64,22,704]{2,1,0:T(8,128)(2,1)} %chip_sum.2), calls=%async_computation.3 | async-start | bytes 4718592 | tf_op jit(solution)/shard_map/all_to_all | solution.py:666
  126.7 16.6 %copy-start.7 = (f32[2,4,704]{2,1,0:T(4,128)S(1)}, f32[2,4,704]{2,1,0:T(4,128)}, u32[]{:S(2)}) copy-start(f32[2,4,704]{2,1,0:T(4,128)} %get-tuple-element.63) | copy-start | bytes 67588
  143.1 28.9 %collective-permute-start.5 = (bf16[8,176,704]{2,1,0:T(8,128)(2,1)}, bf16[8,176,704]{2,1,0:T(8,128)(2,1)}, u32[]{:S(2)}, u32[]{:S(2)}) collective-permute-start(bf16[8,176,704]{2,1,0:T(8,128)(2,1)} %bitcast.62), channel_id=1, source_target_pairs={{0,8},{1,9},{2,10},{3,11},{4,12},{5,13},{6,14},{7,15},{8,0},{9,1},... | collective-permute-start | bytes 5947400 | tf_op jit(solution)/shard_map/ppermute | solution.py:632
  143.4 14.3 %copy-start.8 = (f32[8,704]{1,0:T(8,128)S(1)}, f32[8,704]{1,0:T(8,128)}, u32[]{:S(2)}) copy-start(f32[8,704]{1,0:T(8,128)} %get-tuple-element.62) | copy-start | bytes 67588
  143.6 39.0 %collective-permute-start.6 = (bf16[24,16,704]{2,1,0:T(8,128)(2,1)}, bf16[24,16,704]{2,1,0:T(8,128)(2,1)}, u32[]{:S(2)}, u32[]{:S(2)}) collective-permute-start(bf16[24,16,704]{2,1,0:T(8,128)(2,1)} %bitcast.65), channel_id=1, source_target_pairs={{0,1},{1,2},{2,3},{3,4},{4,5},{5,6},{6,7},{8,9},{9,10},{10,11},{11... | collective-permute-start | bytes 1622024 | tf_op jit(solution)/shard_map/ppermute | solution.py:679
  147.7 34.9 %collective-permute-start.7 = (bf16[24,16,704]{2,1,0:T(8,128)(2,1)}, bf16[24,16,704]{2,1,0:T(8,128)(2,1)}, u32[]{:S(2)}, u32[]{:S(2)}) collective-permute-start(bf16[24,16,704]{2,1,0:T(8,128)(2,1)} %bitcast.64), channel_id=1, source_target_pairs={{1,0},{2,1},{3,2},{4,3},{5,4},{6,5},{7,6},{9,8},{10,9},{11,10},{12... | collective-permute-start | bytes 1622024 | tf_op jit(solution)/shard_map/ppermute | solution.py:679
  175.7 37.4 %all-to-all-start.4 = ((bf16[64,24,768]{2,1,0:T(8,128)(2,1)}), bf16[64,24,768]{2,1,0:T(8,128)(2,1)S(1)}, u32[]{:S(2)}, u32[]{:S(2)}) async-start(bf16[64,24,768]{2,1,0:T(8,128)(2,1)} %chip_sum.3), calls=%async_computation.4 | async-start | bytes 4718592 | tf_op jit(solution)/shard_map/all_to_all | solution.py:666
  213.5 11.5 %copy-start.4 = (f32[4,128,704]{2,1,0:T(8,128)S(1)}, f32[4,128,704]{2,1,0:T(8,128)}, u32[]{:S(2)}) copy-start(f32[4,128,704]{2,1,0:T(8,128)} %conv_back.1) | copy-start | bytes 4325380
  213.6 4.7 %collective-permute-start.10 = (f32[4,704]{1,0:T(4,128)S(1)}, f32[4,704]{1,0:T(4,128)S(1)}, u32[]{:S(2)}, u32[]{:S(2)}) collective-permute-start(f32[4,704]{1,0:T(4,128)S(1)} %pad_maximum_fusion.6), channel_id=1, source_target_pairs={{0,72},{1,73},{2,74},{3,75},{4,76},{5,77},{6,78},{7,79},{8,64},{9,... | collective-permute-start | bytes 33800 | tf_op jit(solution)/shard_map/ppermute | solution.py:636
  213.7 4.6 %collective-permute-start.8 = (f32[4,704]{1,0:T(4,128)S(1)}, f32[4,704]{1,0:T(4,128)S(1)}, u32[]{:S(2)}, u32[]{:S(2)}) collective-permute-start(f32[4,704]{1,0:T(4,128)S(1)} %pad_maximum_fusion.6), channel_id=1, source_target_pairs={{0,8},{1,9},{2,10},{3,11},{4,12},{5,13},{6,14},{7,15},{8,0},{9,1},... | collective-permute-start | bytes 33800 | tf_op jit(solution)/shard_map/ppermute | solution.py:632
  215.1 5.2 %collective-permute-start.9 = (f32[4,704]{1,0:T(4,128)S(1)}, f32[4,704]{1,0:T(4,128)S(1)}, u32[]{:S(2)}, u32[]{:S(2)}) collective-permute-start(f32[4,704]{1,0:T(4,128)S(1)} %pad_maximum_fusion.6), channel_id=1, source_target_pairs={{0,64},{1,65},{2,66},{3,67},{4,68},{5,69},{6,70},{7,71},{8,72},{9,... | collective-permute-start | bytes 33800 | tf_op jit(solution)/shard_map/ppermute | solution.py:636
  221.4 14.3 %all-to-all-start.5 = ((bf16[8,26,1408]{2,1,0:T(8,128)(2,1)}), bf16[8,26,1408]{2,1,0:T(8,128)(2,1)S(1)}, u32[]{:S(2)}, u32[]{:S(2)}) async-start(bf16[8,26,1408]{2,1,0:T(8,128)(2,1)} %broadcast_in_dim.42), calls=%async_computation.5 | async-start | bytes 1441792 | tf_op jit(solution)/shard_map/all_to_all | solution.py:670

commit v6 on v5

--- a/solution.py
+++ b/solution.py
@@ -198,6 +198,10 @@
     )(part, above, below, kernel, gain.reshape(1, width))
 
 
+IN_VMEM = pl.BlockSpec(memory_space=pltpu.VMEM)
+STAY = pltpu.CompilerParams(vmem_limit_bytes=12 * 1024 * 1024)
+
+
 def with_rows(h, mine, other, step):
     pl.when(h < 2)(lambda: step(mine))
     pl.when(h >= 2)(lambda: step(other))
@@ -240,16 +244,17 @@
 
 
 def mixed_kernel(weighted, w_mine, w_other, act_ref, sq, gm_ref, sums, gm_sum):
+    h = pl.program_id(0)
+
     def step(w):
         nt = (((1,), (1,)), ((), ()))
         gm = lax.dot_general(weighted[...], w[...], nt, preferred_element_type=F32)
         gm_ref[0] = gm
-        act = act_ref[0]
-        sums[0, 0:1, :] = jnp.sum(sq[0], axis=0, keepdims=True)
-        sums[0, 1:2, :] = jnp.sum(gm * act, axis=0, keepdims=True)
-        gm_sum[0] = jnp.sum(gm, axis=0, keepdims=True)
-
-    with_rows(pl.program_id(0), w_mine, w_other, step)
+        sums[pl.ds(h, 1), :] = jnp.sum(sq[0], axis=0, keepdims=True)
+        sums[pl.ds(h + 4, 1), :] = jnp.sum(gm * act_ref[0], axis=0, keepdims=True)
+        gm_sum[pl.ds(h, 1), :] = jnp.sum(gm, axis=0, keepdims=True)
+
+    with_rows(h, w_mine, w_other, step)
 
 
 def mixed_grad(weighted, w_down, act, sq):
@@ -265,15 +270,11 @@
             cols,
             pl.BlockSpec((1, 8, block), lambda h: (h, 0, 0)),
         ],
-        out_specs=[
-            cols,
-            pl.BlockSpec((1, 2, block), lambda h: (h, 0, 0)),
-            pl.BlockSpec((1, 1, block), lambda h: (h, 0, 0)),
-        ],
+        out_specs=[cols, whole_block(8, block), whole_block(4, block)],
         out_shape=[
             jax.ShapeDtypeStruct((4, pixels, block), F32),
-            jax.ShapeDtypeStruct((4, 2, block), F32),
-            jax.ShapeDtypeStruct((4, 1, block), F32),
+            jax.ShapeDtypeStruct((8, block), F32),
+            jax.ShapeDtypeStruct((4, block), F32),
         ],
         compiler_params=params("arbitrary"),
         cost_estimate=cost(8),
@@ -291,31 +292,34 @@
     return energy / mean, (grad_ratio / mean - shared) / energy
 
 
+def store_rows(half, i, value):
+    block = half.shape[0] // 2
+    half[pl.ds(pl.multiple_of(i * block, block), block), :] = value
+
+
 def outer(left, right):
     return lax.dot_general(left, right, (((0,), (0,)), ((), ())), preferred_element_type=F32).astype(BF16)
 
 
-def mixed_of(a, gamma, ratio, beta):
-    return (gamma * a * ratio + beta + a).astype(BF16)
+def down_rows_of(half, first, act, weighted, gamma, ratio, beta):
+    def one(i, carry):
+        row = pl.ds(first + i, 1)
+        a = act[first + i]
+        mixed = (gamma[row, :] * a * ratio[row, :] + beta[row, :] + a).astype(BF16)
+        store_rows(half, i, outer(mixed, weighted[...]))
+        return carry
+
+    lax.fori_loop(0, 2, one, 0)
 
 
 def down_other_kernel(act, weighted, sums, local, gm_sum, gamma, beta, other, ratio, twice, parts):
-    h = pl.program_id(0)
-
-    @pl.when(h == 0)
-    def _():
-        crop = jnp.sum(sums[...], axis=0)
-        sq = jnp.concatenate([crop[n, 0:1] for n in range(4)], axis=0)
-        dot = jnp.concatenate([crop[n, 1:2] for n in range(4)], axis=0)
-        r, t = ratio_of(sq, dot, gamma[...])
-        ratio[...] = r
-        twice[...] = t
-        for n in range(4):
-            parts[0, n : n + 1, :] = local[n, 1:2] * r[n : n + 1]
-            parts[1, n : n + 1, :] = gm_sum[n]
-
-    row = pl.ds(h + 2, 1)
-    other[...] = outer(mixed_of(act[0], gamma[row, :], ratio[row, :], beta[row, :]), weighted[...])
+    crop = jnp.sum(sums[...], axis=0)
+    r, t = ratio_of(crop[:4], crop[4:], gamma[...])
+    ratio[...] = r
+    twice[...] = t
+    parts[0] = local[4:, :] * r
+    parts[1] = gm_sum[...]
+    down_rows_of(other, 2, act, weighted, gamma, ratio, beta)
 
 
 def down_other(act, weighted, sums, local, gm_sum, gamma, beta):
@@ -324,37 +328,22 @@
     vec = jax.ShapeDtypeStruct((4, block), F32)
     return pl.pallas_call(
         down_other_kernel,
-        grid=(2,),
-        in_specs=[
-            pl.BlockSpec((1, pixels, block), lambda h: (h + 2, 0, 0)),
-            whole_block(pixels, width),
-            whole_block(*sums.shape),
-            whole_block(*local.shape),
-            whole_block(*gm_sum.shape),
-            whole_block(4, block),
-            whole_block(4, block),
-        ],
-        out_specs=[
-            pl.BlockSpec((block, width), lambda h: (h, 0)),
-            whole_block(4, block),
-            whole_block(4, block),
-            whole_block(2, 4, block),
-        ],
+        in_specs=[IN_VMEM] * 7,
+        out_specs=[IN_VMEM] * 4,
         out_shape=[
             jax.ShapeDtypeStruct((2 * block, width), BF16),
             vec,
             vec,
             jax.ShapeDtypeStruct((2, 4, block), F32),
         ],
-        compiler_params=params("arbitrary"),
+        compiler_params=STAY,
         cost_estimate=cost(4),
         name="down_other",
     )(act, weighted, sums, local, gm_sum, gamma, beta)
 
 
 def down_mine_kernel(act, weighted, ratio, gamma, beta, mine):
-    row = pl.ds(pl.program_id(0), 1)
-    mine[...] = outer(mixed_of(act[0], gamma[row, :], ratio[row, :], beta[row, :]), weighted[...])
+    down_rows_of(mine, 0, act, weighted, gamma, ratio, beta)
 
 
 def down_mine(act, weighted, ratio, gamma, beta):
@@ -362,17 +351,10 @@
     width = weighted.shape[1]
     return pl.pallas_call(
         down_mine_kernel,
-        grid=(2,),
-        in_specs=[
-            pl.BlockSpec((1, pixels, block), lambda h: (h, 0, 0)),
-            whole_block(pixels, width),
-            whole_block(4, block),
-            whole_block(4, block),
-            whole_block(4, block),
-        ],
-        out_specs=pl.BlockSpec((block, width), lambda h: (h, 0)),
+        in_specs=[IN_VMEM] * 5,
+        out_specs=IN_VMEM,
         out_shape=jax.ShapeDtypeStruct((2 * block, width), BF16),
-        compiler_params=params("arbitrary"),
+        compiler_params=STAY,
         cost_estimate=cost(4),
         name="down_mine",
     )(act, weighted, ratio, gamma, beta)
@@ -564,22 +546,25 @@
 
 def chip_kernel(mine, other, vector, edge, out):
     width = mine.shape[2]
-    for q in range(mine.shape[0]):
+    def one(q, carry):
         high = (mine[q, :128, :].astype(F32) + other[q, :128, :].astype(F32)).astype(BF16)
         low = mine[q, 128:, :].astype(F32) + other[q, 128:, :].astype(F32)
         for s in range(8):
             out[q * 8 + s, :16, :width] = high[16 * s : 16 * (s + 1), :]
             rest = low[6 * s : 6 * (s + 1), :]
             if vector is not None:
-                rest = jnp.concatenate([rest, vector[s]], axis=0)
-                out[q * 8 + s, :16, width:] = edge[s, :16, :].astype(BF16)
-                out[q * 8 + s, 16:, width:] = edge[s, 16:, :].astype(BF16)
+                at = q // 4 * 8 + s
+                rest = jnp.concatenate([rest, vector[at]], axis=0)
+                out[q * 8 + s, :16, width:] = edge[at, :16, :].astype(BF16)
+                out[q * 8 + s, 16:, width:] = edge[at, 16:, :].astype(BF16)
             out[q * 8 + s, 16:, :width] = rest.astype(BF16)
+        return carry
+
+    lax.fori_loop(0, mine.shape[0], one, 0)
 
 
 def chip_sum(mine, other, vector=None, edge=None):
     owners, owned, width = mine.shape
-    rows = pl.BlockSpec((owners // 2, owned, width), lambda q: (q, 0, 0))
     if vector is None:
         given, piece, lanes = [], owned // 8, width
         kernel = lambda mine, other, out: chip_kernel(mine, other, None, None, out)
@@ -588,11 +573,10 @@
         kernel = chip_kernel
     return pl.pallas_call(
         kernel,
-        grid=(2,),
-        in_specs=[rows, rows] + [pl.BlockSpec((8,) + v.shape[1:], lambda q: (q, 0, 0)) for v in given],
-        out_specs=pl.BlockSpec((owners * 4, piece, lanes), lambda q: (q, 0, 0)),
+        in_specs=[IN_VMEM] * (2 + len(given)),
+        out_specs=IN_VMEM,
         out_shape=jax.ShapeDtypeStruct((owners * 8, piece, lanes), BF16),
-        compiler_params=params("arbitrary"),
+        compiler_params=STAY,
         cost_estimate=cost(0.3),
         name="chip_sum",
     )(mine, other, *given)

time: 241 us -> 239 us (level)
  Pallas kernels: 78.5 us -> 72.1 us
  waiting for transfers between devices: 82 us -> 84.6 us
    pallas_call x4, Pallas kernels: 16.1 us -> 9.57 us  [the longest x2 6.05 us: chip_sum(): pl.pallas_call(kernel, in_specs=[IN_VMEM] * (2 + len(given)), out_specs=I...]
    unnamed x31 -> x45, local copies, waits for them, and re-layouts: 6.29 us -> 9.24 us
  transfers between devices with their start and end apart: 17 -> 17, of which waited for: 10 -> 10; matrix products, arithmetic and copies ran while one was open for 7% -> 5% of each run, Pallas kernels for 26% -> 25%
where the time goes in v6:
time: 239 us; the launch traced here: 237 us
  waiting for transfers between devices  84.6 us (35%)
  Pallas kernels  72.1 us (30%)
  starting transfers between devices  50.4 us (21%)
  local copies, waits for them, and re-layouts  23.8 us (10%)
  other arithmetic  5.17 us (2%)
    all_to_all x2, waiting for transfers between devices, sum_blocks(): lax.all_to_all(blocks, BOTH, 0, 0, axis_index_groups=CORES).astype(F32)  32.8 us
    ppermute x4, waiting for transfers between devices, shift(): return lax.ppermute(flat, 'space', pairs).reshape(rows.shape)  18.6 us
    all_to_all x2, starting transfers between devices, gather_mine(): lax.all_to_all(jnp.broadcast_to(shard, (8,) + shard.shape), BOTH, 0, 0, a...  17.1 us
    pallas_call x1, Pallas kernels, hidden_grad(): pl.pallas_call(hidden_kernel, grid=(4,), in_specs=[cols, cols, cols, mine...  16.5 us
    all_to_all x2, waiting for transfers between devices, exchange(): return lax.all_to_all(value, axis, 0, 0)  15.9 us
    all_to_all x2, starting transfers between devices, sum_blocks(): lax.all_to_all(blocks, BOTH, 0, 0, axis_index_groups=CORES).astype(F32)  12.9 us
    pallas_call x1, Pallas kernels, up_project(): pl.pallas_call(up_kernel, grid=(4,), in_specs=[whole_block(pixels, width)...  9.64 us
    unnamed x45, local copies, waits for them, and re-layouts  9.24 us
  transfers between devices with their start and end apart: 17, of which 10 were waited for; matrix products, arithmetic and copies ran while one was open for 5% of the time, Pallas kernels for 25%

profile of v6, /device:TPU:0, one launch (start us, length us, event | category | flops | bytes accessed | tf_op | source)
XLA Modules:
  0.0 237.2 jit_solution(14562091889032800842)
XLA Ops:
  0.6 2.5 %broadcast_in_dim.34 = bf16[8,176,704]{2,1,0:T(8,128)(2,1)} broadcast(bf16[176,704]{1,0:T(8,128)(2,1)} %param.13), dimensions={1,2} | broadcast | bytes 2230272 | tf_op jit(solution)/shard_map/broadcast_in_dim | solution.py:624
  3.1 8.0 %all-to-all-start = ((bf16[8,176,704]{2,1,0:T(8,128)(2,1)}), bf16[8,176,704]{2,1,0:T(8,128)(2,1)}, u32[]{:S(2)}, u32[]{:S(2)}) async-start(bf16[8,176,704]{2,1,0:T(8,128)(2,1)} %broadcast_in_dim.34), calls=%async_computation | async-start | bytes 4325376 | tf_op jit(solution)/shard_map/all_to_all | solution.py:624
  11.5 2.1 collective-permute-start
  14.9 5.0 %conv_own.1.part = f32[4,128,704]{2,1,0:T(8,128)} custom-call(bf16[4,128,704]{2,1,0:T(8,128)(2,1)} %bitcast.46, f32[7,7,704]{2,1,0:T(8,128)} %k_ref.5), custom_call_target="tpu_custom_call" | custom-call | flops 2000000000 | tf_op jit(solution)/shard_map/conv_own/pallas_call | solution.py:107
  19.8 18.6 %collective-permute-done = bf16[24,16,704]{2,1,0:T(8,128)(2,1)S(1)} collective-permute-done((bf16[24,16,704]{2,1,0:T(8,128)(2,1)S(1)}, bf16[24,16,704]{2,1,0:T(8,128)(2,1)S(1)}, u32[]{:S(2)}, u32[]{:S(2)}) %collective-permute-start) | collective-permute-done | bytes 540704 | tf_op jit(solution)/shard_map/ppermute | solution.py:663
  38.6 2.7 %broadcast_in_dim.37 = bf16[8,176,704]{2,1,0:T(8,128)(2,1)} broadcast(bf16[176,704]{1,0:T(8,128)(2,1)} %param.16), dimensions={1,2} | broadcast | bytes 2230272 | tf_op jit(solution)/shard_map/broadcast_in_dim | solution.py:624
  41.3 9.1 %all-to-all-start.1 = ((bf16[8,176,704]{2,1,0:T(8,128)(2,1)}), bf16[8,176,704]{2,1,0:T(8,128)(2,1)}, u32[]{:S(2)}, u32[]{:S(2)}) async-start(bf16[8,176,704]{2,1,0:T(8,128)(2,1)} %broadcast_in_dim.37), calls=%async_computation.1 | async-start | bytes 4325376 | tf_op jit(solution)/shard_map/all_to_all | solution.py:624
  51.0 7.0 %conv_norm.1 = (bf16[512,704]{1,0:T(8,128)(2,1)}, f32[512,704]{1,0:T(8,128)}, f32[512,128]{1,0:T(8,128)}) custom-call(f32[4,128,704]{2,1,0:T(8,128)} %conv_own.1.part, bf16[3,128,704]{2,1,0:T(8,128)(2,1)} %bitcast.56, bf16[3,128,704]{2,1,0:T(8,128)(2,1)} %bitcast.58, f32[7,7,704]{2,1,0:T(8,128)} %k_ref.5, f32[1,704]{1,0:T(1,128)} %reshape.181.gain), custom_call_target="tpu_custom_call" | custom-call | flops 2800000000 | tf_op jit(solution)/shard_map/conv_norm/pallas_call | solution.py:174
  59.3 9.6 %up_project.1 = (f32[4,512,704]{2,1,0:T(8,128)}, f32[4,512,704]{2,1,0:T(8,128)}, f32[4,8,704]{2,1,0:T(8,128)}) custom-call(bf16[512,704]{1,0:T(8,128)(2,1)} %get-tuple-element.42.normed, bf16[1408,704]{1,0:T(8,128)(2,1)} %bitcast.5.w_mine, bf16[1408,704]{1,0:T(8,128)(2,1)} %bitcast.49), custom_call_target="tpu_custom_call" | custom-call | flops 3600000000 | tf_op jit(solution)/shard_map/up_project/pallas_call | solution.py:234
  69.0 8.8 %all-to-all-done.1 = bf16[8,176,704]{2,1,0:T(8,128)(2,1)} async-done(((bf16[8,176,704]{2,1,0:T(8,128)(2,1)}), bf16[8,176,704]{2,1,0:T(8,128)(2,1)}, u32[]{:S(2)}, u32[]{:S(2)}) %all-to-all-start.1) | async-done | bytes 1982496 | tf_op jit(solution)/shard_map/all_to_all | solution.py:624
  79.9 2.5 %collective-permute-done.3 = bf16[8,176,704]{2,1,0:T(8,128)(2,1)} collective-permute-done((bf16[8,176,704]{2,1,0:T(8,128)(2,1)}, bf16[8,176,704]{2,1,0:T(8,128)(2,1)}, u32[]{:S(2)}, u32[]{:S(2)}) %collective-permute-start.3) | collective-permute-done | bytes 1982496 | tf_op jit(solution)/shard_map/ppermute | solution.py:616
  82.4 8.6 %mixed_grad.1 = (f32[4,512,704]{2,1,0:T(8,128)}, f32[8,704]{1,0:T(8,128)}, f32[4,704]{1,0:T(4,128)}) custom-call(bf16[512,704]{1,0:T(8,128)(2,1)} %fusion.weighted, bf16[1408,704]{1,0:T(8,128)(2,1)} %bitcast.10.w_mine, bf16[1408,704]{1,0:T(8,128)(2,1)} %bitcast.11.w_other, f32[4,512,704]{2,1,0:T(8,128)} %get-tuple-element.44.act_ref.act, ...), custom_call_target="tpu_custom_call" | custom-call | flops 3200000000 | tf_op jit(solution)/shard_map/mixed_grad/pallas_call | solution.py:264
  92.4 4.3 %all-to-all-start.2 = ((f32[8,8,704]{2,1,0:T(8,128)}), f32[8,8,704]{2,1,0:T(8,128)S(1)}, u32[]{:S(2)}, u32[]{:S(2)}) async-start(f32[8,8,704]{2,1,0:T(8,128)} %broadcast_in_dim.38), calls=%async_computation.2 | async-start | bytes 393216 | tf_op jit(solution)/shard_map/all_to_all | solution.py:654
  96.9 6.7 %all-to-all-done.2.sums = f32[8,8,704]{2,1,0:T(8,128)S(1)} async-done(((f32[8,8,704]{2,1,0:T(8,128)}), f32[8,8,704]{2,1,0:T(8,128)S(1)}, u32[]{:S(2)}, u32[]{:S(2)}) %all-to-all-start.2) | async-done | bytes 180256 | tf_op jit(solution)/shard_map/all_to_all | solution.py:654
  103.6 2.8 %copy-done = f32[4,512,704]{2,1,0:T(8,128)S(1)} copy-done((f32[4,512,704]{2,1,0:T(8,128)S(1)}, f32[4,512,704]{2,1,0:T(8,128)}, u32[]{:S(2)}) %copy-start) | copy-done | bytes 5767192
  107.9 1.8 down_other.1
  112.0 2.5 %collective-permute-done.4.other = bf16[8,176,704]{2,1,0:T(8,128)(2,1)S(1)} collective-permute-done((bf16[8,176,704]{2,1,0:T(8,128)(2,1)S(1)}, bf16[8,176,704]{2,1,0:T(8,128)(2,1)S(1)}, u32[]{:S(2)}, u32[]{:S(2)}) %collective-permute-start.4) | collective-permute-done | bytes 1982496 | tf_op jit(solution)/shard_map/ppermute | solution.py:616
  114.6 2.0 chip_sum.2
  116.6 7.8 %all-to-all-start.3 = ((bf16[64,22,704]{2,1,0:T(8,128)(2,1)}), bf16[64,22,704]{2,1,0:T(8,128)(2,1)}, u32[]{:S(2)}, u32[]{:S(2)}) async-start(bf16[64,22,704]{2,1,0:T(8,128)(2,1)} %chip_sum.2), calls=%async_computation.3 | async-start | bytes 4718592 | tf_op jit(solution)/shard_map/all_to_all | solution.py:650
  124.4 16.5 %hidden_grad.1 = (bf16[1408,704]{1,0:T(8,128)(2,1)}, bf16[1408,704]{1,0:T(8,128)(2,1)}, f32[512,704]{1,0:T(8,128)}, bf16[384,704]{1,0:T(8,128)(2,1)}, bf16[384,704]{1,0:T(8,128)(2,1)}, /*index=5*/f32[8,704]{1,0:T(8,128)}) custom-call(f32[4,512,704]{2,1,0:T(8,128)} %get-tuple-element.44.act_ref.act, f32[4,512,704]{2,1,0:T(8,128)} %get-tuple-element.45.slope, ...), custom_call_target="tpu_custom_call" | custom-call | flops 5600000000 | tf_op jit(solution)/shard_map/hidden_grad/pallas_call | solution.py:424
  141.2 4.1 %collective-permute-start.6 = (bf16[24,16,704]{2,1,0:T(8,128)(2,1)}, bf16[24,16,704]{2,1,0:T(8,128)(2,1)}, u32[]{:S(2)}, u32[]{:S(2)}) collective-permute-start(bf16[24,16,704]{2,1,0:T(8,128)(2,1)} %bitcast.67), channel_id=1, source_target_pairs={{0,1},{1,2},{2,3},{3,4},{4,5},{5,6},{6,7},{8,9},{9,10},{10,11},{11... | collective-permute-start | bytes 1622024 | tf_op jit(solution)/shard_map/ppermute | solution.py:663
  146.5 7.8 %taps_grad.1 = f32[7,7,704]{2,1,0:T(8,128)} custom-call(bf16[4,128,704]{2,1,0:T(8,128)(2,1)} %bitcast.47, bf16[3,128,704]{2,1,0:T(8,128)(2,1)} %bitcast.57, bf16[3,128,704]{2,1,0:T(8,128)(2,1)} %bitcast.59, f32[4,128,704]{2,1,0:T(8,128)} %bitcast.51), custom_call_target="tpu_custom_call" | custom-call | flops 400000000 | tf_op jit(solution)/shard_map/taps_grad/pallas_call | solution.py:475
  155.7 13.7 %all-to-all-done.3 = bf16[64,22,704]{2,1,0:T(8,128)(2,1)} async-done(((bf16[64,22,704]{2,1,0:T(8,128)(2,1)}), bf16[64,22,704]{2,1,0:T(8,128)(2,1)}, u32[]{:S(2)}, u32[]{:S(2)}) %all-to-all-start.3) | async-done | bytes 1982496 | tf_op jit(solution)/shard_map/all_to_all | solution.py:650
  169.3 2.1 convert_reduce_fusion.1
  171.4 4.0 %chip_sum.3 = bf16[64,24,768]{2,1,0:T(8,128)(2,1)} custom-call(bf16[8,176,704]{2,1,0:T(8,128)(2,1)S(1)} %bitcast.44, bf16[8,176,704]{2,1,0:T(8,128)(2,1)} %collective-permute-done.5.other, f32[16,2,704]{2,1,0:T(2,128)S(1)} %get-tuple-element.103.vector, f32[16,24,64]{2,1,0:T(8,128)S(1)} %pad.9.edge), custom_call_target="tpu_custom_call" | custom-call | flops 120000000 | tf_op jit(solution)/shard_map/chip_sum/pallas_call | solution.py:574
  175.5 5.1 %all-to-all-start.4 = ((bf16[64,24,768]{2,1,0:T(8,128)(2,1)}), bf16[64,24,768]{2,1,0:T(8,128)(2,1)S(1)}, u32[]{:S(2)}, u32[]{:S(2)}) async-start(bf16[64,24,768]{2,1,0:T(8,128)(2,1)} %chip_sum.3), calls=%async_computation.4 | async-start | bytes 4718592 | tf_op jit(solution)/shard_map/all_to_all | solution.py:650
  182.6 8.1 %conv_back.1 = f32[4,128,704]{2,1,0:T(8,128)} custom-call(f32[4,128,704]{2,1,0:T(8,128)} %bitcast.52, bf16[3,128,704]{2,1,0:T(8,128)(2,1)} %bitcast.23.above, bf16[3,128,704]{2,1,0:T(8,128)(2,1)} %bitcast.25.below, f32[7,7,704]{2,1,0:T(8,128)} %k_ref.5, bf16[4,128,704]{2,1,0:T(8,128)(2,1)} %bitcast.54, f32[4,128,128]{2,1,0:T(8,128)} %broadcast_in_dim.40.weight), custom_call_target="tpu_custom_call" | custom-call | flops 24000000000 | tf_op jit(solution)/shard_map/conv_back/pallas_call | solution.py:524
  190.7 19.1 %all-to-all-done.4 = bf16[64,24,768]{2,1,0:T(8,128)(2,1)S(1)} async-done(((bf16[64,24,768]{2,1,0:T(8,128)(2,1)}), bf16[64,24,768]{2,1,0:T(8,128)(2,1)S(1)}, u32[]{:S(2)}, u32[]{:S(2)}) %all-to-all-start.4) | async-done | bytes 2359328 | tf_op jit(solution)/shard_map/all_to_all | solution.py:650
  210.4 1.9 collective-permute-start.8
  215.0 2.5 %collective-permute-done.9 = f32[4,704]{1,0:T(4,128)S(1)} collective-permute-done((f32[4,704]{1,0:T(4,128)S(1)}, f32[4,704]{1,0:T(4,128)S(1)}, u32[]{:S(2)}, u32[]{:S(2)}) %collective-permute-start.9) | collective-permute-done | bytes 11296 | tf_op jit(solution)/shard_map/ppermute | solution.py:620
  218.6 3.5 %all-to-all-start.5 = ((bf16[8,26,1408]{2,1,0:T(8,128)(2,1)}), bf16[8,26,1408]{2,1,0:T(8,128)(2,1)S(1)}, u32[]{:S(2)}, u32[]{:S(2)}) async-start(bf16[8,26,1408]{2,1,0:T(8,128)(2,1)} %broadcast_in_dim.42), calls=%async_computation.5 | async-start | bytes 1441792 | tf_op jit(solution)/shard_map/all_to_all | solution.py:654
  223.7 9.2 %all-to-all-done.5 = bf16[8,26,1408]{2,1,0:T(8,128)(2,1)S(1)} async-done(((bf16[8,26,1408]{2,1,0:T(8,128)(2,1)}), bf16[8,26,1408]{2,1,0:T(8,128)(2,1)S(1)}, u32[]{:S(2)}, u32[]{:S(2)}) %all-to-all-start.5) | async-done | bytes 585760 | tf_op jit(solution)/shard_map/all_to_all | solution.py:654
  (115 shorter events, 26.2 us)
Async XLA Ops:
  3.1 8.0 %copy-start.12 = (bf16[1,4,128,704]{2,3,1,0:T(8,128)(2,1)S(1)}, bf16[1,4,128,704]{2,3,1,0:T(8,128)(2,1)}, u32[]{:S(2)}) copy-start(bf16[1,4,128,704]{2,3,1,0:T(8,128)(2,1)} %param.10) | copy-start | bytes 2162692
  3.1 35.4 %all-to-all-start = ((bf16[8,176,704]{2,1,0:T(8,128)(2,1)}), bf16[8,176,704]{2,1,0:T(8,128)(2,1)}, u32[]{:S(2)}, u32[]{:S(2)}) async-start(bf16[8,176,704]{2,1,0:T(8,128)(2,1)} %broadcast_in_dim.34), calls=%async_computation | async-start | bytes 4325376 | tf_op jit(solution)/shard_map/all_to_all | solution.py:624
  11.4 3.5 %copy-start.8 = (bf16[1,4,128,704]{3,2,1,0:T(8,128)(2,1)}, bf16[1,4,128,704]{3,2,1,0:T(8,128)(2,1)S(1)}, u32[]{:S(2)}) copy-start(bf16[1,4,128,704]{3,2,1,0:T(8,128)(2,1)S(1)} %copy.39) | copy-start | bytes 2162692
  11.5 27.0 %collective-permute-start = (bf16[24,16,704]{2,1,0:T(8,128)(2,1)S(1)}, bf16[24,16,704]{2,1,0:T(8,128)(2,1)S(1)}, u32[]{:S(2)}, u32[]{:S(2)}) collective-permute-start(bf16[24,16,704]{2,1,0:T(8,128)(2,1)S(1)} %bitcast.61), channel_id=1, source_target_pairs={{0,1},{1,2},{2,3},{3,4},{4,5},{5,6},{6,7},{8,9},{9,10},{10,11},{11... | collective-permute-start | bytes 1622024 | tf_op jit(solution)/shard_map/ppermute | solution.py:663
  13.6 24.9 %collective-permute-start.1 = (bf16[24,16,704]{2,1,0:T(8,128)(2,1)S(1)}, bf16[24,16,704]{2,1,0:T(8,128)(2,1)S(1)}, u32[]{:S(2)}, u32[]{:S(2)}) collective-permute-start(bf16[24,16,704]{2,1,0:T(8,128)(2,1)S(1)} %bitcast.60), channel_id=1, source_target_pairs={{1,0},{2,1},{3,2},{4,3},{5,4},{6,5},{7,6},{9,8},{10,9},{11,10},{12... | collective-permute-start | bytes 1622024 | tf_op jit(solution)/shard_map/ppermute | solution.py:663
  38.5 2.8 %copy-start.13 = (bf16[24,16,704]{2,1,0:T(8,128)(2,1)}, bf16[24,16,704]{2,1,0:T(8,128)(2,1)S(1)}, u32[]{:S(2)}) copy-start(bf16[24,16,704]{2,1,0:T(8,128)(2,1)S(1)} %collective-permute-done) | copy-start | bytes 1622020
  38.5 2.8 %copy-start.14 = (bf16[24,16,704]{2,1,0:T(8,128)(2,1)}, bf16[24,16,704]{2,1,0:T(8,128)(2,1)S(1)}, u32[]{:S(2)}) copy-start(bf16[24,16,704]{2,1,0:T(8,128)(2,1)S(1)} %collective-permute-done.1) | copy-start | bytes 1622020
  38.5 19.5 %collective-permute-start.2 = (bf16[8,176,704]{2,1,0:T(8,128)(2,1)}, bf16[8,176,704]{2,1,0:T(8,128)(2,1)S(1)}, u32[]{:S(2)}, u32[]{:S(2)}) collective-permute-start(bf16[8,176,704]{2,1,0:T(8,128)(2,1)} %all-to-all-done), channel_id=1, source_target_pairs={{0,8},{1,9},{2,10},{3,11},{4,12},{5,13},{6,14},{7,15},{8,0},{9,1},... | collective-permute-start | bytes 5947400 | tf_op jit(solution)/shard_map/ppermute | solution.py:616
  41.3 9.1 %copy-start.18 = (f32[704]{0:T(1024)S(1)}, f32[704]{0:T(1024)}, u32[]{:S(2)}) copy-start(f32[704]{0:T(1024)} %param.12) | copy-start | bytes 8452
  41.3 36.5 %all-to-all-start.1 = ((bf16[8,176,704]{2,1,0:T(8,128)(2,1)}), bf16[8,176,704]{2,1,0:T(8,128)(2,1)}, u32[]{:S(2)}, u32[]{:S(2)}) async-start(bf16[8,176,704]{2,1,0:T(8,128)(2,1)} %broadcast_in_dim.37), calls=%async_computation.1 | async-start | bytes 4325376 | tf_op jit(solution)/shard_map/all_to_all | solution.py:624
  59.3 18.5 %copy-start.9 = (bf16[1,4,128,704]{2,3,1,0:T(8,128)(2,1)S(1)}, bf16[1,4,128,704]{2,3,1,0:T(8,128)(2,1)}, u32[]{:S(2)}) copy-start(bf16[1,4,128,704]{2,3,1,0:T(8,128)(2,1)} %param.17) | copy-start | bytes 2162692
  68.9 9.1 %copy-start.16 = (f32[2816]{0:T(1024)S(1)}, f32[2816]{0:T(1024)}, u32[]{:S(2)}) copy-start(f32[2816]{0:T(1024)} %param.14) | copy-start | bytes 33796
  68.9 9.2 %copy-start.17 = (f32[2816]{0:T(1024)S(1)}, f32[2816]{0:T(1024)}, u32[]{:S(2)}) copy-start(f32[2816]{0:T(1024)} %param.15) | copy-start | bytes 33796
  69.0 9.6 %copy-start.19 = (s32[1,4,128]{2,1,0:T(4,128)S(1)}, s32[1,4,128]{2,1,0:T(4,128)}, u32[]{:S(2)}) copy-start(s32[1,4,128]{2,1,0:T(4,128)} %param.18) | copy-start | bytes 6148
  69.0 9.6 %copy-start.20 = (f32[150]{0:T(256)S(1)}, f32[150]{0:T(256)}, u32[]{:S(2)}) copy-start(f32[150]{0:T(256)} %param.19) | copy-start | bytes 1804
  77.8 4.6 %collective-permute-start.3 = (bf16[8,176,704]{2,1,0:T(8,128)(2,1)}, bf16[8,176,704]{2,1,0:T(8,128)(2,1)}, u32[]{:S(2)}, u32[]{:S(2)}) collective-permute-start(bf16[8,176,704]{2,1,0:T(8,128)(2,1)} %all-to-all-done.1), channel_id=1, source_target_pairs={{0,8},{1,9},{2,10},{3,11},{4,12},{5,13},{6,14},{7,15},{8,0},{9,1},... | collective-permute-start | bytes 5947400 | tf_op jit(solution)/shard_map/ppermute | solution.py:616
  82.4 21.3 %copy-start.1 = (bf16[512,704]{1,0:T(8,128)(2,1)S(1)}, bf16[512,704]{1,0:T(8,128)(2,1)}, u32[]{:S(2)}) copy-start(bf16[512,704]{1,0:T(8,128)(2,1)} %fusion.weighted) | copy-start | bytes 2162692
  92.4 11.2 %all-to-all-start.2 = ((f32[8,8,704]{2,1,0:T(8,128)}), f32[8,8,704]{2,1,0:T(8,128)S(1)}, u32[]{:S(2)}, u32[]{:S(2)}) async-start(f32[8,8,704]{2,1,0:T(8,128)} %broadcast_in_dim.38), calls=%async_computation.2 | async-start | bytes 393216 | tf_op jit(solution)/shard_map/all_to_all | solution.py:654
  96.8 13.6 %copy-start.3 = (f32[4,704]{1,0:T(4,128)}, f32[4,704]{1,0:T(4,128)S(1)}, u32[]{:S(2)}) copy-start(f32[4,704]{1,0:T(4,128)S(1)} %pad_maximum_fusion.4.gamma) | copy-start | bytes 33796
  110.3 4.3 %collective-permute-start.4 = (bf16[8,176,704]{2,1,0:T(8,128)(2,1)S(1)}, bf16[8,176,704]{2,1,0:T(8,128)(2,1)S(1)}, u32[]{:S(2)}, u32[]{:S(2)}) collective-permute-start(bf16[8,176,704]{2,1,0:T(8,128)(2,1)S(1)} %bitcast.45), channel_id=1, source_target_pairs={{0,8},{1,9},{2,10},{3,11},{4,12},{5,13},{6,14},{7,15},{8,0},{9,1},... | collective-permute-start | bytes 5947400 | tf_op jit(solution)/shard_map/ppermute | solution.py:616
  116.6 52.8 %all-to-all-start.3 = ((bf16[64,22,704]{2,1,0:T(8,128)(2,1)}), bf16[64,22,704]{2,1,0:T(8,128)(2,1)}, u32[]{:S(2)}, u32[]{:S(2)}) async-start(bf16[64,22,704]{2,1,0:T(8,128)(2,1)} %chip_sum.2), calls=%async_computation.3 | async-start | bytes 4718592 | tf_op jit(solution)/shard_map/all_to_all | solution.py:650
  140.8 30.6 %collective-permute-start.5 = (bf16[8,176,704]{2,1,0:T(8,128)(2,1)}, bf16[8,176,704]{2,1,0:T(8,128)(2,1)}, u32[]{:S(2)}, u32[]{:S(2)}) collective-permute-start(bf16[8,176,704]{2,1,0:T(8,128)(2,1)} %bitcast.65), channel_id=1, source_target_pairs={{0,8},{1,9},{2,10},{3,11},{4,12},{5,13},{6,14},{7,15},{8,0},{9,1},... | collective-permute-start | bytes 5947400 | tf_op jit(solution)/shard_map/ppermute | solution.py:616
  141.0 14.2 %copy-start.15 = (f32[8,704]{1,0:T(8,128)S(1)}, f32[8,704]{1,0:T(8,128)}, u32[]{:S(2)}) copy-start(f32[8,704]{1,0:T(8,128)} %get-tuple-element.62) | copy-start | bytes 67588
  141.2 40.6 %collective-permute-start.6 = (bf16[24,16,704]{2,1,0:T(8,128)(2,1)}, bf16[24,16,704]{2,1,0:T(8,128)(2,1)}, u32[]{:S(2)}, u32[]{:S(2)}) collective-permute-start(bf16[24,16,704]{2,1,0:T(8,128)(2,1)} %bitcast.67), channel_id=1, source_target_pairs={{0,1},{1,2},{2,3},{3,4},{4,5},{5,6},{6,7},{8,9},{9,10},{10,11},{11... | collective-permute-start | bytes 1622024 | tf_op jit(solution)/shard_map/ppermute | solution.py:663
  145.3 36.5 %collective-permute-start.7 = (bf16[24,16,704]{2,1,0:T(8,128)(2,1)}, bf16[24,16,704]{2,1,0:T(8,128)(2,1)}, u32[]{:S(2)}, u32[]{:S(2)}) collective-permute-start(bf16[24,16,704]{2,1,0:T(8,128)(2,1)} %bitcast.66), channel_id=1, source_target_pairs={{1,0},{2,1},{3,2},{4,3},{5,4},{6,5},{7,6},{9,8},{10,9},{11,10},{12... | collective-permute-start | bytes 1622024 | tf_op jit(solution)/shard_map/ppermute | solution.py:663
  155.3 16.2 %copy-start.2 = (bf16[1408,704]{1,0:T(8,128)(2,1)S(1)}, bf16[1408,704]{1,0:T(8,128)(2,1)}, u32[]{:S(2)}) copy-start(bf16[1408,704]{1,0:T(8,128)(2,1)} %get-tuple-element.59) | copy-start | bytes 5947396
  175.5 34.3 %all-to-all-start.4 = ((bf16[64,24,768]{2,1,0:T(8,128)(2,1)}), bf16[64,24,768]{2,1,0:T(8,128)(2,1)S(1)}, u32[]{:S(2)}, u32[]{:S(2)}) async-start(bf16[64,24,768]{2,1,0:T(8,128)(2,1)} %chip_sum.3), calls=%async_computation.4 | async-start | bytes 4718592 | tf_op jit(solution)/shard_map/all_to_all | solution.py:650
  210.1 12.1 %copy-start.11 = (f32[4,128,704]{2,1,0:T(8,128)S(1)}, f32[4,128,704]{2,1,0:T(8,128)}, u32[]{:S(2)}) copy-start(f32[4,128,704]{2,1,0:T(8,128)} %conv_back.1) | copy-start | bytes 4325380
  210.3 4.7 %collective-permute-start.10 = (f32[4,704]{1,0:T(4,128)S(1)}, f32[4,704]{1,0:T(4,128)S(1)}, u32[]{:S(2)}, u32[]{:S(2)}) collective-permute-start(f32[4,704]{1,0:T(4,128)S(1)} %pad_maximum_fusion.6), channel_id=1, source_target_pairs={{0,72},{1,73},{2,74},{3,75},{4,76},{5,77},{6,78},{7,79},{8,64},{9,... | collective-permute-start | bytes 33800 | tf_op jit(solution)/shard_map/ppermute | solution.py:620
  210.4 4.6 %collective-permute-start.8 = (f32[4,704]{1,0:T(4,128)S(1)}, f32[4,704]{1,0:T(4,128)S(1)}, u32[]{:S(2)}, u32[]{:S(2)}) collective-permute-start(f32[4,704]{1,0:T(4,128)S(1)} %pad_maximum_fusion.6), channel_id=1, source_target_pairs={{0,8},{1,9},{2,10},{3,11},{4,12},{5,13},{6,14},{7,15},{8,0},{9,1},... | collective-permute-start | bytes 33800 | tf_op jit(solution)/shard_map/ppermute | solution.py:616
  212.3 5.2 %collective-permute-start.9 = (f32[4,704]{1,0:T(4,128)S(1)}, f32[4,704]{1,0:T(4,128)S(1)}, u32[]{:S(2)}, u32[]{:S(2)}) collective-permute-start(f32[4,704]{1,0:T(4,128)S(1)} %pad_maximum_fusion.6), channel_id=1, source_target_pairs={{0,64},{1,65},{2,66},{3,67},{4,68},{5,69},{6,70},{7,71},{8,72},{9,... | collective-permute-start | bytes 33800 | tf_op jit(solution)/shard_map/ppermute | solution.py:620
  218.6 14.3 %all-to-all-start.5 = ((bf16[8,26,1408]{2,1,0:T(8,128)(2,1)}), bf16[8,26,1408]{2,1,0:T(8,128)(2,1)S(1)}, u32[]{:S(2)}, u32[]{:S(2)}) async-start(bf16[8,26,1408]{2,1,0:T(8,128)(2,1)} %broadcast_in_dim.42), calls=%async_computation.5 | async-start | bytes 1441792 | tf_op jit(solution)/shard_map/all_to_all | solution.py:654
  (6 other events, 7.9 us)

commit v7 on v6

--- a/solution.py
+++ b/solution.py
@@ -250,14 +250,17 @@
         nt = (((1,), (1,)), ((), ()))
         gm = lax.dot_general(weighted[...], w[...], nt, preferred_element_type=F32)
         gm_ref[0] = gm
-        sums[pl.ds(h, 1), :] = jnp.sum(sq[0], axis=0, keepdims=True)
-        sums[pl.ds(h + 4, 1), :] = jnp.sum(gm * act_ref[0], axis=0, keepdims=True)
+        square = jnp.sum(sq[0], axis=0, keepdims=True)
+        dot = jnp.sum(gm * act_ref[0], axis=0, keepdims=True)
+        for d in range(sums.shape[0]):
+            sums[d, pl.ds(h, 1), :] = square
+            sums[d, pl.ds(h + 4, 1), :] = dot
         gm_sum[pl.ds(h, 1), :] = jnp.sum(gm, axis=0, keepdims=True)
 
     with_rows(h, w_mine, w_other, step)
 
 
-def mixed_grad(weighted, w_down, act, sq):
+def mixed_grad(weighted, w_down, act, sq, members):
     pixels, width = weighted.shape
     block = w_down[0].shape[0] // 2
     cols = pl.BlockSpec((1, pixels, block), lambda h: (h, 0, 0))
@@ -270,10 +273,10 @@
             cols,
             pl.BlockSpec((1, 8, block), lambda h: (h, 0, 0)),
         ],
-        out_specs=[cols, whole_block(8, block), whole_block(4, block)],
+        out_specs=[cols, whole_block(members, 8, block), whole_block(4, block)],
         out_shape=[
             jax.ShapeDtypeStruct((4, pixels, block), F32),
-            jax.ShapeDtypeStruct((8, block), F32),
+            jax.ShapeDtypeStruct((members, 8, block), F32),
             jax.ShapeDtypeStruct((4, block), F32),
         ],
         compiler_params=params("arbitrary"),
@@ -317,7 +320,7 @@
     r, t = ratio_of(crop[:4], crop[4:], gamma[...])
     ratio[...] = r
     twice[...] = t
-    parts[0] = local[4:, :] * r
+    parts[0] = local[0, 4:, :] * r
     parts[1] = gm_sum[...]
     down_rows_of(other, 2, act, weighted, gamma, ratio, beta)
 
@@ -620,8 +623,12 @@
     return lax.ppermute(value, BOTH, moved(lambda y, z, c, x, low: (1 - y, z, 1 - c if cross else c, x, low)))
 
 
-def gather_mine(shard):
-    return lax.all_to_all(jnp.broadcast_to(shard, (8,) + shard.shape), BOTH, 0, 0, axis_index_groups=OWNERS)
+def copies(shard):
+    return jnp.broadcast_to(shard, (8,) + shard.shape)
+
+
+def gather_mine(shards):
+    return lax.all_to_all(shards, BOTH, 0, 0, axis_index_groups=OWNERS)
 
 
 def with_other(mine):
@@ -677,8 +684,9 @@
     falling = [(j, i) for i, j in rising]
     above = shift(feat[rows - 3 :], rising)
     below = shift(feat[:3], falling)
-    part = conv_own(feat, kernel)
-    w_up_mine = gather_mine(w_up)
+    w_up_mine = gather_mine(copies(w_up))
+    inner, w_down = lax.optimization_barrier((feat, copies(w_down)))
+    part = conv_own(inner, kernel)
     w_up_mine, w_down, part, above, below = lax.optimization_barrier((w_up_mine, w_down, part, above, below))
     w_down_mine = gather_mine(w_down)
     gamma, beta = local_order(grn_gamma, owned), local_order(grn_beta, owned)
@@ -693,8 +701,8 @@
     act, slope, sq = up_project(normed, w_up_all)
     w_down_mine, sq = lax.optimization_barrier((w_down_mine, sq))
     w_down_all = with_other(w_down_mine)
-    gm, local, gm_sum = mixed_grad(weighted, w_down_all, act, sq)
-    sums = everyone(local, "space")
+    gm, local, gm_sum = mixed_grad(weighted, w_down_all, act, sq, space)
+    sums = exchange(local, "space")
     down_other_term, ratio, twice, parts = down_other(act, weighted, sums, local, gm_sum, gamma, beta)
     by_owner = lambda rows: rows.reshape(8, owned, width)
     came = to_other_core(by_owner(down_other_term))

time: 239 us -> 235 us (0.983)
    unnamed x45 -> x47, local copies, waits for them, and re-layouts: 9.24 us -> 10.4 us
  transfers between devices with their start and end apart: 17 -> 17, of which waited for: 10 -> 10; matrix products, arithmetic and copies ran while one was open for 5% -> 5% of each run, Pallas kernels for 25% -> 26%
where the time goes in v7:
time: 235 us; the launch traced here: 233 us
  waiting for transfers between devices  82.4 us (35%)
  Pallas kernels  72.1 us (31%)
  starting transfers between devices  50.4 us (21%)
  local copies, waits for them, and re-layouts  22.2 us (9%)
  other arithmetic  5.13 us (2%)
    all_to_all x2, waiting for transfers between devices, sum_blocks(): lax.all_to_all(blocks, BOTH, 0, 0, axis_index_groups=CORES).astype(F32)  32.8 us
    ppermute x4, waiting for transfers between devices, shift(): return lax.ppermute(flat, 'space', pairs).reshape(rows.shape)  17.1 us
    all_to_all x2, starting transfers between devices, gather_mine(): return lax.all_to_all(shards, BOTH, 0, 0, axis_index_groups=OWNERS)  17 us
    pallas_call x1, Pallas kernels, hidden_grad(): pl.pallas_call(hidden_kernel, grid=(4,), in_specs=[cols, cols, cols, mine...  16.5 us
    all_to_all x2, waiting for transfers between devices, exchange(): return lax.all_to_all(value, axis, 0, 0)  15.9 us
    all_to_all x2, starting transfers between devices, sum_blocks(): lax.all_to_all(blocks, BOTH, 0, 0, axis_index_groups=CORES).astype(F32)  12.9 us
    unnamed x47, local copies, waits for them, and re-layouts  10.4 us
    pallas_call x1, Pallas kernels, up_project(): pl.pallas_call(up_kernel, grid=(4,), in_specs=[whole_block(pixels, width)...  9.66 us
  transfers between devices with their start and end apart: 17, of which 10 were waited for; matrix products, arithmetic and copies ran while one was open for 5% of the time, Pallas kernels for 26%

profile of v7, /device:TPU:0, one launch (start us, length us, event | category | flops | bytes accessed | tf_op | source)
XLA Modules:
  0.0 233.4 jit_solution(14809257387812499926)
XLA Ops:
  0.6 2.4 %broadcast_in_dim.31 = bf16[8,176,704]{2,1,0:T(8,128)(2,1)} broadcast(bf16[176,704]{1,0:T(8,128)(2,1)} %param.13), dimensions={1,2} | broadcast | bytes 2230272 | tf_op jit(solution)/shard_map/broadcast_in_dim | solution.py:627
  3.0 8.0 %all-to-all-start = ((bf16[8,176,704]{2,1,0:T(8,128)(2,1)}), bf16[8,176,704]{2,1,0:T(8,128)(2,1)}, u32[]{:S(2)}, u32[]{:S(2)}) async-start(bf16[8,176,704]{2,1,0:T(8,128)(2,1)} %broadcast_in_dim.31), calls=%async_computation | async-start | bytes 4325376 | tf_op jit(solution)/shard_map/all_to_all | solution.py:631
  11.4 2.2 collective-permute-start
  16.4 5.0 %conv_own.1.part = f32[4,128,704]{2,1,0:T(8,128)} custom-call(bf16[4,128,704]{2,1,0:T(8,128)(2,1)} %bitcast.46, f32[7,7,704]{2,1,0:T(8,128)} %k_ref.5), custom_call_target="tpu_custom_call" | custom-call | flops 2000000000 | tf_op jit(solution)/shard_map/conv_own/pallas_call | solution.py:107
  21.4 17.1 %collective-permute-done = bf16[24,16,704]{2,1,0:T(8,128)(2,1)S(1)} collective-permute-done((bf16[24,16,704]{2,1,0:T(8,128)(2,1)S(1)}, bf16[24,16,704]{2,1,0:T(8,128)(2,1)S(1)}, u32[]{:S(2)}, u32[]{:S(2)}) %collective-permute-start) | collective-permute-done | bytes 540704 | tf_op jit(solution)/shard_map/ppermute | solution.py:670
  39.6 9.0 %all-to-all-start.1 = ((bf16[8,176,704]{2,1,0:T(8,128)(2,1)}), bf16[8,176,704]{2,1,0:T(8,128)(2,1)}, u32[]{:S(2)}, u32[]{:S(2)}) async-start(bf16[8,176,704]{2,1,0:T(8,128)(2,1)} %broadcast_in_dim.32), calls=%async_computation.1 | async-start | bytes 4325376 | tf_op jit(solution)/shard_map/all_to_all | solution.py:631
  49.2 7.0 %conv_norm.1 = (bf16[512,704]{1,0:T(8,128)(2,1)}, f32[512,704]{1,0:T(8,128)}, f32[512,128]{1,0:T(8,128)}) custom-call(f32[4,128,704]{2,1,0:T(8,128)} %conv_own.1.part, bf16[3,128,704]{2,1,0:T(8,128)(2,1)} %bitcast.56, bf16[3,128,704]{2,1,0:T(8,128)(2,1)} %bitcast.58, f32[7,7,704]{2,1,0:T(8,128)} %k_ref.5, f32[1,704]{1,0:T(1,128)} %reshape.181.gain), custom_call_target="tpu_custom_call" | custom-call | flops 2800000000 | tf_op jit(solution)/shard_map/conv_norm/pallas_call | solution.py:174
  57.5 9.7 %up_project.1 = (f32[4,512,704]{2,1,0:T(8,128)}, f32[4,512,704]{2,1,0:T(8,128)}, f32[4,8,704]{2,1,0:T(8,128)}) custom-call(bf16[512,704]{1,0:T(8,128)(2,1)} %get-tuple-element.46.normed, bf16[1408,704]{1,0:T(8,128)(2,1)} %bitcast.5.w_mine, bf16[1408,704]{1,0:T(8,128)(2,1)} %bitcast.49), custom_call_target="tpu_custom_call" | custom-call | flops 3600000000 | tf_op jit(solution)/shard_map/up_project/pallas_call | solution.py:234
  67.2 8.0 %all-to-all-done.1 = bf16[8,176,704]{2,1,0:T(8,128)(2,1)} async-done(((bf16[8,176,704]{2,1,0:T(8,128)(2,1)}), bf16[8,176,704]{2,1,0:T(8,128)(2,1)}, u32[]{:S(2)}, u32[]{:S(2)}) %all-to-all-start.1) | async-done | bytes 1982496 | tf_op jit(solution)/shard_map/all_to_all | solution.py:631
  77.3 2.5 %collective-permute-done.3 = bf16[8,176,704]{2,1,0:T(8,128)(2,1)} collective-permute-done((bf16[8,176,704]{2,1,0:T(8,128)(2,1)}, bf16[8,176,704]{2,1,0:T(8,128)(2,1)}, u32[]{:S(2)}, u32[]{:S(2)}) %collective-permute-start.3) | collective-permute-done | bytes 1982496 | tf_op jit(solution)/shard_map/ppermute | solution.py:619
  79.8 8.7 %mixed_grad.1 = (f32[4,512,704]{2,1,0:T(8,128)}, f32[8,8,704]{2,1,0:T(8,128)}, f32[4,704]{1,0:T(4,128)}) custom-call(bf16[512,704]{1,0:T(8,128)(2,1)} %fusion.weighted, bf16[1408,704]{1,0:T(8,128)(2,1)} %bitcast.10.w_mine, bf16[1408,704]{1,0:T(8,128)(2,1)} %bitcast.11.w_other, f32[4,512,704]{2,1,0:T(8,128)} %get-tuple-element.48.act_ref.act, ...), custom_call_target="tpu_custom_call" | custom-call | flops 3200000000 | tf_op jit(solution)/shard_map/mixed_grad/pallas_call | solution.py:267
  88.5 4.3 %all-to-all-start.2 = ((f32[8,8,704]{2,1,0:T(8,128)}), f32[8,8,704]{2,1,0:T(8,128)S(1)}, u32[]{:S(2)}, u32[]{:S(2)}) async-start(f32[8,8,704]{2,1,0:T(8,128)} %get-tuple-element.55.local), calls=%async_computation.2 | async-start | bytes 393216 | tf_op jit(solution)/shard_map/all_to_all | solution.py:661
  93.0 6.7 %all-to-all-done.2.sums = f32[8,8,704]{2,1,0:T(8,128)S(1)} async-done(((f32[8,8,704]{2,1,0:T(8,128)}), f32[8,8,704]{2,1,0:T(8,128)S(1)}, u32[]{:S(2)}, u32[]{:S(2)}) %all-to-all-start.2) | async-done | bytes 180256 | tf_op jit(solution)/shard_map/all_to_all | solution.py:661
  99.7 2.8 %copy-done = f32[4,512,704]{2,1,0:T(8,128)S(1)} copy-done((f32[4,512,704]{2,1,0:T(8,128)S(1)}, f32[4,512,704]{2,1,0:T(8,128)}, u32[]{:S(2)}) %copy-start) | copy-done | bytes 5767192
  104.1 1.8 down_other.1
  108.3 2.5 %collective-permute-done.4.other = bf16[8,176,704]{2,1,0:T(8,128)(2,1)S(1)} collective-permute-done((bf16[8,176,704]{2,1,0:T(8,128)(2,1)S(1)}, bf16[8,176,704]{2,1,0:T(8,128)(2,1)S(1)}, u32[]{:S(2)}, u32[]{:S(2)}) %collective-permute-start.4) | collective-permute-done | bytes 1982496 | tf_op jit(solution)/shard_map/ppermute | solution.py:619
  110.8 2.0 chip_sum.2
  112.8 7.8 %all-to-all-start.3 = ((bf16[64,22,704]{2,1,0:T(8,128)(2,1)}), bf16[64,22,704]{2,1,0:T(8,128)(2,1)}, u32[]{:S(2)}, u32[]{:S(2)}) async-start(bf16[64,22,704]{2,1,0:T(8,128)(2,1)} %chip_sum.2), calls=%async_computation.3 | async-start | bytes 4718592 | tf_op jit(solution)/shard_map/all_to_all | solution.py:657
  120.6 16.5 %hidden_grad.1 = (bf16[1408,704]{1,0:T(8,128)(2,1)}, bf16[1408,704]{1,0:T(8,128)(2,1)}, f32[512,704]{1,0:T(8,128)}, bf16[384,704]{1,0:T(8,128)(2,1)}, bf16[384,704]{1,0:T(8,128)(2,1)}, /*index=5*/f32[8,704]{1,0:T(8,128)}) custom-call(f32[4,512,704]{2,1,0:T(8,128)} %get-tuple-element.48.act_ref.act, f32[4,512,704]{2,1,0:T(8,128)} %get-tuple-element.49.slope, ...), custom_call_target="tpu_custom_call" | custom-call | flops 5600000000 | tf_op jit(solution)/shard_map/hidden_grad/pallas_call | solution.py:427
  137.5 4.0 %collective-permute-start.6 = (bf16[24,16,704]{2,1,0:T(8,128)(2,1)}, bf16[24,16,704]{2,1,0:T(8,128)(2,1)}, u32[]{:S(2)}, u32[]{:S(2)}) collective-permute-start(bf16[24,16,704]{2,1,0:T(8,128)(2,1)} %bitcast.67), channel_id=1, source_target_pairs={{0,1},{1,2},{2,3},{3,4},{4,5},{5,6},{6,7},{8,9},{9,10},{10,11},{11... | collective-permute-start | bytes 1622024 | tf_op jit(solution)/shard_map/ppermute | solution.py:670
  142.8 7.8 %taps_grad.1 = f32[7,7,704]{2,1,0:T(8,128)} custom-call(bf16[4,128,704]{2,1,0:T(8,128)(2,1)} %bitcast.47, bf16[3,128,704]{2,1,0:T(8,128)(2,1)} %bitcast.57, bf16[3,128,704]{2,1,0:T(8,128)(2,1)} %bitcast.59, f32[4,128,704]{2,1,0:T(8,128)} %bitcast.51), custom_call_target="tpu_custom_call" | custom-call | flops 400000000 | tf_op jit(solution)/shard_map/taps_grad/pallas_call | solution.py:478
  151.9 13.7 %all-to-all-done.3 = bf16[64,22,704]{2,1,0:T(8,128)(2,1)} async-done(((bf16[64,22,704]{2,1,0:T(8,128)(2,1)}), bf16[64,22,704]{2,1,0:T(8,128)(2,1)}, u32[]{:S(2)}, u32[]{:S(2)}) %all-to-all-start.3) | async-done | bytes 1982496 | tf_op jit(solution)/shard_map/all_to_all | solution.py:657
  165.6 2.1 convert_reduce_fusion.1
  167.7 4.0 %chip_sum.3 = bf16[64,24,768]{2,1,0:T(8,128)(2,1)} custom-call(bf16[8,176,704]{2,1,0:T(8,128)(2,1)S(1)} %bitcast.44, bf16[8,176,704]{2,1,0:T(8,128)(2,1)} %collective-permute-done.5.other, f32[16,2,704]{2,1,0:T(2,128)S(1)} %get-tuple-element.107.vector, f32[16,24,64]{2,1,0:T(8,128)S(1)} %pad.9.edge), custom_call_target="tpu_custom_call" | custom-call | flops 120000000 | tf_op jit(solution)/shard_map/chip_sum/pallas_call | solution.py:577
  171.7 5.1 %all-to-all-start.4 = ((bf16[64,24,768]{2,1,0:T(8,128)(2,1)}), bf16[64,24,768]{2,1,0:T(8,128)(2,1)S(1)}, u32[]{:S(2)}, u32[]{:S(2)}) async-start(bf16[64,24,768]{2,1,0:T(8,128)(2,1)} %chip_sum.3), calls=%async_computation.4 | async-start | bytes 4718592 | tf_op jit(solution)/shard_map/all_to_all | solution.py:657
  178.8 8.0 %conv_back.1 = f32[4,128,704]{2,1,0:T(8,128)} custom-call(f32[4,128,704]{2,1,0:T(8,128)} %bitcast.52, bf16[3,128,704]{2,1,0:T(8,128)(2,1)} %bitcast.23.above, bf16[3,128,704]{2,1,0:T(8,128)(2,1)} %bitcast.25.below, f32[7,7,704]{2,1,0:T(8,128)} %k_ref.5, bf16[4,128,704]{2,1,0:T(8,128)(2,1)} %bitcast.54, f32[4,128,128]{2,1,0:T(8,128)} %broadcast_in_dim.36.weight), custom_call_target="tpu_custom_call" | custom-call | flops 24000000000 | tf_op jit(solution)/shard_map/conv_back/pallas_call | solution.py:527
  186.9 19.1 %all-to-all-done.4 = bf16[64,24,768]{2,1,0:T(8,128)(2,1)S(1)} async-done(((bf16[64,24,768]{2,1,0:T(8,128)(2,1)}), bf16[64,24,768]{2,1,0:T(8,128)(2,1)S(1)}, u32[]{:S(2)}, u32[]{:S(2)}) %all-to-all-start.4) | async-done | bytes 2359328 | tf_op jit(solution)/shard_map/all_to_all | solution.py:657
  206.6 1.9 collective-permute-start.8
  208.5 1.7 collective-permute-start.9
  211.2 2.5 %collective-permute-done.9 = f32[4,704]{1,0:T(4,128)S(1)} collective-permute-done((f32[4,704]{1,0:T(4,128)S(1)}, f32[4,704]{1,0:T(4,128)S(1)}, u32[]{:S(2)}, u32[]{:S(2)}) %collective-permute-start.9) | collective-permute-done | bytes 11296 | tf_op jit(solution)/shard_map/ppermute | solution.py:623
  214.8 3.5 %all-to-all-start.5 = ((bf16[8,26,1408]{2,1,0:T(8,128)(2,1)}), bf16[8,26,1408]{2,1,0:T(8,128)(2,1)S(1)}, u32[]{:S(2)}, u32[]{:S(2)}) async-start(bf16[8,26,1408]{2,1,0:T(8,128)(2,1)} %broadcast_in_dim.38), calls=%async_computation.5 | async-start | bytes 1441792 | tf_op jit(solution)/shard_map/all_to_all | solution.py:661
  219.9 9.2 %all-to-all-done.5 = bf16[8,26,1408]{2,1,0:T(8,128)(2,1)S(1)} async-done(((bf16[8,26,1408]{2,1,0:T(8,128)(2,1)}), bf16[8,26,1408]{2,1,0:T(8,128)(2,1)S(1)}, u32[]{:S(2)}, u32[]{:S(2)}) %all-to-all-start.5) | async-done | bytes 585760 | tf_op jit(solution)/shard_map/all_to_all | solution.py:661
  (116 shorter events, 25.6 us)
Async XLA Ops:
  3.0 8.0 %copy-start.12 = (bf16[1,4,128,704]{2,3,1,0:T(8,128)(2,1)S(1)}, bf16[1,4,128,704]{2,3,1,0:T(8,128)(2,1)}, u32[]{:S(2)}) copy-start(bf16[1,4,128,704]{2,3,1,0:T(8,128)(2,1)} %param.10) | copy-start | bytes 2162692
  3.0 35.5 %all-to-all-start = ((bf16[8,176,704]{2,1,0:T(8,128)(2,1)}), bf16[8,176,704]{2,1,0:T(8,128)(2,1)}, u32[]{:S(2)}, u32[]{:S(2)}) async-start(bf16[8,176,704]{2,1,0:T(8,128)(2,1)} %broadcast_in_dim.31), calls=%async_computation | async-start | bytes 4325376 | tf_op jit(solution)/shard_map/all_to_all | solution.py:631
  11.3 5.1 %copy-start.8 = (bf16[1,4,128,704]{3,2,1,0:T(8,128)(2,1)}, bf16[1,4,128,704]{3,2,1,0:T(8,128)(2,1)S(1)}, u32[]{:S(2)}) copy-start(bf16[1,4,128,704]{3,2,1,0:T(8,128)(2,1)S(1)} %copy.39) | copy-start | bytes 2162692
  11.3 3.6 %copy-start.15 = (bf16[176,704]{1,0:T(8,128)(2,1)S(1)}, bf16[176,704]{1,0:T(8,128)(2,1)}, u32[]{:S(2)}) copy-start(bf16[176,704]{1,0:T(8,128)(2,1)} %param.16) | copy-start | bytes 743428
  11.4 27.1 %collective-permute-start = (bf16[24,16,704]{2,1,0:T(8,128)(2,1)S(1)}, bf16[24,16,704]{2,1,0:T(8,128)(2,1)S(1)}, u32[]{:S(2)}, u32[]{:S(2)}) collective-permute-start(bf16[24,16,704]{2,1,0:T(8,128)(2,1)S(1)} %bitcast.61), channel_id=1, source_target_pairs={{0,1},{1,2},{2,3},{3,4},{4,5},{5,6},{6,7},{8,9},{9,10},{10,11},{11... | collective-permute-start | bytes 1622024 | tf_op jit(solution)/shard_map/ppermute | solution.py:670
  13.6 24.9 %collective-permute-start.1 = (bf16[24,16,704]{2,1,0:T(8,128)(2,1)S(1)}, bf16[24,16,704]{2,1,0:T(8,128)(2,1)S(1)}, u32[]{:S(2)}, u32[]{:S(2)}) collective-permute-start(bf16[24,16,704]{2,1,0:T(8,128)(2,1)S(1)} %bitcast.60), channel_id=1, source_target_pairs={{1,0},{2,1},{3,2},{4,3},{5,4},{6,5},{7,6},{9,8},{10,9},{11,10},{12... | collective-permute-start | bytes 1622024 | tf_op jit(solution)/shard_map/ppermute | solution.py:670
  38.5 10.0 %copy-start.19 = (f32[704]{0:T(1024)S(1)}, f32[704]{0:T(1024)}, u32[]{:S(2)}) copy-start(f32[704]{0:T(1024)} %param.12) | copy-start | bytes 8452
  38.6 17.6 %collective-permute-start.2 = (bf16[8,176,704]{2,1,0:T(8,128)(2,1)}, bf16[8,176,704]{2,1,0:T(8,128)(2,1)S(1)}, u32[]{:S(2)}, u32[]{:S(2)}) collective-permute-start(bf16[8,176,704]{2,1,0:T(8,128)(2,1)} %all-to-all-done), channel_id=1, source_target_pairs={{0,8},{1,9},{2,10},{3,11},{4,12},{5,13},{6,14},{7,15},{8,0},{9,1},... | collective-permute-start | bytes 5947400 | tf_op jit(solution)/shard_map/ppermute | solution.py:619
  39.6 35.6 %all-to-all-start.1 = ((bf16[8,176,704]{2,1,0:T(8,128)(2,1)}), bf16[8,176,704]{2,1,0:T(8,128)(2,1)}, u32[]{:S(2)}, u32[]{:S(2)}) async-start(bf16[8,176,704]{2,1,0:T(8,128)(2,1)} %broadcast_in_dim.32), calls=%async_computation.1 | async-start | bytes 4325376 | tf_op jit(solution)/shard_map/all_to_all | solution.py:631
  57.5 17.8 %copy-start.9 = (bf16[1,4,128,704]{2,3,1,0:T(8,128)(2,1)S(1)}, bf16[1,4,128,704]{2,3,1,0:T(8,128)(2,1)}, u32[]{:S(2)}) copy-start(bf16[1,4,128,704]{2,3,1,0:T(8,128)(2,1)} %param.17) | copy-start | bytes 2162692
  67.1 8.4 %copy-start.17 = (f32[2816]{0:T(1024)S(1)}, f32[2816]{0:T(1024)}, u32[]{:S(2)}) copy-start(f32[2816]{0:T(1024)} %param.14) | copy-start | bytes 33796
  67.1 8.5 %copy-start.18 = (f32[2816]{0:T(1024)S(1)}, f32[2816]{0:T(1024)}, u32[]{:S(2)}) copy-start(f32[2816]{0:T(1024)} %param.15) | copy-start | bytes 33796
  67.2 8.9 %copy-start.20 = (s32[1,4,128]{2,1,0:T(4,128)S(1)}, s32[1,4,128]{2,1,0:T(4,128)}, u32[]{:S(2)}) copy-start(s32[1,4,128]{2,1,0:T(4,128)} %param.18) | copy-start | bytes 6148
  67.2 8.8 %copy-start.21 = (f32[150]{0:T(256)S(1)}, f32[150]{0:T(256)}, u32[]{:S(2)}) copy-start(f32[150]{0:T(256)} %param.19) | copy-start | bytes 1804
  75.2 4.6 %collective-permute-start.3 = (bf16[8,176,704]{2,1,0:T(8,128)(2,1)}, bf16[8,176,704]{2,1,0:T(8,128)(2,1)}, u32[]{:S(2)}, u32[]{:S(2)}) collective-permute-start(bf16[8,176,704]{2,1,0:T(8,128)(2,1)} %all-to-all-done.1), channel_id=1, source_target_pairs={{0,8},{1,9},{2,10},{3,11},{4,12},{5,13},{6,14},{7,15},{8,0},{9,1},... | collective-permute-start | bytes 5947400 | tf_op jit(solution)/shard_map/ppermute | solution.py:619
  79.8 19.9 %copy-start.1 = (bf16[512,704]{1,0:T(8,128)(2,1)S(1)}, bf16[512,704]{1,0:T(8,128)(2,1)}, u32[]{:S(2)}) copy-start(bf16[512,704]{1,0:T(8,128)(2,1)} %fusion.weighted) | copy-start | bytes 2162692
  88.5 11.2 %all-to-all-start.2 = ((f32[8,8,704]{2,1,0:T(8,128)}), f32[8,8,704]{2,1,0:T(8,128)S(1)}, u32[]{:S(2)}, u32[]{:S(2)}) async-start(f32[8,8,704]{2,1,0:T(8,128)} %get-tuple-element.55.local), calls=%async_computation.2 | async-start | bytes 393216 | tf_op jit(solution)/shard_map/all_to_all | solution.py:661
  92.8 13.7 %copy-start.4 = (f32[4,704]{1,0:T(4,128)}, f32[4,704]{1,0:T(4,128)S(1)}, u32[]{:S(2)}) copy-start(f32[4,704]{1,0:T(4,128)S(1)} %pad_maximum_fusion.4.gamma) | copy-start | bytes 33796
  99.7 2.8 %copy-start = (f32[4,512,704]{2,1,0:T(8,128)S(1)}, f32[4,512,704]{2,1,0:T(8,128)}, u32[]{:S(2)}) copy-start(f32[4,512,704]{2,1,0:T(8,128)} %get-tuple-element.48.act_ref.act) | copy-start | bytes 17301508
  106.6 4.3 %collective-permute-start.4 = (bf16[8,176,704]{2,1,0:T(8,128)(2,1)S(1)}, bf16[8,176,704]{2,1,0:T(8,128)(2,1)S(1)}, u32[]{:S(2)}, u32[]{:S(2)}) collective-permute-start(bf16[8,176,704]{2,1,0:T(8,128)(2,1)S(1)} %bitcast.45), channel_id=1, source_target_pairs={{0,8},{1,9},{2,10},{3,11},{4,12},{5,13},{6,14},{7,15},{8,0},{9,1},... | collective-permute-start | bytes 5947400 | tf_op jit(solution)/shard_map/ppermute | solution.py:619
  112.8 52.8 %all-to-all-start.3 = ((bf16[64,22,704]{2,1,0:T(8,128)(2,1)}), bf16[64,22,704]{2,1,0:T(8,128)(2,1)}, u32[]{:S(2)}, u32[]{:S(2)}) async-start(bf16[64,22,704]{2,1,0:T(8,128)(2,1)} %chip_sum.2), calls=%async_computation.3 | async-start | bytes 4718592 | tf_op jit(solution)/shard_map/all_to_all | solution.py:657
  137.1 30.6 %collective-permute-start.5 = (bf16[8,176,704]{2,1,0:T(8,128)(2,1)}, bf16[8,176,704]{2,1,0:T(8,128)(2,1)}, u32[]{:S(2)}, u32[]{:S(2)}) collective-permute-start(bf16[8,176,704]{2,1,0:T(8,128)(2,1)} %bitcast.65), channel_id=1, source_target_pairs={{0,8},{1,9},{2,10},{3,11},{4,12},{5,13},{6,14},{7,15},{8,0},{9,1},... | collective-permute-start | bytes 5947400 | tf_op jit(solution)/shard_map/ppermute | solution.py:619
  137.3 14.2 %copy-start.16 = (f32[8,704]{1,0:T(8,128)S(1)}, f32[8,704]{1,0:T(8,128)}, u32[]{:S(2)}) copy-start(f32[8,704]{1,0:T(8,128)} %get-tuple-element.66) | copy-start | bytes 67588
  137.5 40.5 %collective-permute-start.6 = (bf16[24,16,704]{2,1,0:T(8,128)(2,1)}, bf16[24,16,704]{2,1,0:T(8,128)(2,1)}, u32[]{:S(2)}, u32[]{:S(2)}) collective-permute-start(bf16[24,16,704]{2,1,0:T(8,128)(2,1)} %bitcast.67), channel_id=1, source_target_pairs={{0,1},{1,2},{2,3},{3,4},{4,5},{5,6},{6,7},{8,9},{9,10},{10,11},{11... | collective-permute-start | bytes 1622024 | tf_op jit(solution)/shard_map/ppermute | solution.py:670
  141.5 36.5 %collective-permute-start.7 = (bf16[24,16,704]{2,1,0:T(8,128)(2,1)}, bf16[24,16,704]{2,1,0:T(8,128)(2,1)}, u32[]{:S(2)}, u32[]{:S(2)}) collective-permute-start(bf16[24,16,704]{2,1,0:T(8,128)(2,1)} %bitcast.66), channel_id=1, source_target_pairs={{1,0},{2,1},{3,2},{4,3},{5,4},{6,5},{7,6},{9,8},{10,9},{11,10},{12... | collective-permute-start | bytes 1622024 | tf_op jit(solution)/shard_map/ppermute | solution.py:670
  151.5 16.2 %copy-start.2 = (bf16[1408,704]{1,0:T(8,128)(2,1)S(1)}, bf16[1408,704]{1,0:T(8,128)(2,1)}, u32[]{:S(2)}) copy-start(bf16[1408,704]{1,0:T(8,128)(2,1)} %get-tuple-element.63) | copy-start | bytes 5947396
  171.7 34.3 %all-to-all-start.4 = ((bf16[64,24,768]{2,1,0:T(8,128)(2,1)}), bf16[64,24,768]{2,1,0:T(8,128)(2,1)S(1)}, u32[]{:S(2)}, u32[]{:S(2)}) async-start(bf16[64,24,768]{2,1,0:T(8,128)(2,1)} %chip_sum.3), calls=%async_computation.4 | async-start | bytes 4718592 | tf_op jit(solution)/shard_map/all_to_all | solution.py:657
  206.3 12.0 %copy-start.11 = (f32[4,128,704]{2,1,0:T(8,128)S(1)}, f32[4,128,704]{2,1,0:T(8,128)}, u32[]{:S(2)}) copy-start(f32[4,128,704]{2,1,0:T(8,128)} %conv_back.1) | copy-start | bytes 4325380
  206.5 4.7 %collective-permute-start.10 = (f32[4,704]{1,0:T(4,128)S(1)}, f32[4,704]{1,0:T(4,128)S(1)}, u32[]{:S(2)}, u32[]{:S(2)}) collective-permute-start(f32[4,704]{1,0:T(4,128)S(1)} %pad_maximum_fusion.6), channel_id=1, source_target_pairs={{0,72},{1,73},{2,74},{3,75},{4,76},{5,77},{6,78},{7,79},{8,64},{9,... | collective-permute-start | bytes 33800 | tf_op jit(solution)/shard_map/ppermute | solution.py:623
  206.6 4.6 %collective-permute-start.8 = (f32[4,704]{1,0:T(4,128)S(1)}, f32[4,704]{1,0:T(4,128)S(1)}, u32[]{:S(2)}, u32[]{:S(2)}) collective-permute-start(f32[4,704]{1,0:T(4,128)S(1)} %pad_maximum_fusion.6), channel_id=1, source_target_pairs={{0,8},{1,9},{2,10},{3,11},{4,12},{5,13},{6,14},{7,15},{8,0},{9,1},... | collective-permute-start | bytes 33800 | tf_op jit(solution)/shard_map/ppermute | solution.py:619
  208.5 5.2 %collective-permute-start.9 = (f32[4,704]{1,0:T(4,128)S(1)}, f32[4,704]{1,0:T(4,128)S(1)}, u32[]{:S(2)}, u32[]{:S(2)}) collective-permute-start(f32[4,704]{1,0:T(4,128)S(1)} %pad_maximum_fusion.6), channel_id=1, source_target_pairs={{0,64},{1,65},{2,66},{3,67},{4,68},{5,69},{6,70},{7,71},{8,72},{9,... | collective-permute-start | bytes 33800 | tf_op jit(solution)/shard_map/ppermute | solution.py:623
  214.8 14.3 %all-to-all-start.5 = ((bf16[8,26,1408]{2,1,0:T(8,128)(2,1)}), bf16[8,26,1408]{2,1,0:T(8,128)(2,1)S(1)}, u32[]{:S(2)}, u32[]{:S(2)}) async-start(bf16[8,26,1408]{2,1,0:T(8,128)(2,1)} %broadcast_in_dim.38), calls=%async_computation.5 | async-start | bytes 1441792 | tf_op jit(solution)/shard_map/all_to_all | solution.py:661
  (7 other events, 7.1 us)

commit v8 on v7

--- a/solution.py
+++ b/solution.py
@@ -619,8 +619,8 @@
     return lax.ppermute(value, BOTH, moved(lambda y, z, c, x, low: (y, z, 1 - c, x, low)))
 
 
-def to_other_half(value, cross):
-    return lax.ppermute(value, BOTH, moved(lambda y, z, c, x, low: (1 - y, z, 1 - c if cross else c, x, low)))
+def to_other_half(value):
+    return lax.ppermute(value, BOTH, moved(lambda y, z, c, x, low: (1 - y, z, c, x, low)))
 
 
 def copies(shard):
@@ -727,7 +727,8 @@
         axis=0,
     )
     lines = vector.shape[0]
-    vector = jnp.pad(vector, ((0, -lines % 64), (0, 0))).reshape(16, 4, width)
+    vector = jnp.pad(vector, ((0, -lines % 64), (0, 0)))
+    vector = (vector + to_other_core(vector)).reshape(16, 4, width)
     piece = owned // space
     lanes = 2 * width // piece
     edge = jnp.pad(vector[:, 2:].reshape(16, piece, lanes), ((0, 0), (0, 2), (0, 0)))
@@ -738,10 +739,9 @@
     up_rows, grad_features = lax.optimization_barrier((up_rows, grad_features))
 
     vector = jnp.concatenate([up_rows[piece:, :width], up_rows[:piece, width:].reshape(2, width)], axis=0)
-    here = vector + to_other_core(vector)
-    there = to_other_half(vector, False) + to_other_half(vector, True)
+    there = to_other_half(vector)
     first = lax.axis_index("dp") < 8
-    vector = jnp.concatenate([jnp.where(first, here, there), jnp.where(first, there, here)], axis=0)
+    vector = jnp.concatenate([jnp.where(first, vector, there), jnp.where(first, there, vector)], axis=0)
     block = jnp.concatenate([up_rows[:piece, :width], down_rows], axis=1)
     block = jnp.concatenate([block, vector.reshape(4, 2 * width)], axis=0)
     block = everyone((scale * block).astype(BF16), "space").astype(F32)

time: 235 us -> 233 us (level)
  waiting for transfers between devices: 82.4 us -> 75.2 us
  starting transfers between devices: 50.4 us -> 56.2 us
    all_to_all x2, waiting for transfers between devices: 32.8 us -> 3.95 us  [sum_blocks(): lax.all_to_all(blocks, BOTH, 0, 0, axis_index_groups=CORES).astype(F32)]
    ppermute x4, waiting for transfers between devices: 17.1 us -> 38.7 us  [shift(): return lax.ppermute(flat, 'space', pairs).reshape(rows.shape)]
    all_to_all x2, starting transfers between devices: 12.9 us -> 19.3 us  [sum_blocks(): lax.all_to_all(blocks, BOTH, 0, 0, axis_index_groups=CORES).astype(F32)]
  transfers between devices with their start and end apart: 17 -> 16, of which waited for: 10 -> 10; matrix products, arithmetic and copies ran while one was open for 5% -> 5% of each run, Pallas kernels for 26% -> 26%
where the time goes in v8:
time: 233 us; the launch traced here: 232 us
  waiting for transfers between devices  75.2 us (32%)
  Pallas kernels  72.1 us (31%)
  starting transfers between devices  56.2 us (24%)
  local copies, waits for them, and re-layouts  22.3 us (10%)
  other arithmetic  5.16 us (2%)
    ppermute x4, waiting for transfers between devices, shift(): return lax.ppermute(flat, 'space', pairs).reshape(rows.shape)  38.7 us
    all_to_all x2, starting transfers between devices, sum_blocks(): lax.all_to_all(blocks, BOTH, 0, 0, axis_index_groups=CORES).astype(F32)  19.3 us
    all_to_all x2, starting transfers between devices, gather_mine(): return lax.all_to_all(shards, BOTH, 0, 0, axis_index_groups=OWNERS)  17 us
    pallas_call x1, Pallas kernels, hidden_grad(): pl.pallas_call(hidden_kernel, grid=(4,), in_specs=[cols, cols, cols, mine...  16.5 us
    all_to_all x2, waiting for transfers between devices, exchange(): return lax.all_to_all(value, axis, 0, 0)  15.3 us
    unnamed x47, local copies, waits for them, and re-layouts  10.4 us
    pallas_call x1, Pallas kernels, up_project(): pl.pallas_call(up_kernel, grid=(4,), in_specs=[whole_block(pixels, width)...  9.65 us
    all_to_all x2, starting transfers between devices, exchange(): return lax.all_to_all(value, axis, 0, 0)  9.15 us
  transfers between devices with their start and end apart: 16, of which 10 were waited for; matrix products, arithmetic and copies ran while one was open for 5% of the time, Pallas kernels for 26%

profile of v8, /device:TPU:0, one launch (start us, length us, event | category | flops | bytes accessed | tf_op | source)
XLA Modules:
  0.0 232.1 jit_solution(320030730380587972)
XLA Ops:
  0.6 2.4 %broadcast_in_dim.31 = bf16[8,176,704]{2,1,0:T(8,128)(2,1)} broadcast(bf16[176,704]{1,0:T(8,128)(2,1)} %param.13), dimensions={1,2} | broadcast | bytes 2230272 | tf_op jit(solution)/shard_map/broadcast_in_dim | solution.py:627
  3.0 8.0 %all-to-all-start = ((bf16[8,176,704]{2,1,0:T(8,128)(2,1)}), bf16[8,176,704]{2,1,0:T(8,128)(2,1)}, u32[]{:S(2)}, u32[]{:S(2)}) async-start(bf16[8,176,704]{2,1,0:T(8,128)(2,1)} %broadcast_in_dim.31), calls=%async_computation | async-start | bytes 4325376 | tf_op jit(solution)/shard_map/all_to_all | solution.py:631
  11.4 2.2 collective-permute-start
  16.4 5.0 %conv_own.1.part = f32[4,128,704]{2,1,0:T(8,128)} custom-call(bf16[4,128,704]{2,1,0:T(8,128)(2,1)} %bitcast.46, f32[7,7,704]{2,1,0:T(8,128)} %k_ref.5), custom_call_target="tpu_custom_call" | custom-call | flops 2000000000 | tf_op jit(solution)/shard_map/conv_own/pallas_call | solution.py:107
  21.4 17.1 %collective-permute-done = bf16[24,16,704]{2,1,0:T(8,128)(2,1)S(1)} collective-permute-done((bf16[24,16,704]{2,1,0:T(8,128)(2,1)S(1)}, bf16[24,16,704]{2,1,0:T(8,128)(2,1)S(1)}, u32[]{:S(2)}, u32[]{:S(2)}) %collective-permute-start) | collective-permute-done | bytes 540704 | tf_op jit(solution)/shard_map/ppermute | solution.py:670
  39.6 9.0 %all-to-all-start.1 = ((bf16[8,176,704]{2,1,0:T(8,128)(2,1)}), bf16[8,176,704]{2,1,0:T(8,128)(2,1)}, u32[]{:S(2)}, u32[]{:S(2)}) async-start(bf16[8,176,704]{2,1,0:T(8,128)(2,1)} %broadcast_in_dim.32), calls=%async_computation.1 | async-start | bytes 4325376 | tf_op jit(solution)/shard_map/all_to_all | solution.py:631
  49.2 7.0 %conv_norm.1 = (bf16[512,704]{1,0:T(8,128)(2,1)}, f32[512,704]{1,0:T(8,128)}, f32[512,128]{1,0:T(8,128)}) custom-call(f32[4,128,704]{2,1,0:T(8,128)} %conv_own.1.part, bf16[3,128,704]{2,1,0:T(8,128)(2,1)} %bitcast.56, bf16[3,128,704]{2,1,0:T(8,128)(2,1)} %bitcast.58, f32[7,7,704]{2,1,0:T(8,128)} %k_ref.5, f32[1,704]{1,0:T(1,128)} %reshape.181.gain), custom_call_target="tpu_custom_call" | custom-call | flops 2800000000 | tf_op jit(solution)/shard_map/conv_norm/pallas_call | solution.py:174
  57.5 9.6 %up_project.1 = (f32[4,512,704]{2,1,0:T(8,128)}, f32[4,512,704]{2,1,0:T(8,128)}, f32[4,8,704]{2,1,0:T(8,128)}) custom-call(bf16[512,704]{1,0:T(8,128)(2,1)} %get-tuple-element.46.normed, bf16[1408,704]{1,0:T(8,128)(2,1)} %bitcast.5.w_mine, bf16[1408,704]{1,0:T(8,128)(2,1)} %bitcast.49), custom_call_target="tpu_custom_call" | custom-call | flops 3600000000 | tf_op jit(solution)/shard_map/up_project/pallas_call | solution.py:234
  67.2 8.0 %all-to-all-done.1 = bf16[8,176,704]{2,1,0:T(8,128)(2,1)} async-done(((bf16[8,176,704]{2,1,0:T(8,128)(2,1)}), bf16[8,176,704]{2,1,0:T(8,128)(2,1)}, u32[]{:S(2)}, u32[]{:S(2)}) %all-to-all-start.1) | async-done | bytes 1982496 | tf_op jit(solution)/shard_map/all_to_all | solution.py:631
  77.3 2.5 %collective-permute-done.3 = bf16[8,176,704]{2,1,0:T(8,128)(2,1)} collective-permute-done((bf16[8,176,704]{2,1,0:T(8,128)(2,1)}, bf16[8,176,704]{2,1,0:T(8,128)(2,1)}, u32[]{:S(2)}, u32[]{:S(2)}) %collective-permute-start.3) | collective-permute-done | bytes 1982496 | tf_op jit(solution)/shard_map/ppermute | solution.py:619
  79.8 8.7 %mixed_grad.1 = (f32[4,512,704]{2,1,0:T(8,128)}, f32[8,8,704]{2,1,0:T(8,128)}, f32[4,704]{1,0:T(4,128)}) custom-call(bf16[512,704]{1,0:T(8,128)(2,1)} %fusion.weighted, bf16[1408,704]{1,0:T(8,128)(2,1)} %bitcast.10.w_mine, bf16[1408,704]{1,0:T(8,128)(2,1)} %bitcast.11.w_other, f32[4,512,704]{2,1,0:T(8,128)} %get-tuple-element.48.act_ref.act, ...), custom_call_target="tpu_custom_call" | custom-call | flops 3200000000 | tf_op jit(solution)/shard_map/mixed_grad/pallas_call | solution.py:267
  88.5 4.3 %all-to-all-start.2 = ((f32[8,8,704]{2,1,0:T(8,128)}), f32[8,8,704]{2,1,0:T(8,128)S(1)}, u32[]{:S(2)}, u32[]{:S(2)}) async-start(f32[8,8,704]{2,1,0:T(8,128)} %get-tuple-element.55.local), calls=%async_computation.2 | async-start | bytes 393216 | tf_op jit(solution)/shard_map/all_to_all | solution.py:661
  93.0 6.7 %all-to-all-done.2.sums = f32[8,8,704]{2,1,0:T(8,128)S(1)} async-done(((f32[8,8,704]{2,1,0:T(8,128)}), f32[8,8,704]{2,1,0:T(8,128)S(1)}, u32[]{:S(2)}, u32[]{:S(2)}) %all-to-all-start.2) | async-done | bytes 180256 | tf_op jit(solution)/shard_map/all_to_all | solution.py:661
  99.7 2.8 %copy-done = f32[4,512,704]{2,1,0:T(8,128)S(1)} copy-done((f32[4,512,704]{2,1,0:T(8,128)S(1)}, f32[4,512,704]{2,1,0:T(8,128)}, u32[]{:S(2)}) %copy-start) | copy-done | bytes 5767192
  104.1 1.8 down_other.1
  106.5 1.7 down_mine.1
  108.2 2.6 %collective-permute-done.4.other = bf16[8,176,704]{2,1,0:T(8,128)(2,1)S(1)} collective-permute-done((bf16[8,176,704]{2,1,0:T(8,128)(2,1)S(1)}, bf16[8,176,704]{2,1,0:T(8,128)(2,1)S(1)}, u32[]{:S(2)}, u32[]{:S(2)}) %collective-permute-start.4) | collective-permute-done | bytes 1982496 | tf_op jit(solution)/shard_map/ppermute | solution.py:619
  110.8 2.0 chip_sum.2
  112.8 7.8 %all-to-all-start.3 = ((bf16[64,22,704]{2,1,0:T(8,128)(2,1)}), bf16[64,22,704]{2,1,0:T(8,128)(2,1)}, u32[]{:S(2)}, u32[]{:S(2)}) async-start(bf16[64,22,704]{2,1,0:T(8,128)(2,1)} %chip_sum.2), calls=%async_computation.3 | async-start | bytes 4718592 | tf_op jit(solution)/shard_map/all_to_all | solution.py:657
  120.6 16.5 %hidden_grad.1 = (bf16[1408,704]{1,0:T(8,128)(2,1)}, bf16[1408,704]{1,0:T(8,128)(2,1)}, f32[512,704]{1,0:T(8,128)}, bf16[384,704]{1,0:T(8,128)(2,1)}, bf16[384,704]{1,0:T(8,128)(2,1)}, /*index=5*/f32[8,704]{1,0:T(8,128)}) custom-call(f32[4,512,704]{2,1,0:T(8,128)} %get-tuple-element.48.act_ref.act, f32[4,512,704]{2,1,0:T(8,128)} %get-tuple-element.49.slope, ...), custom_call_target="tpu_custom_call" | custom-call | flops 5600000000 | tf_op jit(solution)/shard_map/hidden_grad/pallas_call | solution.py:427
  137.4 7.7 %taps_grad.1 = f32[7,7,704]{2,1,0:T(8,128)} custom-call(bf16[4,128,704]{2,1,0:T(8,128)(2,1)} %bitcast.47, bf16[3,128,704]{2,1,0:T(8,128)(2,1)} %bitcast.57, bf16[3,128,704]{2,1,0:T(8,128)(2,1)} %bitcast.59, f32[4,128,704]{2,1,0:T(8,128)} %bitcast.51), custom_call_target="tpu_custom_call" | custom-call | flops 400000000 | tf_op jit(solution)/shard_map/taps_grad/pallas_call | solution.py:478
  146.8 4.1 %collective-permute-start.7 = (bf16[24,16,704]{2,1,0:T(8,128)(2,1)}, bf16[24,16,704]{2,1,0:T(8,128)(2,1)}, u32[]{:S(2)}, u32[]{:S(2)}) collective-permute-start(bf16[24,16,704]{2,1,0:T(8,128)(2,1)} %bitcast.22), channel_id=1, source_target_pairs={{0,1},{1,2},{2,3},{3,4},{4,5},{5,6},{6,7},{8,9},{9,10},{10,11},{11... | collective-permute-start | bytes 1622024 | tf_op jit(solution)/shard_map/ppermute | solution.py:670
  152.7 2.1 convert_reduce_fusion.1
  154.8 4.0 %chip_sum.3 = bf16[64,24,768]{2,1,0:T(8,128)(2,1)} custom-call(bf16[8,176,704]{2,1,0:T(8,128)(2,1)S(1)} %bitcast.44, bf16[8,176,704]{2,1,0:T(8,128)(2,1)} %collective-permute-done.5.other, f32[16,2,704]{2,1,0:T(2,128)S(1)} %get-tuple-element.107.vector, f32[16,24,64]{2,1,0:T(8,128)S(1)} %pad.9.edge), custom_call_target="tpu_custom_call" | custom-call | flops 120000000 | tf_op jit(solution)/shard_map/chip_sum/pallas_call | solution.py:577
  158.9 11.5 %all-to-all-start.4 = ((bf16[64,24,768]{2,1,0:T(8,128)(2,1)}), bf16[64,24,768]{2,1,0:T(8,128)(2,1)S(1)}, u32[]{:S(2)}, u32[]{:S(2)}) async-start(bf16[64,24,768]{2,1,0:T(8,128)(2,1)} %chip_sum.3), calls=%async_computation.4 | async-start | bytes 4718592 | tf_op jit(solution)/shard_map/all_to_all | solution.py:657
  171.6 21.6 %collective-permute-done.7 = bf16[24,16,704]{2,1,0:T(8,128)(2,1)} collective-permute-done((bf16[24,16,704]{2,1,0:T(8,128)(2,1)}, bf16[24,16,704]{2,1,0:T(8,128)(2,1)}, u32[]{:S(2)}, u32[]{:S(2)}) %collective-permute-start.7) | collective-permute-done | bytes 540704 | tf_op jit(solution)/shard_map/ppermute | solution.py:670
  194.0 8.1 %conv_back.1 = f32[4,128,704]{2,1,0:T(8,128)} custom-call(f32[4,128,704]{2,1,0:T(8,128)} %bitcast.52, bf16[3,128,704]{2,1,0:T(8,128)(2,1)} %bitcast.23.above, bf16[3,128,704]{2,1,0:T(8,128)(2,1)} %bitcast.25.below, f32[7,7,704]{2,1,0:T(8,128)} %k_ref.5, bf16[4,128,704]{2,1,0:T(8,128)(2,1)} %bitcast.54, f32[4,128,128]{2,1,0:T(8,128)} %broadcast_in_dim.36.weight), custom_call_target="tpu_custom_call" | custom-call | flops 24000000000 | tf_op jit(solution)/shard_map/conv_back/pallas_call | solution.py:527
  202.0 3.8 %all-to-all-done.4 = bf16[64,24,768]{2,1,0:T(8,128)(2,1)S(1)} async-done(((bf16[64,24,768]{2,1,0:T(8,128)(2,1)}), bf16[64,24,768]{2,1,0:T(8,128)(2,1)S(1)}, u32[]{:S(2)}, u32[]{:S(2)}) %all-to-all-start.4) | async-done | bytes 2359328 | tf_op jit(solution)/shard_map/all_to_all | solution.py:657
  207.5 4.1 %collective-permute-done.9 = f32[4,704]{1,0:T(4,128)S(1)} collective-permute-done((f32[4,704]{1,0:T(4,128)S(1)}, f32[4,704]{1,0:T(4,128)S(1)}, u32[]{:S(2)}, u32[]{:S(2)}) %collective-permute-start.9) | collective-permute-done | bytes 11296 | tf_op jit(solution)/shard_map/ppermute | solution.py:623
  212.8 4.8 %all-to-all-start.5 = ((bf16[8,26,1408]{2,1,0:T(8,128)(2,1)}), bf16[8,26,1408]{2,1,0:T(8,128)(2,1)S(1)}, u32[]{:S(2)}, u32[]{:S(2)}) async-start(bf16[8,26,1408]{2,1,0:T(8,128)(2,1)} %broadcast_in_dim.38), calls=%async_computation.5 | async-start | bytes 1441792 | tf_op jit(solution)/shard_map/all_to_all | solution.py:661
  217.7 1.6 copy.50
  219.2 8.6 %all-to-all-done.5 = bf16[8,26,1408]{2,1,0:T(8,128)(2,1)S(1)} async-done(((bf16[8,26,1408]{2,1,0:T(8,128)(2,1)}), bf16[8,26,1408]{2,1,0:T(8,128)(2,1)S(1)}, u32[]{:S(2)}, u32[]{:S(2)}) %all-to-all-start.5) | async-done | bytes 585760 | tf_op jit(solution)/shard_map/all_to_all | solution.py:661
  (115 shorter events, 23.3 us)
Async XLA Ops:
  3.0 8.0 %copy-start.12 = (bf16[1,4,128,704]{2,3,1,0:T(8,128)(2,1)S(1)}, bf16[1,4,128,704]{2,3,1,0:T(8,128)(2,1)}, u32[]{:S(2)}) copy-start(bf16[1,4,128,704]{2,3,1,0:T(8,128)(2,1)} %param.10) | copy-start | bytes 2162692
  3.0 35.5 %all-to-all-start = ((bf16[8,176,704]{2,1,0:T(8,128)(2,1)}), bf16[8,176,704]{2,1,0:T(8,128)(2,1)}, u32[]{:S(2)}, u32[]{:S(2)}) async-start(bf16[8,176,704]{2,1,0:T(8,128)(2,1)} %broadcast_in_dim.31), calls=%async_computation | async-start | bytes 4325376 | tf_op jit(solution)/shard_map/all_to_all | solution.py:631
  11.3 5.1 %copy-start.8 = (bf16[1,4,128,704]{3,2,1,0:T(8,128)(2,1)}, bf16[1,4,128,704]{3,2,1,0:T(8,128)(2,1)S(1)}, u32[]{:S(2)}) copy-start(bf16[1,4,128,704]{3,2,1,0:T(8,128)(2,1)S(1)} %copy.39) | copy-start | bytes 2162692
  11.3 3.6 %copy-start.15 = (bf16[176,704]{1,0:T(8,128)(2,1)S(1)}, bf16[176,704]{1,0:T(8,128)(2,1)}, u32[]{:S(2)}) copy-start(bf16[176,704]{1,0:T(8,128)(2,1)} %param.16) | copy-start | bytes 743428
  11.4 27.1 %collective-permute-start = (bf16[24,16,704]{2,1,0:T(8,128)(2,1)S(1)}, bf16[24,16,704]{2,1,0:T(8,128)(2,1)S(1)}, u32[]{:S(2)}, u32[]{:S(2)}) collective-permute-start(bf16[24,16,704]{2,1,0:T(8,128)(2,1)S(1)} %bitcast.61), channel_id=1, source_target_pairs={{0,1},{1,2},{2,3},{3,4},{4,5},{5,6},{6,7},{8,9},{9,10},{10,11},{11... | collective-permute-start | bytes 1622024 | tf_op jit(solution)/shard_map/ppermute | solution.py:670
  13.6 24.9 %collective-permute-start.1 = (bf16[24,16,704]{2,1,0:T(8,128)(2,1)S(1)}, bf16[24,16,704]{2,1,0:T(8,128)(2,1)S(1)}, u32[]{:S(2)}, u32[]{:S(2)}) collective-permute-start(bf16[24,16,704]{2,1,0:T(8,128)(2,1)S(1)} %bitcast.60), channel_id=1, source_target_pairs={{1,0},{2,1},{3,2},{4,3},{5,4},{6,5},{7,6},{9,8},{10,9},{11,10},{12... | collective-permute-start | bytes 1622024 | tf_op jit(solution)/shard_map/ppermute | solution.py:670
  38.6 10.0 %copy-start.19 = (f32[704]{0:T(1024)S(1)}, f32[704]{0:T(1024)}, u32[]{:S(2)}) copy-start(f32[704]{0:T(1024)} %param.12) | copy-start | bytes 8452
  38.6 17.6 %collective-permute-start.2 = (bf16[8,176,704]{2,1,0:T(8,128)(2,1)}, bf16[8,176,704]{2,1,0:T(8,128)(2,1)S(1)}, u32[]{:S(2)}, u32[]{:S(2)}) collective-permute-start(bf16[8,176,704]{2,1,0:T(8,128)(2,1)} %all-to-all-done), channel_id=1, source_target_pairs={{0,8},{1,9},{2,10},{3,11},{4,12},{5,13},{6,14},{7,15},{8,0},{9,1},... | collective-permute-start | bytes 5947400 | tf_op jit(solution)/shard_map/ppermute | solution.py:619
  39.6 35.6 %all-to-all-start.1 = ((bf16[8,176,704]{2,1,0:T(8,128)(2,1)}), bf16[8,176,704]{2,1,0:T(8,128)(2,1)}, u32[]{:S(2)}, u32[]{:S(2)}) async-start(bf16[8,176,704]{2,1,0:T(8,128)(2,1)} %broadcast_in_dim.32), calls=%async_computation.1 | async-start | bytes 4325376 | tf_op jit(solution)/shard_map/all_to_all | solution.py:631
  57.5 17.7 %copy-start.9 = (bf16[1,4,128,704]{2,3,1,0:T(8,128)(2,1)S(1)}, bf16[1,4,128,704]{2,3,1,0:T(8,128)(2,1)}, u32[]{:S(2)}) copy-start(bf16[1,4,128,704]{2,3,1,0:T(8,128)(2,1)} %param.17) | copy-start | bytes 2162692
  67.2 8.4 %copy-start.17 = (f32[2816]{0:T(1024)S(1)}, f32[2816]{0:T(1024)}, u32[]{:S(2)}) copy-start(f32[2816]{0:T(1024)} %param.14) | copy-start | bytes 33796
  67.2 8.5 %copy-start.18 = (f32[2816]{0:T(1024)S(1)}, f32[2816]{0:T(1024)}, u32[]{:S(2)}) copy-start(f32[2816]{0:T(1024)} %param.15) | copy-start | bytes 33796
  67.2 8.8 %copy-start.20 = (s32[1,4,128]{2,1,0:T(4,128)S(1)}, s32[1,4,128]{2,1,0:T(4,128)}, u32[]{:S(2)}) copy-start(s32[1,4,128]{2,1,0:T(4,128)} %param.18) | copy-start | bytes 6148
  67.2 8.8 %copy-start.21 = (f32[150]{0:T(256)S(1)}, f32[150]{0:T(256)}, u32[]{:S(2)}) copy-start(f32[150]{0:T(256)} %param.19) | copy-start | bytes 1804
  75.2 4.6 %collective-permute-start.3 = (bf16[8,176,704]{2,1,0:T(8,128)(2,1)}, bf16[8,176,704]{2,1,0:T(8,128)(2,1)}, u32[]{:S(2)}, u32[]{:S(2)}) collective-permute-start(bf16[8,176,704]{2,1,0:T(8,128)(2,1)} %all-to-all-done.1), channel_id=1, source_target_pairs={{0,8},{1,9},{2,10},{3,11},{4,12},{5,13},{6,14},{7,15},{8,0},{9,1},... | collective-permute-start | bytes 5947400 | tf_op jit(solution)/shard_map/ppermute | solution.py:619
  79.8 19.9 %copy-start.1 = (bf16[512,704]{1,0:T(8,128)(2,1)S(1)}, bf16[512,704]{1,0:T(8,128)(2,1)}, u32[]{:S(2)}) copy-start(bf16[512,704]{1,0:T(8,128)(2,1)} %fusion.weighted) | copy-start | bytes 2162692
  88.5 11.2 %all-to-all-start.2 = ((f32[8,8,704]{2,1,0:T(8,128)}), f32[8,8,704]{2,1,0:T(8,128)S(1)}, u32[]{:S(2)}, u32[]{:S(2)}) async-start(f32[8,8,704]{2,1,0:T(8,128)} %get-tuple-element.55.local), calls=%async_computation.2 | async-start | bytes 393216 | tf_op jit(solution)/shard_map/all_to_all | solution.py:661
  92.8 13.7 %copy-start.4 = (f32[4,704]{1,0:T(4,128)}, f32[4,704]{1,0:T(4,128)S(1)}, u32[]{:S(2)}) copy-start(f32[4,704]{1,0:T(4,128)S(1)} %pad_maximum_fusion.4.gamma) | copy-start | bytes 33796
  99.7 2.8 %copy-start = (f32[4,512,704]{2,1,0:T(8,128)S(1)}, f32[4,512,704]{2,1,0:T(8,128)}, u32[]{:S(2)}) copy-start(f32[4,512,704]{2,1,0:T(8,128)} %get-tuple-element.48.act_ref.act) | copy-start | bytes 17301508
  106.5 1.7 copy-start.5
  106.5 4.3 %collective-permute-start.4 = (bf16[8,176,704]{2,1,0:T(8,128)(2,1)S(1)}, bf16[8,176,704]{2,1,0:T(8,128)(2,1)S(1)}, u32[]{:S(2)}, u32[]{:S(2)}) collective-permute-start(bf16[8,176,704]{2,1,0:T(8,128)(2,1)S(1)} %bitcast.45), channel_id=1, source_target_pairs={{0,8},{1,9},{2,10},{3,11},{4,12},{5,13},{6,14},{7,15},{8,0},{9,1},... | collective-permute-start | bytes 5947400 | tf_op jit(solution)/shard_map/ppermute | solution.py:619
  112.8 39.9 %all-to-all-start.3 = ((bf16[64,22,704]{2,1,0:T(8,128)(2,1)}), bf16[64,22,704]{2,1,0:T(8,128)(2,1)}, u32[]{:S(2)}, u32[]{:S(2)}) async-start(bf16[64,22,704]{2,1,0:T(8,128)(2,1)} %chip_sum.2), calls=%async_computation.3 | async-start | bytes 4718592 | tf_op jit(solution)/shard_map/all_to_all | solution.py:657
  137.1 17.8 %collective-permute-start.5 = (bf16[8,176,704]{2,1,0:T(8,128)(2,1)}, bf16[8,176,704]{2,1,0:T(8,128)(2,1)}, u32[]{:S(2)}, u32[]{:S(2)}) collective-permute-start(bf16[8,176,704]{2,1,0:T(8,128)(2,1)} %bitcast.65), channel_id=1, source_target_pairs={{0,8},{1,9},{2,10},{3,11},{4,12},{5,13},{6,14},{7,15},{8,0},{9,1},... | collective-permute-start | bytes 5947400 | tf_op jit(solution)/shard_map/ppermute | solution.py:619
  137.3 8.9 %copy-start.16 = (f32[8,704]{1,0:T(8,128)S(1)}, f32[8,704]{1,0:T(8,128)}, u32[]{:S(2)}) copy-start(f32[8,704]{1,0:T(8,128)} %get-tuple-element.66) | copy-start | bytes 67588
  146.2 6.1 %collective-permute-start.6 = (f32[64,704]{1,0:T(8,128)S(1)}, f32[64,704]{1,0:T(8,128)S(1)}, u32[]{:S(2)}, u32[]{:S(2)}) collective-permute-start(f32[64,704]{1,0:T(8,128)S(1)} %select_maximum_fusion), channel_id=1, source_target_pairs={{0,8},{1,9},{2,10},{3,11},{4,12},{5,13},{6,14},{7,15},{8,0},{9,1},... | collective-permute-start | bytes 540680 | tf_op jit(solution)/shard_map/ppermute | solution.py:619
  146.8 46.3 %collective-permute-start.7 = (bf16[24,16,704]{2,1,0:T(8,128)(2,1)}, bf16[24,16,704]{2,1,0:T(8,128)(2,1)}, u32[]{:S(2)}, u32[]{:S(2)}) collective-permute-start(bf16[24,16,704]{2,1,0:T(8,128)(2,1)} %bitcast.22), channel_id=1, source_target_pairs={{0,1},{1,2},{2,3},{3,4},{4,5},{5,6},{6,7},{8,9},{9,10},{10,11},{11... | collective-permute-start | bytes 1622024 | tf_op jit(solution)/shard_map/ppermute | solution.py:670
  150.8 4.0 %copy-start.2 = (bf16[1408,704]{1,0:T(8,128)(2,1)S(1)}, bf16[1408,704]{1,0:T(8,128)(2,1)}, u32[]{:S(2)}) copy-start(bf16[1408,704]{1,0:T(8,128)(2,1)} %get-tuple-element.63) | copy-start | bytes 5947396
  150.8 42.3 %collective-permute-start.8 = (bf16[24,16,704]{2,1,0:T(8,128)(2,1)}, bf16[24,16,704]{2,1,0:T(8,128)(2,1)}, u32[]{:S(2)}, u32[]{:S(2)}) collective-permute-start(bf16[24,16,704]{2,1,0:T(8,128)(2,1)} %bitcast.66), channel_id=1, source_target_pairs={{1,0},{2,1},{3,2},{4,3},{5,4},{6,5},{7,6},{9,8},{10,9},{11,10},{12... | collective-permute-start | bytes 1622024 | tf_op jit(solution)/shard_map/ppermute | solution.py:670
  158.9 47.0 %all-to-all-start.4 = ((bf16[64,24,768]{2,1,0:T(8,128)(2,1)}), bf16[64,24,768]{2,1,0:T(8,128)(2,1)S(1)}, u32[]{:S(2)}, u32[]{:S(2)}) async-start(bf16[64,24,768]{2,1,0:T(8,128)(2,1)} %chip_sum.3), calls=%async_computation.4 | async-start | bytes 4718592 | tf_op jit(solution)/shard_map/all_to_all | solution.py:657
  206.2 11.4 %copy-start.11 = (f32[4,128,704]{2,1,0:T(8,128)S(1)}, f32[4,128,704]{2,1,0:T(8,128)}, u32[]{:S(2)}) copy-start(f32[4,128,704]{2,1,0:T(8,128)} %conv_back.1) | copy-start | bytes 4325380
  206.4 5.3 %collective-permute-start.9 = (f32[4,704]{1,0:T(4,128)S(1)}, f32[4,704]{1,0:T(4,128)S(1)}, u32[]{:S(2)}, u32[]{:S(2)}) collective-permute-start(f32[4,704]{1,0:T(4,128)S(1)} %pad_maximum_fusion.6), channel_id=1, source_target_pairs={{0,64},{1,65},{2,66},{3,67},{4,68},{5,69},{6,70},{7,71},{8,72},{9,... | collective-permute-start | bytes 33800 | tf_op jit(solution)/shard_map/ppermute | solution.py:623
  212.8 15.0 %all-to-all-start.5 = ((bf16[8,26,1408]{2,1,0:T(8,128)(2,1)}), bf16[8,26,1408]{2,1,0:T(8,128)(2,1)S(1)}, u32[]{:S(2)}, u32[]{:S(2)}) async-start(bf16[8,26,1408]{2,1,0:T(8,128)(2,1)} %broadcast_in_dim.38), calls=%async_computation.5 | async-start | bytes 1441792 | tf_op jit(solution)/shard_map/all_to_all | solution.py:661
  (6 other events, 5.4 us)
